TPU v7x, 32 devices: a whole 2x2x4 slice. The times are simulated.
32 devices in a mesh: grp: 4 (over y, core), dev: 8 (over z, x).
Axes of the slice: x: 2, y: 2, z: 4, core: 2. Of those that a mesh axis runs over, the one named last changes fastest.
Arguments:
- features: bfloat16 [64, 128, 768], P(('grp', 'dev'))
- tile_counts: int32 [64], P(('grp', 'dev')), may hold values from 20 to 120
- projection: bfloat16 [768, 512], replicated, may hold values from -0.21875 to 0.21875
Outputs:
- tile_maxima: float32 [64, 64, 128], P('grp', 'dev')
- chamfer: float32 [64, 64], P('grp', 'dev')
All inputs are finite; a program needn't handle non-finite values.
Results may differ from a plain program's by a relative error of at most 0.0014.
Values may be sent and summed in bfloat16 or wider, within the bound.
No kernel may reach another device: no remote copies, remote signals or barrier semaphores. Data moves between devices by JAX's collectives and lax.ppermute only.
A program may use at most 64 MiB of HBM per device.

v0:
```python
import math

import jax
import jax.numpy as jnp
from jax import lax
from jax.sharding import PartitionSpec as P


def spread(value, axis, root):
    mine = lax.axis_index(axis) == root
    return lax.psum(jnp.where(mine, value, jnp.zeros_like(value)), axis)


def embed_tiles(features, projection):
    raw = jnp.einsum("spf,fe->spe", features, projection, preferred_element_type=jnp.float32)
    scale = lax.rsqrt(jnp.sum(raw * raw, axis=2, keepdims=True) + 1e-06)
    return (raw * scale).astype(jnp.bfloat16)


def score_block(rows, row_counts, cols, col_counts):
    slots = rows.shape[1]
    position = jnp.arange(slots, dtype=jnp.int32)
    row_valid = position[None, :] < row_counts[:, None]
    col_valid = position[None, :] < col_counts[:, None]
    score = jnp.einsum("ape,bqe->abpq", rows, cols, preferred_element_type=jnp.float32)
    forward = jnp.max(jnp.where(col_valid[None, :, None, :], score, -4.0), axis=3)
    forward = jnp.where(row_valid[:, None, :], forward, 0.0)
    back = jnp.max(jnp.where(row_valid[:, None, :, None], score, -4.0), axis=2)
    back = jnp.where(col_valid[None, :, :], back, 0.0)
    row_mean = jnp.sum(forward, axis=2) / row_counts[:, None].astype(jnp.float32)
    col_mean = jnp.sum(back, axis=2) / col_counts[None, :].astype(jnp.float32)
    return (forward, 0.5 * (row_mean + col_mean))


def on_device(features, tile_counts, projection):
    ratio = lax.axis_size("dev") // lax.axis_size("grp")
    column = lax.axis_index("dev")
    holder = column // ratio
    own = embed_tiles(features, projection)
    rows, row_counts = (
        lax.all_gather(own, "dev", axis=0, tiled=True),
        lax.all_gather(tile_counts, "dev", axis=0, tiled=True),
    )
    width = rows.shape[0] // ratio
    offset = column % ratio * width
    piece = lax.dynamic_slice_in_dim(rows, offset, width, 0)
    piece_counts = lax.dynamic_slice_in_dim(row_counts, offset, width, 0)
    cols, col_counts = (spread(piece, "grp", holder), spread(piece_counts, "grp", holder))
    total = rows.shape[0]
    group = math.gcd(total, 4)
    blocks = rows.reshape(total // group, group, rows.shape[1], rows.shape[2])
    block_counts = row_counts.reshape(total // group, group)

    def one_block(pair):
        return score_block(pair[0], pair[1], cols, col_counts)

    forward, chamfer = lax.map(one_block, (blocks, block_counts))
    tile_maxima = forward.reshape(total, cols.shape[0], rows.shape[1])
    return (tile_maxima, chamfer.reshape(total, cols.shape[0]))


def solution(mesh):
    return jax.shard_map(
        on_device,
        mesh=mesh,
        in_specs=(P(("grp", "dev"), None, None), P(("grp", "dev")), P()),
        out_specs=(P("grp", "dev", None), P("grp", "dev")),
        check_vma=False,
    )
```

profile of v0, /device:TPU:0, one launch (start us, length us, event | category | flops | bytes accessed | tf_op | source)
XLA Modules:
  0.0 118.1 jit_solution(11165826155830453473)
XLA Ops:
  7.2 1.1 copy-done
  8.3 1.4 %multiply_reduce_fusion = (f32[2,128]{1,0:T(2,128)S(1)}, f32[2,128,512]{2,1,0:T(8,128)S(1)}) fusion(bf16[2,128,768]{2,1,0:T(8,128)(2,1)} %param.5, bf16[768,512]{1,0:T(8,128)(2,1)S(1)} %copy-done), kind=kOutput, calls=%fused_computation.22 | convolution fusion | flops 201588480 | bytes 1704960 | tf_op jit(solution)/shard_map/spf,fe->spe/dot_general | solution.py:15
  9.8 0.8 multiply_convert_fusion
  10.7 52.1 %all-gather.2.cloned.1.call-done = bf16[16,128,512]{2,1,0:T(8,128)(2,1)} async-done(((bf16[2,128,512]{2,1,0:T(8,128)(2,1)}), bf16[16,128,512]{2,1,0:T(8,128)(2,1)}) %all-gather.2.cloned.1.call-update) | async-done | bytes 2097168 | tf_op jit(solution)/shard_map/all_gather | solution.py:41
  62.8 2.3 %dynamic-slice_select_fusion = bf16[8,128,512]{2,1,0:T(8,128)(2,1)} fusion(bf16[16,128,512]{2,1,0:T(8,128)(2,1)} %all-gather.2.cloned.1.call-done, s32[]{:T(128)S(6)} %select_n.66, pred[]{:T(512)S(6)} %eq.6), kind=kLoop, calls=%fused_computation.18 | loop fusion | flops 524288 | bytes 2097157 | tf_op jit(solution)/shard_map/jit(_where)/select_n | solution.py:11
  65.1 0.6 dynamic-slice
  66.4 0.2 dynamic-update-slice
  66.6 9.8 %all-reduce = s32[16]{0:T(128)S(1)} all-reduce(s32[16]{0:T(128)S(1)} %dynamic-update-slice), channel_id=1, replica_groups=mesh['grp'=4,'dev'=8] {'dev'}, use_global_device_ids=true, to_apply=%add | all-reduce | flops 16 | bytes 128
  76.4 0.1 broadcast_select_fusion
  76.5 4.9 %psum.14 = s32[8]{0:T(128)S(1)} all-reduce(s32[8]{0:T(128)S(1)} %broadcast_select_fusion), channel_id=1, replica_groups=mesh['grp'=4,'dev'=8] {'grp'}, use_global_device_ids=true, to_apply=%region_1.2 | all-reduce | flops 8 | bytes 64 | tf_op jit(solution)/shard_map/psum | solution.py:11
  81.4 0.1 reshape.189
  81.5 18.3 %all-reduce.3.cloned.1.call-done = bf16[8,128,512]{2,1,0:T(8,128)(2,1)} async-done(((bf16[8,128,512]{2,1,0:T(8,128)(2,1)}), bf16[8,128,512]{2,1,0:T(8,128)(2,1)}) %all-reduce.3.cloned.1.call-update) | async-done | bytes 1048592 | tf_op jit(solution)/shard_map/psum | solution.py:11
  99.8 10.8 %while.13 = (s32[]{:T(128)}, f32[4,4,8,128]{3,2,1,0:T(8,128)S(1)}, f32[4,4,8]{2,1,0:T(4,128)S(1)}, s32[4,4]{1,0:T(4,128)S(1)}, s32[8]{0:T(128)S(1)}, /*index=5*/...) while((s32[]{:T(128)}, f32[4,4,8,128]{3,2,1,0:T(8,128)S(1)}, ...), condition=%wide.region_8.9_spmd, body=%wide.region_3.8_spmd.sunk | while | flops 538981952 | bytes 1684425 | solution.py:57
  99.8 0.1 iota_compare_fusion.4
  99.9 0.1 iota_compare_fusion.5
  100.0 2.3 %select_reduce_fusion.4 = (f32[4,8,128]{2,1,0:T(8,128)S(1)}, f32[4,128,8]{1,2,0:T(8,128)S(1)}) fusion(pred[4,128]{1,0:T(4,128)(4,1)S(1)} %iota_compare_fusion.4, pred[8,128]{1,0:T(8,128)(4,1)S(1)} %iota_compare_fusion.5, bf16[8,128,512]{2,1,0:T(8,128)(2,1)} %get-tuple-element.188, bf16[4,4,128,512]{3,2,1,0:T(8,128)(2,1)} %get-tuple-element.187, ...), kind=kOutput, calls=%fused_computation.clone.1 | convolution fusion | flops 538959872 | bytes 1607680 | tf_op jit(solution)/shard_map/while/body/eval_jaxpr/ape,bqe->abpq/dot_general | solution.py:25
  102.3 0.1 fusion.18
  102.4 0.1 multiply_dynamic-update-slice_fusion.2
  102.5 0.1 iota_compare_fusion.4
  102.6 0.1 iota_compare_fusion.5
  102.7 2.3 %select_reduce_fusion.4 = (f32[4,8,128]{2,1,0:T(8,128)S(1)}, f32[4,128,8]{1,2,0:T(8,128)S(1)}) fusion(pred[4,128]{1,0:T(4,128)(4,1)S(1)} %iota_compare_fusion.4, pred[8,128]{1,0:T(8,128)(4,1)S(1)} %iota_compare_fusion.5, bf16[8,128,512]{2,1,0:T(8,128)(2,1)} %get-tuple-element.188, bf16[4,4,128,512]{3,2,1,0:T(8,128)(2,1)} %get-tuple-element.187, ...), kind=kOutput, calls=%fused_computation.clone.1 | convolution fusion | flops 538959872 | bytes 1607680 | tf_op jit(solution)/shard_map/while/body/eval_jaxpr/ape,bqe->abpq/dot_general | solution.py:25
  105.0 0.1 fusion.18
  105.1 0.1 multiply_dynamic-update-slice_fusion.2
  105.2 0.1 iota_compare_fusion.4
  105.4 2.3 %select_reduce_fusion.4 = (f32[4,8,128]{2,1,0:T(8,128)S(1)}, f32[4,128,8]{1,2,0:T(8,128)S(1)}) fusion(pred[4,128]{1,0:T(4,128)(4,1)S(1)} %iota_compare_fusion.4, pred[8,128]{1,0:T(8,128)(4,1)S(1)} %iota_compare_fusion.5, bf16[8,128,512]{2,1,0:T(8,128)(2,1)} %get-tuple-element.188, bf16[4,4,128,512]{3,2,1,0:T(8,128)(2,1)} %get-tuple-element.187, ...), kind=kOutput, calls=%fused_computation.clone.1 | convolution fusion | flops 538959872 | bytes 1607680 | tf_op jit(solution)/shard_map/while/body/eval_jaxpr/ape,bqe->abpq/dot_general | solution.py:25
  107.7 0.1 fusion.18
  107.8 0.1 multiply_dynamic-update-slice_fusion.2
  107.9 0.1 iota_compare_fusion.4
  108.1 2.3 %select_reduce_fusion.4 = (f32[4,8,128]{2,1,0:T(8,128)S(1)}, f32[4,128,8]{1,2,0:T(8,128)S(1)}) fusion(pred[4,128]{1,0:T(4,128)(4,1)S(1)} %iota_compare_fusion.4, pred[8,128]{1,0:T(8,128)(4,1)S(1)} %iota_compare_fusion.5, bf16[8,128,512]{2,1,0:T(8,128)(2,1)} %get-tuple-element.188, bf16[4,4,128,512]{3,2,1,0:T(8,128)(2,1)} %get-tuple-element.187, ...), kind=kOutput, calls=%fused_computation.clone.1 | convolution fusion | flops 538959872 | bytes 1607680 | tf_op jit(solution)/shard_map/while/body/eval_jaxpr/ape,bqe->abpq/dot_general | solution.py:25
  110.4 0.1 fusion.18
  110.5 0.1 multiply_dynamic-update-slice_fusion.2
  110.6 0.7 copy.6
  (26 shorter events, 0.4 us)
Async XLA Ops:
  7.2 1.1 copy-start
  7.2 55.6 %all-gather.2.cloned.1.call-start = ((), (), s32[]{:S(2)}) async-start(), calls=%async_computation | async-start | bytes 2359296 | tf_op jit(solution)/shard_map/all_gather | solution.py:41
  9.8 55.3 %copy-start.3 = (u32[32]{0:T(128)S(1)}, u32[32]{0:T(128)}, u32[]{:S(2)}) copy-start(u32[32]{0:T(128)} %constant.79) | copy-start | bytes 388
  9.8 56.6 %copy-start.2 = (s32[2]{0:T(128)S(1)}, s32[2]{0:T(128)}, u32[]{:S(2)}) copy-start(s32[2]{0:T(128)} %param.6) | copy-start | bytes 28
  10.6 89.2 %all-reduce.3.cloned.1.call-start = ((), (), s32[]{:S(2)}) async-start(), calls=%async_computation.1 | async-start | bytes 2097152 | tf_op jit(solution)/shard_map/psum | solution.py:11
  110.6 0.7 copy-start.1
Sparse Core Ops, SparseCore 0:
  10.8 51.9 all-gather.1
  65.2 34.5 all-reduce.2
where the time goes:
time: 118 us
  waiting for transfers between devices  70.4 us (60%)
  between operations  14.8 us (13%)
  blocking collectives  14.7 us (12%)
  matrix products  10.8 us (9%)
  other arithmetic  4.51 us (4%)
  local copies, waits for them, and re-layouts  2.68 us (2%)
    all_gather x1, waiting for transfers between devices, on_device(): lax.all_gather(own, 'dev', axis=0, tiled=True)  52.1 us
    psum x1, waiting for transfers between devices, spread(): return lax.psum(jnp.where(mine, value, jnp.zeros_like(value)), axis)  18.3 us
    unnamed x1, blocking collectives  9.82 us
    dot_general x4, matrix products, score_block(): jnp.einsum('ape,bqe->abpq', rows, cols, preferred_element_type=jnp.float32)  9.39 us
    psum x1, blocking collectives, spread(): return lax.psum(jnp.where(mine, value, jnp.zeros_like(value)), axis)  4.89 us
    unnamed x12, local copies, waits for them, and re-layouts  2.6 us
  transfers between devices with their start and end apart: 2, of which 2 were waited for; matrix products, arithmetic and copies ran while one was open for 1% of the time, Pallas kernels for 0%

commit v1 on v0

v1 whole, which is shorter than its diff:
```python
import functools

import jax
import jax.numpy as jnp
from jax import lax
from jax.experimental import pallas as pl
from jax.experimental.pallas import tpu as pltpu
from jax.sharding import PartitionSpec as P

USED = 120
CHUNK = 16
TAIL = 8
MAIN = USED - TAIL
MARK = 4.0
VMEM_LIMIT = 40 * 1024 * 1024
NT = (((1,), (1,)), ((), ()))
VMEM = pl.BlockSpec(memory_space=pltpu.VMEM)
HBM = pl.BlockSpec(memory_space=pltpu.HBM)
PARAMS = pltpu.CompilerParams(vmem_limit_bytes=VMEM_LIMIT)


def embed_kernel(features_in, counts_in, projection_in, *refs):
    out_ref, features_ref, counts_ref, projection_ref, sems = refs
    copies = [
        pltpu.make_async_copy(projection_in, projection_ref, sems.at[0]),
        pltpu.make_async_copy(features_in, features_ref, sems.at[1]),
        pltpu.make_async_copy(counts_in, counts_ref, sems.at[2]),
    ]
    for copy in copies:
        copy.start()
    for copy in copies:
        copy.wait()
    slides, slots, _ = features_ref.shape
    tails = []
    for s in range(slides):
        raw = jnp.dot(features_ref[s], projection_ref[...], preferred_element_type=jnp.float32)
        scale = lax.rsqrt(jnp.sum(raw * raw, axis=1, keepdims=True) + 1e-06)
        unit = raw * scale
        slot = lax.broadcasted_iota(jnp.int32, unit.shape, 0)
        lane = lax.broadcasted_iota(jnp.int32, unit.shape, 1)
        filled = slot < counts_ref[s]
        unit = jnp.where(filled, unit, jnp.where(lane == 0, MARK, unit[:1]))
        out_ref[pl.ds(s * MAIN, MAIN), :] = unit[:MAIN].astype(out_ref.dtype)
        tails.append(unit[MAIN:USED])
    out_ref[pl.ds(slides * MAIN, slides * TAIL), :] = jnp.concatenate(tails, axis=0).astype(out_ref.dtype)


def embed_tiles(features, tile_counts, projection):
    slides = features.shape[0]
    width = projection.shape[1]
    return pl.pallas_call(
        embed_kernel,
        out_shape=jax.ShapeDtypeStruct((slides * USED, width), jnp.bfloat16),
        in_specs=[HBM] * 3,
        out_specs=VMEM,
        scratch_shapes=[
            pltpu.VMEM(features.shape, features.dtype),
            pltpu.SMEM(tile_counts.shape, tile_counts.dtype),
            pltpu.VMEM(projection.shape, projection.dtype),
            pltpu.SemaphoreType.DMA((3,)),
        ],
        compiler_params=PARAMS,
        name="embed",
    )(*[pltpu.with_memory_space_constraint(x, pltpu.HBM) for x in (features, tile_counts, projection)])


def marked(part):
    return part[:, :1] > 0.5 * MARK


def count_rows(flags, s, per):
    own = [flags[s * MAIN : (s + 1) * MAIN], flags[per * MAIN + s * TAIL : per * MAIN + (s + 1) * TAIL]]
    return sum(jnp.sum(jnp.where(flag, 0.0, 1.0), axis=0, keepdims=True) for flag in own)


def lay_columns(blocks, labels, per, cols, weight_ref):
    tiles, _, width = cols.shape
    chunks = MAIN // CHUNK
    col_slides = tiles * CHUNK // USED
    span = col_slides * CHUNK
    mine = lax.axis_index("grp")
    lane = lax.broadcasted_iota(jnp.int32, (1, span), 1)
    row = lax.broadcasted_iota(jnp.int32, (CHUNK, width), 0)
    column = lax.broadcasted_iota(jnp.int32, (CHUNK, width), 1)
    counts = jnp.ones((1, span), jnp.float32)
    tail_counts = jnp.ones((1, span // 2), jnp.float32)
    whole = {}
    for (mask, pair, offset), block in zip(labels, blocks):
        for start in range(0, block.shape[0], CHUNK):
            whole.setdefault((mask, pair), {})[offset + start] = block[pl.ds(start, CHUNK), :]
    for (mask, pair), parts in whole.items():
        first = ((mine ^ mask) * 2 + pair) * per
        parts = {start: part.astype(jnp.float32) for start, part in parts.items()}
        flags = jnp.concatenate([marked(parts[start]).astype(jnp.float32) for start in sorted(parts)], axis=0) > 0.5
        tops = [parts[s * MAIN][:1] for s in range(per)]
        for s in range(per):
            count = count_rows(flags, s, per)
            counts = jnp.where(lane // CHUNK == first + s, count, counts)
            tail_counts = jnp.where(lane[:, : span // 2] // TAIL == first + s, count, tail_counts)
        for start, part in parts.items():
            flag = jnp.logical_and(marked(part), column == 0)
            if start < per * MAIN:
                s, k = start // MAIN, start % MAIN // CHUNK
                top, index = tops[s], k * col_slides + first + s
            else:
                s = (start - per * MAIN) // TAIL
                top = jnp.where(row < TAIL, tops[s], tops[s + 1])
                index = chunks * col_slides + (first + s) // 2
            cols[index] = jnp.where(flag, top, part).astype(cols.dtype)
    for k in range(chunks):
        tile = (k * CHUNK + lane % CHUNK).astype(jnp.float32)
        weight_ref[pl.ds(k, 1), :] = jnp.where(tile < counts, 0.5 / counts, 0.0)
    tile = (MAIN + lane % TAIL).astype(jnp.float32)[:, : span // 2]
    weight_ref[pl.ds(chunks, 1), : span // 2] = jnp.where(tile < tail_counts, 0.5 / tail_counts, 0.0)


def unmark(piece, per):
    head = piece[:, :128].astype(jnp.float32)
    flag = marked(head)
    row = lax.broadcasted_iota(jnp.int32, head.shape, 0)
    column = lax.broadcasted_iota(jnp.int32, head.shape, 1)
    top = head[:1]
    for s in range(1, per):
        here = jnp.where(row < per * MAIN, row // MAIN, (row - per * MAIN) // TAIL) == s
        top = jnp.where(here, head[s * MAIN : s * MAIN + 1], top)
    head = jnp.where(jnp.logical_and(flag, column == 0), top, head).astype(piece.dtype)
    return jnp.concatenate([head, piece[:, 128:]], axis=1), [count_rows(flag, s, per) for s in range(per)]


def score_pieces(pieces, cols, weight_ref, per, slots, put):
    tiles, _, width = cols.shape
    chunks = MAIN // CHUNK
    col_slides = tiles * CHUNK // USED
    span = col_slides * CHUNK
    flat = cols[...].reshape(tiles * CHUNK, width)
    tile = lax.broadcasted_iota(jnp.int32, (1, slots), 1)
    lane = lax.broadcasted_iota(jnp.int32, (col_slides, span), 1)
    slide = lax.broadcasted_iota(jnp.int32, (col_slides, span), 0)
    clean = [unmark(piece[...], per) for piece in pieces]
    rows = jnp.concatenate([block for block, _ in clean], axis=0)
    score = lax.dot_general(rows, flat, NT, preferred_element_type=jnp.float32)
    parts = [score[:, k * span : (k + 1) * span] for k in range(chunks)]
    last = score[:, chunks * span :]
    best = functools.reduce(jnp.maximum, parts)
    for t in range(len(pieces) * per):
        base, s = t // per * per * USED, t % per
        spots = (base + s * MAIN, MAIN), (base + per * MAIN + s * TAIL, TAIL)
        count = clean[t // per][1][s]

        def gathered(values):
            own = [values[start : start + size] for start, size in spots]
            return jnp.concatenate([*own, jnp.zeros((slots - USED, values.shape[1]), jnp.float32)], axis=0).T

        def highest(values):
            return functools.reduce(
                jnp.maximum, [jnp.max(values[start : start + size], axis=0, keepdims=True) for start, size in spots]
            )

        mine = jnp.maximum(
            jnp.max(gathered(best).reshape(col_slides, CHUNK, slots), axis=1),
            jnp.max(gathered(last).reshape(col_slides, TAIL, slots), axis=1),
        )
        mine = jnp.where(tile.astype(jnp.float32) < count, mine, 0.0)
        back = functools.reduce(jnp.add, [highest(part) * weight_ref[pl.ds(k, 1), :] for k, part in enumerate(parts)])
        rest = highest(last) * weight_ref[pl.ds(chunks, 1), : span // 2]
        mean = jnp.sum(mine * (0.5 / count), axis=1, keepdims=True)
        mean = mean + jnp.sum(jnp.where(lane // CHUNK == slide, back, 0.0), axis=1, keepdims=True)
        half = slice(0, span // 2)
        mean = mean + jnp.sum(jnp.where(lane[:, half] // TAIL == slide[:, half], rest, 0.0), axis=1, keepdims=True)
        put(t, jnp.where(tile == slots - 1, mean, mine))


def first_kernel(count, labels, per, slots, *refs):
    pieces, blocks, (cols, weight_ref, out_ref) = refs[:count], refs[count:-3], refs[-3:]
    lay_columns(blocks, labels, per, cols, weight_ref)

    def put(t, best):
        out_ref[t] = best

    score_pieces(pieces, cols, weight_ref, per, slots, put)


def first_step(pieces, columns, labels, per, slots):
    count = len(pieces) * per
    rows, width = sum(block.shape[0] for block in columns), columns[0].shape[1]
    col_slides = rows // USED
    return pl.pallas_call(
        functools.partial(first_kernel, len(pieces), labels, per, slots),
        out_shape=(
            jax.ShapeDtypeStruct((rows // CHUNK, CHUNK, width), columns[0].dtype),
            jax.ShapeDtypeStruct((MAIN // CHUNK + 1, col_slides * CHUNK), jnp.float32),
            jax.ShapeDtypeStruct((count, col_slides, slots), jnp.float32),
        ),
        in_specs=[VMEM] * (len(pieces) + len(columns)),
        out_specs=(VMEM,) * 3,
        compiler_params=PARAMS,
        name="first_scores",
    )(*pieces, *columns)


def score_kernel(count, per, slots, *refs):
    pieces, (cols, weight_ref, out_ref) = refs[:count], refs[count:]

    def put(t, best):
        out_ref[t] = best

    score_pieces(pieces, cols, weight_ref, per, slots, put)


def score_step(pieces, cols, weight, per, slots):
    count = len(pieces) * per
    return pl.pallas_call(
        functools.partial(score_kernel, len(pieces), per, slots),
        out_shape=jax.ShapeDtypeStruct((count, cols.shape[0] * CHUNK // USED, slots), jnp.float32),
        in_specs=[VMEM] * (len(pieces) + 2),
        out_specs=VMEM,
        compiler_params=PARAMS,
        name="scores",
    )(*pieces, cols, weight)


def finish_kernel(size, groups, count, per, slots, *refs):
    pieces, (cols, weight_ref), refs = refs[:count], refs[count : count + 2], refs[count + 2 :]
    done, out_ref = refs[:-1], refs[-1]
    wide = out_ref.shape[2]
    block = lax.axis_index("dev") // groups
    first = sum(ref.shape[0] for ref in done)

    def keep(r, best):
        for g in range(groups):
            out_ref[g * (size // groups) + block, r] = best[g * wide : (g + 1) * wide]

    r = 0
    for ref in done:
        for n in range(ref.shape[0]):
            keep(r, ref[n])
            r += 1
    score_pieces(pieces, cols, weight_ref, per, slots, lambda t, best: keep(first + t, best))


def finish_step(pieces, cols, weight, done, size, groups, per, slots):
    count = len(pieces) * per + sum(part.shape[0] for part in done)
    wide = done[0].shape[1] // groups
    operands = [*pieces, cols, weight, *done]
    return pl.pallas_call(
        functools.partial(finish_kernel, size, groups, len(pieces), per, slots),
        out_shape=jax.ShapeDtypeStruct((size, count, wide, slots), jnp.float32),
        in_specs=[VMEM] * len(operands),
        out_specs=VMEM,
        compiler_params=PARAMS,
        name="finish",
    )(*operands)


def gather_kernel(size, groups, rows, parts, best_ref, chamfer_ref):
    slots = best_ref.shape[2]
    per = parts.shape[2] // 2
    first = lax.axis_index("dev") % (size // groups) * groups
    tile = lax.broadcasted_iota(jnp.int32, (1, slots), 1)
    lane = lax.broadcasted_iota(jnp.int32, (per, chamfer_ref.shape[1]), 1)
    means = [jnp.zeros((per, chamfer_ref.shape[1]), jnp.float32)] * groups
    for k in range(groups):
        for r, (mask, s) in enumerate(rows):
            a = ((first + k) ^ mask) * per + s
            part = parts[first + k, r]
            kept = jnp.where(tile < USED, part, 0.0)
            for pair in range(2):
                e = k ^ (2 * pair)
                best_ref[a, pl.ds(e * per, per), :] = kept[pair * per : (pair + 1) * per]
                mean = part[pair * per : (pair + 1) * per, slots - 1 :]
                means[e] = jnp.where(lane == a, mean, means[e])
    for e in range(groups):
        chamfer_ref[pl.ds(e * per, per), :] = means[e]


def gather_results(parts, rows, size, groups):
    _, count, wide, slots = parts.shape
    return pl.pallas_call(
        functools.partial(gather_kernel, size, groups, rows),
        out_shape=(
            jax.ShapeDtypeStruct((2 * count, groups * wide // 2, slots), jnp.float32),
            jax.ShapeDtypeStruct((groups * wide // 2, 2 * count), jnp.float32),
        ),
        in_specs=[VMEM],
        out_specs=(VMEM, VMEM),
        compiler_params=PARAMS,
        name="gather_results",
    )(parts)


def flip(value, axis, mask):
    return lax.ppermute(value, axis, [(i, i ^ mask) for i in range(lax.axis_size(axis))])


def relay_kernel(in_ref, out_ref):
    out_ref[...] = in_ref[...]


def relay(block):
    return pl.pallas_call(
        relay_kernel,
        out_shape=jax.ShapeDtypeStruct(block.shape, block.dtype),
        in_specs=[VMEM],
        out_specs=VMEM,
        compiler_params=PARAMS,
        name="relay",
    )(block)


def split_kernel(in_ref, *outs):
    start = 0
    for out_ref in outs:
        out_ref[...] = in_ref[pl.ds(start, out_ref.shape[0]), :]
        start += out_ref.shape[0]


def split_block(block, count):
    rows, width = block.shape
    ends = [-(-n * rows // (count * CHUNK)) * CHUNK for n in range(count + 1)]
    return pl.pallas_call(
        split_kernel,
        out_shape=[jax.ShapeDtypeStruct((end - start, width), block.dtype) for start, end in zip(ends, ends[1:])],
        in_specs=[VMEM],
        out_specs=[VMEM] * count,
        compiler_params=PARAMS,
        name="split_block",
    )(block)


def on_device(features, tile_counts, projection):
    size, groups = lax.axis_size("dev"), lax.axis_size("grp")
    slots = features.shape[1]
    whole = embed_tiles(features, tile_counts, projection)
    per = features.shape[0]
    mirror, across, beside = flip(whole, "dev", 6), flip(whole, "dev", 1), flip(whole, "dev", 2)
    labels, columns = [(0, 0, 0), (0, 1, 0)], [whole, beside]
    bit = groups // 2
    while bit > 1:
        columns += [flip(block, "grp", bit) for block in columns]
        labels += [(mask ^ bit, pair, 0) for mask, pair, _ in labels]
        bit //= 2
    cut = [2, 2, 2, 4]
    cut = [split_block(block, count) for block, count in zip(columns, cut + [2] * len(columns))]
    mirror, cut[0] = lax.optimization_barrier((mirror, cut[0]))
    swapped = [flip(part, "grp", 1) for part in cut[0]]
    swapped, cut[-1] = lax.optimization_barrier((swapped, cut[-1]))
    across, cut[-2] = lax.optimization_barrier((across, cut[-2]))
    ends = [
        (part, (mask, pair, sum(other.shape[0] for other in parts[:n])))
        for parts, (mask, pair, _) in zip(cut, labels)
        for n, part in enumerate(parts)
    ]
    columns += swapped + [flip(part, "grp", 1) for part, _ in ends[len(swapped) :]]
    labels += [(mask ^ 1, pair, offset) for _, (mask, pair, offset) in ends]
    rows = [(whole, 0), (across, 1), (mirror, 6), (flip(mirror, "dev", 1), 7)]
    bit = 8
    while bit < size:
        rows += [(flip(block, "dev", bit), mask ^ bit) for block, mask in rows]
        bit *= 2
    blocks = [block for block, _ in rows]
    early, late = blocks[:-1], blocks[-1:]
    cols, weight, scored = first_step(early[:3], columns, labels, per, slots)
    done = [scored, *[score_step(early[i : i + 3], cols, weight, per, slots) for i in range(3, len(early), 3)]]
    results = finish_step(late, cols, weight, done, size, groups, per, slots)
    parts = lax.all_to_all(results, "dev", split_axis=0, concat_axis=0, tiled=True)
    names = tuple((mask, s) for _, mask in rows for s in range(per))
    best, chamfer = gather_results(parts, names, size, groups)
    return best, chamfer.T


def solution(mesh):
    return jax.shard_map(
        on_device,
        mesh=mesh,
        in_specs=(P(("grp", "dev"), None, None), P(("grp", "dev")), P()),
        out_specs=(P("grp", "dev", None), P("grp", "dev")),
        check_vma=False,
    )
```

time: 118 us -> 43.2 us (0.37)
  waiting for transfers between devices: 70.4 us -> 8.01 us
  starting transfers between devices: 0.08 us -> 14.3 us
  between operations: 14.8 us -> 0.7 us
  matrix products: 10.8 us -> 0 us
  Pallas kernels: 0 us -> 6.23 us
  other arithmetic: 4.51 us -> 0 us
  local copies, waits for them, and re-layouts: 2.68 us -> 0 us
    all_gather x1 -> x0, waiting for transfers between devices: 52.1 us -> none  [on_device(): lax.all_gather(own, 'dev', axis=0, tiled=True)]
    psum x1 -> x0, waiting for transfers between devices: 18.3 us -> none  [spread(): return lax.psum(jnp.where(mine, value, jnp.zeros_like(value)), axis)]
    ppermute x0 -> x16, starting transfers between devices: none -> 14.3 us  [flip(): lax.ppermute(value, axis, [(i, i ^ mask) for i in range(lax.axis_size(axi...]
    all_to_all x0 -> x1, blocking collectives: none -> 13.8 us  [on_device(): lax.all_to_all(results, 'dev', split_axis=0, concat_axis=0, tiled=True)]
    dot_general x5 -> x0, matrix products: 10.8 us -> none  [the longest x4 9.39 us: score_block(): jnp.einsum('ape,bqe->abpq', rows, cols, preferred_element_type=jnp.float32)]
    unnamed x1 -> x0, blocking collectives: 9.82 us -> none
    ppermute x0 -> x16, waiting for transfers between devices: none -> 8.01 us  [flip(): lax.ppermute(value, axis, [(i, i ^ mask) for i in range(lax.axis_size(axi...]
    pallas_call x0 -> x8, Pallas kernels: none -> 6.23 us  [the longest x1 2.73 us: first_step(): pl.pallas_call(functools.partial(first_kernel, len(pieces), labels, per,...]
  transfers between devices with their start and end apart: 2 -> 16, of which waited for: 2 -> 4; matrix products, arithmetic and copies ran while one was open for 1% -> 0% of each run, Pallas kernels for 0% -> 7%
where the time goes in v1:
time: 43.2 us; the launch traced here: 43 us
  starting transfers between devices  14.3 us (33%)
  blocking collectives  13.8 us (32%)
  waiting for transfers between devices  8.01 us (19%)
  Pallas kernels  6.23 us (14%)
  between operations  0.7 us (2%)
    ppermute x16, starting transfers between devices, flip(): lax.ppermute(value, axis, [(i, i ^ mask) for i in range(lax.axis_size(axi...  14.3 us
    all_to_all x1, blocking collectives, on_device(): lax.all_to_all(results, 'dev', split_axis=0, concat_axis=0, tiled=True)  13.8 us
    ppermute x16, waiting for transfers between devices, flip(): lax.ppermute(value, axis, [(i, i ^ mask) for i in range(lax.axis_size(axi...  8.01 us
    pallas_call x1, Pallas kernels, first_step(): pl.pallas_call(functools.partial(first_kernel, len(pieces), labels, per,...  2.73 us
    pallas_call x1, Pallas kernels, embed_tiles(): pl.pallas_call(embed_kernel, out_shape=jax.ShapeDtypeStruct((slides * USE...  1.73 us
    pallas_call x1, Pallas kernels, finish_step(): pl.pallas_call(functools.partial(finish_kernel, size, groups, len(pieces)...  1 us
  transfers between devices with their start and end apart: 16, of which 4 were waited for; matrix products, arithmetic and copies ran while one was open for 0% of the time, Pallas kernels for 7%

profile of v1, /device:TPU:0, one launch (start us, length us, event | category | flops | bytes accessed | tf_op | source)
XLA Modules:
  0.0 43.0 jit_solution(4089888888524357983)
XLA Ops:
  0.6 1.7 %embed.1.in_ref.refs_0_.refs_3_ = bf16[240,512]{1,0:T(8,128)(2,1)S(1)} custom-call(bf16[2,128,768]{2,1,0:T(8,128)(2,1)} %features_in.1, s32[2]{0:T(128)} %counts_in.1, bf16[768,512]{1,0:T(8,128)(2,1)} %projection_in.1), custom_call_target="tpu_custom_call" | custom-call | tf_op jit(solution)/shard_map/embed/pallas_call | solution.py:51
  2.4 3.1 %collective-permute-start.4 = (bf16[240,512]{1,0:T(8,128)(2,1)S(1)}, bf16[240,512]{1,0:T(8,128)(2,1)S(1)}, u32[]{:S(2)}, u32[]{:S(2)}) collective-permute-start(bf16[240,512]{1,0:T(8,128)(2,1)S(1)} %embed.1.in_ref.refs_0_.refs_3_), channel_id=1, source_target_pairs={{0,2},{1,3},{2,0},{3,1},{4,6},{5,7},{6,4},{7,5},{8,10},{9,11},{10,... | collective-permute-start | bytes 737288 | tf_op jit(solution)/shard_map/ppermute | solution.py:292
  5.5 2.5 %collective-permute-start = (bf16[240,512]{1,0:T(8,128)(2,1)S(1)}, bf16[240,512]{1,0:T(8,128)(2,1)S(1)}, u32[]{:S(2)}, u32[]{:S(2)}) collective-permute-start(bf16[240,512]{1,0:T(8,128)(2,1)S(1)} %embed.1.in_ref.refs_0_.refs_3_), channel_id=1, source_target_pairs={{0,6},{1,7},{2,4},{3,5},{4,2},{5,3},{6,0},{7,1},{8,14},{9,15},{10,... | collective-permute-start | bytes 737288 | tf_op jit(solution)/shard_map/ppermute | solution.py:292
  7.9 1.5 %collective-permute-start.3 = (bf16[240,512]{1,0:T(8,128)(2,1)S(1)}, bf16[240,512]{1,0:T(8,128)(2,1)S(1)}, u32[]{:S(2)}, u32[]{:S(2)}) collective-permute-start(bf16[240,512]{1,0:T(8,128)(2,1)S(1)} %embed.1.in_ref.refs_0_.refs_3_), channel_id=1, source_target_pairs={{0,16},{8,24},{16,0},{24,8},{1,17},{9,25},{17,1},{25,9},{2,18},{10... | collective-permute-start | bytes 737288 | tf_op jit(solution)/shard_map/ppermute | solution.py:292
  9.5 1.5 %collective-permute-start.2 = (bf16[240,512]{1,0:T(8,128)(2,1)S(1)}, bf16[240,512]{1,0:T(8,128)(2,1)S(1)}, u32[]{:S(2)}, u32[]{:S(2)}) collective-permute-start(bf16[240,512]{1,0:T(8,128)(2,1)S(1)} %embed.1.in_ref.refs_0_.refs_3_), channel_id=1, source_target_pairs={{0,1},{1,0},{2,3},{3,2},{4,5},{5,4},{6,7},{7,6},{8,9},{9,8},{10,11... | collective-permute-start | bytes 737288 | tf_op jit(solution)/shard_map/ppermute | solution.py:292
  10.9 0.9 %collective-permute-done.4.in_ref.refs_4_ = bf16[240,512]{1,0:T(8,128)(2,1)S(1)} collective-permute-done((bf16[240,512]{1,0:T(8,128)(2,1)S(1)}, bf16[240,512]{1,0:T(8,128)(2,1)S(1)}, u32[]{:S(2)}, u32[]{:S(2)}) %collective-permute-start.4) | collective-permute-done | bytes 245792 | tf_op jit(solution)/shard_map/ppermute | solution.py:292
  11.8 1.5 %collective-permute-start.5 = (bf16[240,512]{1,0:T(8,128)(2,1)S(1)}, bf16[240,512]{1,0:T(8,128)(2,1)S(1)}, u32[]{:S(2)}, u32[]{:S(2)}) collective-permute-start(bf16[240,512]{1,0:T(8,128)(2,1)S(1)} %collective-permute-done.4.in_ref.refs_4_), channel_id=1, source_target_pairs={{0,16},{8,24},{16,0},{24,8},{1,17},{9,25},{17,1},{25,9},{2,18},{10... | collective-permute-start | bytes 737288 | tf_op jit(solution)/shard_map/ppermute | solution.py:292
  13.4 5.6 %collective-permute-done.refs_2_ = bf16[240,512]{1,0:T(8,128)(2,1)S(1)} collective-permute-done((bf16[240,512]{1,0:T(8,128)(2,1)S(1)}, bf16[240,512]{1,0:T(8,128)(2,1)S(1)}, u32[]{:S(2)}, u32[]{:S(2)}) %collective-permute-start) | collective-permute-done | bytes 245792 | tf_op jit(solution)/shard_map/ppermute | solution.py:292
  19.0 0.0 collective-permute-start.6
  19.0 0.5 %collective-permute-start.7 = (bf16[112,512]{1,0:T(8,128)(2,1)S(1)}, bf16[112,512]{1,0:T(8,128)(2,1)S(1)}, u32[]{:S(2)}, u32[]{:S(2)}) collective-permute-start(bf16[112,512]{1,0:T(8,128)(2,1)S(1)} %get-tuple-element.36), channel_id=1, source_target_pairs={{0,8},{8,0},{16,24},{24,16},{1,9},{9,1},{17,25},{25,17},{2,10},{10... | collective-permute-start | bytes 344072 | tf_op jit(solution)/shard_map/ppermute | solution.py:292
  19.5 1.5 %collective-permute-start.1 = (bf16[240,512]{1,0:T(8,128)(2,1)S(1)}, bf16[240,512]{1,0:T(8,128)(2,1)S(1)}, u32[]{:S(2)}, u32[]{:S(2)}) collective-permute-start(bf16[240,512]{1,0:T(8,128)(2,1)S(1)} %collective-permute-done.refs_2_), channel_id=1, source_target_pairs={{0,1},{1,0},{2,3},{3,2},{4,5},{5,4},{6,7},{7,6},{8,9},{9,8},{10,11... | collective-permute-start | bytes 737288 | tf_op jit(solution)/shard_map/ppermute | solution.py:292
  21.0 0.0 collective-permute-done.2.refs_1_
  21.0 0.1 collective-permute-start.8
  21.1 0.6 %collective-permute-start.9 = (bf16[112,512]{1,0:T(8,128)(2,1)S(1)}, bf16[112,512]{1,0:T(8,128)(2,1)S(1)}, u32[]{:S(2)}, u32[]{:S(2)}) collective-permute-start(bf16[112,512]{1,0:T(8,128)(2,1)S(1)} %get-tuple-element.44), channel_id=1, source_target_pairs={{0,8},{8,0},{16,24},{24,16},{1,9},{9,1},{17,25},{25,17},{2,10},{10... | collective-permute-start | bytes 344072 | tf_op jit(solution)/shard_map/ppermute | solution.py:292
  21.7 0.1 collective-permute-start.11
  21.8 0.0 collective-permute-done.5.in_ref.refs_6_
  21.8 0.4 collective-permute-start.10
  22.2 0.4 collective-permute-done.9.refs_10_
  22.7 0.4 collective-permute-start.12
  23.0 0.0 collective-permute-done.11.refs_12_
  23.0 0.2 collective-permute-start.13
  23.2 0.0 collective-permute-done.8.refs_9_
  23.2 0.4 collective-permute-start.14
  23.5 0.0 collective-permute-done.10.refs_11_
  23.5 0.2 collective-permute-start.15
  23.7 1.1 %collective-permute-done.15.refs_16_ = bf16[48,512]{1,0:T(8,128)(2,1)S(1)} collective-permute-done((bf16[48,512]{1,0:T(8,128)(2,1)S(1)}, bf16[48,512]{1,0:T(8,128)(2,1)S(1)}, u32[]{:S(2)}, u32[]{:S(2)}) %collective-permute-start.15) | collective-permute-done | bytes 49184 | tf_op jit(solution)/shard_map/ppermute | solution.py:292
  24.8 0.0 collective-permute-done.12.refs_13_
  24.8 0.0 collective-permute-done.13.refs_14_
  24.8 2.7 %first_scores.1 = (bf16[120,16,512]{2,1,0:T(8,128)(2,1)S(1)}, f32[8,256]{1,0:T(8,128)S(1)}, f32[6,16,128]{2,1,0:T(8,128)S(1)}) custom-call(bf16[240,512]{1,0:T(8,128)(2,1)S(1)} %embed.1.in_ref.refs_0_.refs_3_, bf16[240,512]{1,0:T(8,128)(2,1)S(1)} %collective-permute-done.2.refs_1_, bf16[240,512]{1,0:T(8,128)(2,1)S(1)} %collective-permute-done.refs_2_, ...), custom_call_target="tpu_custom_call" | custom-call | tf_op jit(solution)/shard_map/first_scores/pallas_call | solution.py:187
  27.5 1.0 %finish.1 = f32[8,8,4,128]{3,2,1,0:T(4,128)S(1)} custom-call(bf16[240,512]{1,0:T(8,128)(2,1)S(1)} %collective-permute-done.1.refs_0_, bf16[120,16,512]{2,1,0:T(8,128)(2,1)S(1)} %get-tuple-element.51.refs_1_, f32[8,256]{1,0:T(8,128)S(1)} %get-tuple-element.52.refs_2_, f32[6,16,128]{2,1,0:T(8,128)S(1)} %get-tuple-element.53.refs_3_), custom_call_target="tpu_custom_call" | custom-call | tf_op jit(solution)/shard_map/finish/pallas_call | solution.py:245
  28.5 13.8 %all_to_all.5.parts = f32[8,8,4,128]{3,2,1,0:T(4,128)S(1)} all-to-all(f32[8,8,4,128]{3,2,1,0:T(4,128)S(1)} %finish.1), channel_id=1, replica_groups=mesh['grp'=4,'dev'=8] {'dev'}, dimensions={0} | all-to-all | bytes 262144 | tf_op jit(solution)/shard_map/all_to_all | solution.py:365
  42.3 0.7 %gather_results.1 = (f32[16,8,128]{2,1,0:T(8,128)}, f32[8,16]{1,0:T(8,128)}) custom-call(f32[8,8,4,128]{3,2,1,0:T(4,128)S(1)} %all_to_all.5.parts), custom_call_target="tpu_custom_call" | custom-call | tf_op jit(solution)/shard_map/gather_results/pallas_call | solution.py:278
  (9 shorter events, 0.1 us)
Async XLA Ops:
  2.4 9.4 %collective-permute-start.4 = (bf16[240,512]{1,0:T(8,128)(2,1)S(1)}, bf16[240,512]{1,0:T(8,128)(2,1)S(1)}, u32[]{:S(2)}, u32[]{:S(2)}) collective-permute-start(bf16[240,512]{1,0:T(8,128)(2,1)S(1)} %embed.1.in_ref.refs_0_.refs_3_), channel_id=1, source_target_pairs={{0,2},{1,3},{2,0},{3,1},{4,6},{5,7},{6,4},{7,5},{8,10},{9,11},{10,... | collective-permute-start | bytes 737288 | tf_op jit(solution)/shard_map/ppermute | solution.py:292
  5.5 13.5 %collective-permute-start = (bf16[240,512]{1,0:T(8,128)(2,1)S(1)}, bf16[240,512]{1,0:T(8,128)(2,1)S(1)}, u32[]{:S(2)}, u32[]{:S(2)}) collective-permute-start(bf16[240,512]{1,0:T(8,128)(2,1)S(1)} %embed.1.in_ref.refs_0_.refs_3_), channel_id=1, source_target_pairs={{0,6},{1,7},{2,4},{3,5},{4,2},{5,3},{6,0},{7,1},{8,14},{9,15},{10,... | collective-permute-start | bytes 737288 | tf_op jit(solution)/shard_map/ppermute | solution.py:292
  7.9 11.6 %collective-permute-start.3 = (bf16[240,512]{1,0:T(8,128)(2,1)S(1)}, bf16[240,512]{1,0:T(8,128)(2,1)S(1)}, u32[]{:S(2)}, u32[]{:S(2)}) collective-permute-start(bf16[240,512]{1,0:T(8,128)(2,1)S(1)} %embed.1.in_ref.refs_0_.refs_3_), channel_id=1, source_target_pairs={{0,16},{8,24},{16,0},{24,8},{1,17},{9,25},{17,1},{25,9},{2,18},{10... | collective-permute-start | bytes 737288 | tf_op jit(solution)/shard_map/ppermute | solution.py:292
  9.5 11.6 %collective-permute-start.2 = (bf16[240,512]{1,0:T(8,128)(2,1)S(1)}, bf16[240,512]{1,0:T(8,128)(2,1)S(1)}, u32[]{:S(2)}, u32[]{:S(2)}) collective-permute-start(bf16[240,512]{1,0:T(8,128)(2,1)S(1)} %embed.1.in_ref.refs_0_.refs_3_), channel_id=1, source_target_pairs={{0,1},{1,0},{2,3},{3,2},{4,5},{5,4},{6,7},{7,6},{8,9},{9,8},{10,11... | collective-permute-start | bytes 737288 | tf_op jit(solution)/shard_map/ppermute | solution.py:292
  11.8 10.0 %collective-permute-start.5 = (bf16[240,512]{1,0:T(8,128)(2,1)S(1)}, bf16[240,512]{1,0:T(8,128)(2,1)S(1)}, u32[]{:S(2)}, u32[]{:S(2)}) collective-permute-start(bf16[240,512]{1,0:T(8,128)(2,1)S(1)} %collective-permute-done.4.in_ref.refs_4_), channel_id=1, source_target_pairs={{0,16},{8,24},{16,0},{24,8},{1,17},{9,25},{17,1},{25,9},{2,18},{10... | collective-permute-start | bytes 737288 | tf_op jit(solution)/shard_map/ppermute | solution.py:292
  19.0 2.7 %collective-permute-start.6 = (bf16[128,512]{1,0:T(8,128)(2,1)S(1)}, bf16[128,512]{1,0:T(8,128)(2,1)S(1)}, u32[]{:S(2)}, u32[]{:S(2)}) collective-permute-start(bf16[128,512]{1,0:T(8,128)(2,1)S(1)} %get-tuple-element.35), channel_id=1, source_target_pairs={{0,8},{8,0},{16,24},{24,16},{1,9},{9,1},{17,25},{25,17},{2,10},{10... | collective-permute-start | bytes 393224 | tf_op jit(solution)/shard_map/ppermute | solution.py:292
  19.0 2.1 %collective-permute-start.7 = (bf16[112,512]{1,0:T(8,128)(2,1)S(1)}, bf16[112,512]{1,0:T(8,128)(2,1)S(1)}, u32[]{:S(2)}, u32[]{:S(2)}) collective-permute-start(bf16[112,512]{1,0:T(8,128)(2,1)S(1)} %get-tuple-element.36), channel_id=1, source_target_pairs={{0,8},{8,0},{16,24},{24,16},{1,9},{9,1},{17,25},{25,17},{2,10},{10... | collective-permute-start | bytes 344072 | tf_op jit(solution)/shard_map/ppermute | solution.py:292
  19.5 8.0 %collective-permute-start.1 = (bf16[240,512]{1,0:T(8,128)(2,1)S(1)}, bf16[240,512]{1,0:T(8,128)(2,1)S(1)}, u32[]{:S(2)}, u32[]{:S(2)}) collective-permute-start(bf16[240,512]{1,0:T(8,128)(2,1)S(1)} %collective-permute-done.refs_2_), channel_id=1, source_target_pairs={{0,1},{1,0},{2,3},{3,2},{4,5},{5,4},{6,7},{7,6},{8,9},{9,8},{10,11... | collective-permute-start | bytes 737288 | tf_op jit(solution)/shard_map/ppermute | solution.py:292
  21.0 2.2 %collective-permute-start.8 = (bf16[128,512]{1,0:T(8,128)(2,1)S(1)}, bf16[128,512]{1,0:T(8,128)(2,1)S(1)}, u32[]{:S(2)}, u32[]{:S(2)}) collective-permute-start(bf16[128,512]{1,0:T(8,128)(2,1)S(1)} %get-tuple-element.43), channel_id=1, source_target_pairs={{0,8},{8,0},{16,24},{24,16},{1,9},{9,1},{17,25},{25,17},{2,10},{10... | collective-permute-start | bytes 393224 | tf_op jit(solution)/shard_map/ppermute | solution.py:292
  21.1 1.5 %collective-permute-start.9 = (bf16[112,512]{1,0:T(8,128)(2,1)S(1)}, bf16[112,512]{1,0:T(8,128)(2,1)S(1)}, u32[]{:S(2)}, u32[]{:S(2)}) collective-permute-start(bf16[112,512]{1,0:T(8,128)(2,1)S(1)} %get-tuple-element.44), channel_id=1, source_target_pairs={{0,8},{8,0},{16,24},{24,16},{1,9},{9,1},{17,25},{25,17},{2,10},{10... | collective-permute-start | bytes 344072 | tf_op jit(solution)/shard_map/ppermute | solution.py:292
  21.7 1.3 %collective-permute-start.11 = (bf16[112,512]{1,0:T(8,128)(2,1)S(1)}, bf16[112,512]{1,0:T(8,128)(2,1)S(1)}, u32[]{:S(2)}, u32[]{:S(2)}) collective-permute-start(bf16[112,512]{1,0:T(8,128)(2,1)S(1)} %get-tuple-element.46), channel_id=1, source_target_pairs={{0,8},{8,0},{16,24},{24,16},{1,9},{9,1},{17,25},{25,17},{2,10},{10... | collective-permute-start | bytes 344072 | tf_op jit(solution)/shard_map/ppermute | solution.py:292
  21.8 1.8 %collective-permute-start.10 = (bf16[128,512]{1,0:T(8,128)(2,1)S(1)}, bf16[128,512]{1,0:T(8,128)(2,1)S(1)}, u32[]{:S(2)}, u32[]{:S(2)}) collective-permute-start(bf16[128,512]{1,0:T(8,128)(2,1)S(1)} %get-tuple-element.45), channel_id=1, source_target_pairs={{0,8},{8,0},{16,24},{24,16},{1,9},{9,1},{17,25},{25,17},{2,10},{10... | collective-permute-start | bytes 393224 | tf_op jit(solution)/shard_map/ppermute | solution.py:292
  22.7 2.1 %collective-permute-start.12 = (bf16[64,512]{1,0:T(8,128)(2,1)S(1)}, bf16[64,512]{1,0:T(8,128)(2,1)S(1)}, u32[]{:S(2)}, u32[]{:S(2)}) collective-permute-start(bf16[64,512]{1,0:T(8,128)(2,1)S(1)} %get-tuple-element.47), channel_id=1, source_target_pairs={{0,8},{8,0},{16,24},{24,16},{1,9},{9,1},{17,25},{25,17},{2,10},{10... | collective-permute-start | bytes 196616 | tf_op jit(solution)/shard_map/ppermute | solution.py:292
  23.0 1.8 %collective-permute-start.13 = (bf16[64,512]{1,0:T(8,128)(2,1)S(1)}, bf16[64,512]{1,0:T(8,128)(2,1)S(1)}, u32[]{:S(2)}, u32[]{:S(2)}) collective-permute-start(bf16[64,512]{1,0:T(8,128)(2,1)S(1)} %get-tuple-element.48), channel_id=1, source_target_pairs={{0,8},{8,0},{16,24},{24,16},{1,9},{9,1},{17,25},{25,17},{2,10},{10... | collective-permute-start | bytes 196616 | tf_op jit(solution)/shard_map/ppermute | solution.py:292
  23.2 1.6 %collective-permute-start.14 = (bf16[64,512]{1,0:T(8,128)(2,1)S(1)}, bf16[64,512]{1,0:T(8,128)(2,1)S(1)}, u32[]{:S(2)}, u32[]{:S(2)}) collective-permute-start(bf16[64,512]{1,0:T(8,128)(2,1)S(1)} %get-tuple-element.49), channel_id=1, source_target_pairs={{0,8},{8,0},{16,24},{24,16},{1,9},{9,1},{17,25},{25,17},{2,10},{10... | collective-permute-start | bytes 196616 | tf_op jit(solution)/shard_map/ppermute | solution.py:292
  23.5 1.2 %collective-permute-start.15 = (bf16[48,512]{1,0:T(8,128)(2,1)S(1)}, bf16[48,512]{1,0:T(8,128)(2,1)S(1)}, u32[]{:S(2)}, u32[]{:S(2)}) collective-permute-start(bf16[48,512]{1,0:T(8,128)(2,1)S(1)} %get-tuple-element.50), channel_id=1, source_target_pairs={{0,8},{8,0},{16,24},{24,16},{1,9},{9,1},{17,25},{25,17},{2,10},{10... | collective-permute-start | bytes 147464 | tf_op jit(solution)/shard_map/ppermute | solution.py:292

commit v2 on v1

--- a/solution.py
+++ b/solution.py
@@ -11,7 +11,8 @@
 CHUNK = 16
 TAIL = 8
 MAIN = USED - TAIL
-MARK = 4.0
+MARK = 128.0
+LANES = 128
 VMEM_LIMIT = 40 * 1024 * 1024
 NT = (((1,), (1,)), ((), ()))
 VMEM = pl.BlockSpec(memory_space=pltpu.VMEM)
@@ -38,8 +39,8 @@
         unit = raw * scale
         slot = lax.broadcasted_iota(jnp.int32, unit.shape, 0)
         lane = lax.broadcasted_iota(jnp.int32, unit.shape, 1)
-        filled = slot < counts_ref[s]
-        unit = jnp.where(filled, unit, jnp.where(lane == 0, MARK, unit[:1]))
+        count = counts_ref[s]
+        unit = jnp.where(slot < count, unit, jnp.where(lane == 0, MARK + count.astype(jnp.float32), unit[:1]))
         out_ref[pl.ds(s * MAIN, MAIN), :] = unit[:MAIN].astype(out_ref.dtype)
         tails.append(unit[MAIN:USED])
     out_ref[pl.ds(slides * MAIN, slides * TAIL), :] = jnp.concatenate(tails, axis=0).astype(out_ref.dtype)
@@ -64,109 +65,86 @@
     )(*[pltpu.with_memory_space_constraint(x, pltpu.HBM) for x in (features, tile_counts, projection)])
 
 
-def marked(part):
-    return part[:, :1] > 0.5 * MARK
-
-
-def count_rows(flags, s, per):
-    own = [flags[s * MAIN : (s + 1) * MAIN], flags[per * MAIN + s * TAIL : per * MAIN + (s + 1) * TAIL]]
-    return sum(jnp.sum(jnp.where(flag, 0.0, 1.0), axis=0, keepdims=True) for flag in own)
+def slide_count(head, row):
+    value = head[row : row + 1, :1]
+    return jnp.where(value > 2.0, value - MARK, float(USED))
+
+
+def unmark(head, top):
+    column = lax.broadcasted_iota(jnp.int32, head.shape, 1)
+    return jnp.where(jnp.logical_and(column == 0, head > 2.0), top, head)
 
 
 def lay_columns(blocks, labels, per, cols, weight_ref):
-    tiles, _, width = cols.shape
-    chunks = MAIN // CHUNK
-    col_slides = tiles * CHUNK // USED
+    chunks, col_slides, _, _ = cols.shape
     span = col_slides * CHUNK
     mine = lax.axis_index("grp")
     lane = lax.broadcasted_iota(jnp.int32, (1, span), 1)
-    row = lax.broadcasted_iota(jnp.int32, (CHUNK, width), 0)
-    column = lax.broadcasted_iota(jnp.int32, (CHUNK, width), 1)
     counts = jnp.ones((1, span), jnp.float32)
-    tail_counts = jnp.ones((1, span // 2), jnp.float32)
     whole = {}
     for (mask, pair, offset), block in zip(labels, blocks):
         for start in range(0, block.shape[0], CHUNK):
-            whole.setdefault((mask, pair), {})[offset + start] = block[pl.ds(start, CHUNK), :]
+            whole.setdefault((mask, pair), {})[offset + start] = block, start
     for (mask, pair), parts in whole.items():
         first = ((mine ^ mask) * 2 + pair) * per
-        parts = {start: part.astype(jnp.float32) for start, part in parts.items()}
-        flags = jnp.concatenate([marked(parts[start]).astype(jnp.float32) for start in sorted(parts)], axis=0) > 0.5
-        tops = [parts[s * MAIN][:1] for s in range(per)]
-        for s in range(per):
-            count = count_rows(flags, s, per)
-            counts = jnp.where(lane // CHUNK == first + s, count, counts)
-            tail_counts = jnp.where(lane[:, : span // 2] // TAIL == first + s, count, tail_counts)
-        for start, part in parts.items():
-            flag = jnp.logical_and(marked(part), column == 0)
-            if start < per * MAIN:
-                s, k = start // MAIN, start % MAIN // CHUNK
-                top, index = tops[s], k * col_slides + first + s
-            else:
-                s = (start - per * MAIN) // TAIL
-                top = jnp.where(row < TAIL, tops[s], tops[s + 1])
-                index = chunks * col_slides + (first + s) // 2
-            cols[index] = jnp.where(flag, top, part).astype(cols.dtype)
+        heads = {spot: ref[pl.ds(start, CHUNK), :LANES].astype(jnp.float32) for spot, (ref, start) in parts.items()}
+        tops = [heads[s * MAIN][:1] for s in range(per)]
+        for spot, (ref, start) in parts.items():
+            if spot < per * MAIN:
+                s, k = spot // MAIN, spot % MAIN // CHUNK
+                cols[k, first + s, :, :LANES] = unmark(heads[spot], tops[s]).astype(cols.dtype)
+                cols[k, first + s, :, LANES:] = ref[pl.ds(start, CHUNK), LANES:]
+                continue
+            tail = ref[pl.ds(start, CHUNK), :].astype(jnp.float32)
+            for n in range(CHUNK // TAIL):
+                s = (spot - per * MAIN) // TAIL + n
+                count = slide_count(heads[spot], (n + 1) * TAIL - 1)
+                counts = jnp.where(lane // CHUNK == first + s, count, counts)
+                own = tail[n * TAIL : (n + 1) * TAIL]
+                own = jnp.concatenate([unmark(own[:, :LANES], tops[s]), own[:, LANES:]], axis=1)
+                cols[chunks - 1, first + s] = jnp.concatenate([own, own], axis=0).astype(cols.dtype)
     for k in range(chunks):
         tile = (k * CHUNK + lane % CHUNK).astype(jnp.float32)
         weight_ref[pl.ds(k, 1), :] = jnp.where(tile < counts, 0.5 / counts, 0.0)
-    tile = (MAIN + lane % TAIL).astype(jnp.float32)[:, : span // 2]
-    weight_ref[pl.ds(chunks, 1), : span // 2] = jnp.where(tile < tail_counts, 0.5 / tail_counts, 0.0)
-
-
-def unmark(piece, per):
-    head = piece[:, :128].astype(jnp.float32)
-    flag = marked(head)
-    row = lax.broadcasted_iota(jnp.int32, head.shape, 0)
-    column = lax.broadcasted_iota(jnp.int32, head.shape, 1)
-    top = head[:1]
-    for s in range(1, per):
-        here = jnp.where(row < per * MAIN, row // MAIN, (row - per * MAIN) // TAIL) == s
-        top = jnp.where(here, head[s * MAIN : s * MAIN + 1], top)
-    head = jnp.where(jnp.logical_and(flag, column == 0), top, head).astype(piece.dtype)
-    return jnp.concatenate([head, piece[:, 128:]], axis=1), [count_rows(flag, s, per) for s in range(per)]
+
+
+def clean_rows(piece, per):
+    head = piece[:, :LANES].astype(jnp.float32)
+    counts = [slide_count(head, per * MAIN + (s + 1) * TAIL - 1) for s in range(per)]
+    parts = [unmark(head[s * MAIN : (s + 1) * MAIN], head[s * MAIN : s * MAIN + 1]) for s in range(per)]
+    for s in range(per):
+        start = per * MAIN + s * TAIL
+        parts.append(unmark(head[start : start + TAIL], head[s * MAIN : s * MAIN + 1]))
+    head = jnp.concatenate(parts, axis=0).astype(piece.dtype)
+    return jnp.concatenate([head, piece[:, LANES:]], axis=1), counts
 
 
 def score_pieces(pieces, cols, weight_ref, per, slots, put):
-    tiles, _, width = cols.shape
-    chunks = MAIN // CHUNK
-    col_slides = tiles * CHUNK // USED
+    chunks, col_slides, _, width = cols.shape
     span = col_slides * CHUNK
-    flat = cols[...].reshape(tiles * CHUNK, width)
+    flat = cols[...].reshape(chunks * span, width)
     tile = lax.broadcasted_iota(jnp.int32, (1, slots), 1)
     lane = lax.broadcasted_iota(jnp.int32, (col_slides, span), 1)
     slide = lax.broadcasted_iota(jnp.int32, (col_slides, span), 0)
-    clean = [unmark(piece[...], per) for piece in pieces]
+    clean = [clean_rows(piece[...], per) for piece in pieces]
     rows = jnp.concatenate([block for block, _ in clean], axis=0)
     score = lax.dot_general(rows, flat, NT, preferred_element_type=jnp.float32)
     parts = [score[:, k * span : (k + 1) * span] for k in range(chunks)]
-    last = score[:, chunks * span :]
     best = functools.reduce(jnp.maximum, parts)
     for t in range(len(pieces) * per):
         base, s = t // per * per * USED, t % per
         spots = (base + s * MAIN, MAIN), (base + per * MAIN + s * TAIL, TAIL)
         count = clean[t // per][1][s]
-
-        def gathered(values):
-            own = [values[start : start + size] for start, size in spots]
-            return jnp.concatenate([*own, jnp.zeros((slots - USED, values.shape[1]), jnp.float32)], axis=0).T
-
-        def highest(values):
-            return functools.reduce(
-                jnp.maximum, [jnp.max(values[start : start + size], axis=0, keepdims=True) for start, size in spots]
-            )
-
-        mine = jnp.maximum(
-            jnp.max(gathered(best).reshape(col_slides, CHUNK, slots), axis=1),
-            jnp.max(gathered(last).reshape(col_slides, TAIL, slots), axis=1),
-        )
+        mine = [best[start : start + size] for start, size in spots]
+        mine = jnp.concatenate([*mine, jnp.zeros((slots - USED, span), jnp.float32)], axis=0).T
+        mine = jnp.max(mine.reshape(col_slides, CHUNK, slots), axis=1)
         mine = jnp.where(tile.astype(jnp.float32) < count, mine, 0.0)
-        back = functools.reduce(jnp.add, [highest(part) * weight_ref[pl.ds(k, 1), :] for k, part in enumerate(parts)])
-        rest = highest(last) * weight_ref[pl.ds(chunks, 1), : span // 2]
-        mean = jnp.sum(mine * (0.5 / count), axis=1, keepdims=True)
-        mean = mean + jnp.sum(jnp.where(lane // CHUNK == slide, back, 0.0), axis=1, keepdims=True)
-        half = slice(0, span // 2)
-        mean = mean + jnp.sum(jnp.where(lane[:, half] // TAIL == slide[:, half], rest, 0.0), axis=1, keepdims=True)
+        back = []
+        for k, part in enumerate(parts):
+            highest = [jnp.max(part[start : start + size], axis=0, keepdims=True) for start, size in spots]
+            back.append(functools.reduce(jnp.maximum, highest) * weight_ref[pl.ds(k, 1), :])
+        back = jnp.where(lane // CHUNK == slide, functools.reduce(jnp.add, back), 0.0)
+        mean = jnp.sum(mine * (0.5 / count), axis=1, keepdims=True) + jnp.sum(back, axis=1, keepdims=True)
         put(t, jnp.where(tile == slots - 1, mean, mine))
 
 
@@ -182,13 +160,13 @@
 
 def first_step(pieces, columns, labels, per, slots):
     count = len(pieces) * per
-    rows, width = sum(block.shape[0] for block in columns), columns[0].shape[1]
-    col_slides = rows // USED
+    chunks, width = slots // CHUNK, columns[0].shape[1]
+    col_slides = sum(block.shape[0] for block in columns) // USED
     return pl.pallas_call(
         functools.partial(first_kernel, len(pieces), labels, per, slots),
         out_shape=(
-            jax.ShapeDtypeStruct((rows // CHUNK, CHUNK, width), columns[0].dtype),
-            jax.ShapeDtypeStruct((MAIN // CHUNK + 1, col_slides * CHUNK), jnp.float32),
+            jax.ShapeDtypeStruct((chunks, col_slides, CHUNK, width), columns[0].dtype),
+            jax.ShapeDtypeStruct((chunks, col_slides * CHUNK), jnp.float32),
             jax.ShapeDtypeStruct((count, col_slides, slots), jnp.float32),
         ),
         in_specs=[VMEM] * (len(pieces) + len(columns)),
@@ -211,7 +189,7 @@
     count = len(pieces) * per
     return pl.pallas_call(
         functools.partial(score_kernel, len(pieces), per, slots),
-        out_shape=jax.ShapeDtypeStruct((count, cols.shape[0] * CHUNK // USED, slots), jnp.float32),
+        out_shape=jax.ShapeDtypeStruct((count, cols.shape[1], slots), jnp.float32),
         in_specs=[VMEM] * (len(pieces) + 2),
         out_specs=VMEM,
         compiler_params=PARAMS,

time: 43.2 us -> 42.8 us (level)
  transfers between devices with their start and end apart: 16 -> 16, of which waited for: 4 -> 5; matrix products, arithmetic and copies ran while one was open for 0% -> 0% of each run, Pallas kernels for 7% -> 6%
where the time goes in v2:
time: 42.8 us; the launch traced here: 42.7 us
  starting transfers between devices  14.3 us (33%)
  blocking collectives  13.6 us (32%)
  waiting for transfers between devices  8.19 us (19%)
  Pallas kernels  5.86 us (14%)
  between operations  0.7 us (2%)
    ppermute x16, starting transfers between devices, flip(): lax.ppermute(value, axis, [(i, i ^ mask) for i in range(lax.axis_size(axi...  14.3 us
    all_to_all x1, blocking collectives, on_device(): lax.all_to_all(results, 'dev', split_axis=0, concat_axis=0, tiled=True)  13.6 us
    ppermute x16, waiting for transfers between devices, flip(): lax.ppermute(value, axis, [(i, i ^ mask) for i in range(lax.axis_size(axi...  8.19 us
    pallas_call x1, Pallas kernels, first_step(): pl.pallas_call(functools.partial(first_kernel, len(pieces), labels, per,...  2.4 us
    pallas_call x1, Pallas kernels, embed_tiles(): pl.pallas_call(embed_kernel, out_shape=jax.ShapeDtypeStruct((slides * USE...  1.73 us
    pallas_call x1, Pallas kernels, finish_step(): pl.pallas_call(functools.partial(finish_kernel, size, groups, len(pieces)...  0.96 us
  transfers between devices with their start and end apart: 16, of which 5 were waited for; matrix products, arithmetic and copies ran while one was open for 0% of the time, Pallas kernels for 6%

profile of v2, /device:TPU:0, one launch (start us, length us, event | category | flops | bytes accessed | tf_op | source)
XLA Modules:
  0.0 42.7 jit_solution(16043777331831956297)
XLA Ops:
  0.6 1.7 %embed.1.in_ref.refs_0_.refs_3_ = bf16[240,512]{1,0:T(8,128)(2,1)S(1)} custom-call(bf16[2,128,768]{2,1,0:T(8,128)(2,1)} %features_in.1, s32[2]{0:T(128)} %counts_in.1, bf16[768,512]{1,0:T(8,128)(2,1)} %projection_in.1), custom_call_target="tpu_custom_call" | custom-call | tf_op jit(solution)/shard_map/embed/pallas_call | solution.py:52
  2.4 3.1 %collective-permute-start.4 = (bf16[240,512]{1,0:T(8,128)(2,1)S(1)}, bf16[240,512]{1,0:T(8,128)(2,1)S(1)}, u32[]{:S(2)}, u32[]{:S(2)}) collective-permute-start(bf16[240,512]{1,0:T(8,128)(2,1)S(1)} %embed.1.in_ref.refs_0_.refs_3_), channel_id=1, source_target_pairs={{0,2},{1,3},{2,0},{3,1},{4,6},{5,7},{6,4},{7,5},{8,10},{9,11},{10,... | collective-permute-start | bytes 737288 | tf_op jit(solution)/shard_map/ppermute | solution.py:270
  5.5 2.5 %collective-permute-start = (bf16[240,512]{1,0:T(8,128)(2,1)S(1)}, bf16[240,512]{1,0:T(8,128)(2,1)S(1)}, u32[]{:S(2)}, u32[]{:S(2)}) collective-permute-start(bf16[240,512]{1,0:T(8,128)(2,1)S(1)} %embed.1.in_ref.refs_0_.refs_3_), channel_id=1, source_target_pairs={{0,6},{1,7},{2,4},{3,5},{4,2},{5,3},{6,0},{7,1},{8,14},{9,15},{10,... | collective-permute-start | bytes 737288 | tf_op jit(solution)/shard_map/ppermute | solution.py:270
  7.9 1.5 %collective-permute-start.3 = (bf16[240,512]{1,0:T(8,128)(2,1)S(1)}, bf16[240,512]{1,0:T(8,128)(2,1)S(1)}, u32[]{:S(2)}, u32[]{:S(2)}) collective-permute-start(bf16[240,512]{1,0:T(8,128)(2,1)S(1)} %embed.1.in_ref.refs_0_.refs_3_), channel_id=1, source_target_pairs={{0,16},{8,24},{16,0},{24,8},{1,17},{9,25},{17,1},{25,9},{2,18},{10... | collective-permute-start | bytes 737288 | tf_op jit(solution)/shard_map/ppermute | solution.py:270
  9.5 1.5 %collective-permute-start.2 = (bf16[240,512]{1,0:T(8,128)(2,1)S(1)}, bf16[240,512]{1,0:T(8,128)(2,1)S(1)}, u32[]{:S(2)}, u32[]{:S(2)}) collective-permute-start(bf16[240,512]{1,0:T(8,128)(2,1)S(1)} %embed.1.in_ref.refs_0_.refs_3_), channel_id=1, source_target_pairs={{0,1},{1,0},{2,3},{3,2},{4,5},{5,4},{6,7},{7,6},{8,9},{9,8},{10,11... | collective-permute-start | bytes 737288 | tf_op jit(solution)/shard_map/ppermute | solution.py:270
  10.9 0.9 %collective-permute-done.4.in_ref.refs_4_ = bf16[240,512]{1,0:T(8,128)(2,1)S(1)} collective-permute-done((bf16[240,512]{1,0:T(8,128)(2,1)S(1)}, bf16[240,512]{1,0:T(8,128)(2,1)S(1)}, u32[]{:S(2)}, u32[]{:S(2)}) %collective-permute-start.4) | collective-permute-done | bytes 245792 | tf_op jit(solution)/shard_map/ppermute | solution.py:270
  11.8 1.5 %collective-permute-start.5 = (bf16[240,512]{1,0:T(8,128)(2,1)S(1)}, bf16[240,512]{1,0:T(8,128)(2,1)S(1)}, u32[]{:S(2)}, u32[]{:S(2)}) collective-permute-start(bf16[240,512]{1,0:T(8,128)(2,1)S(1)} %collective-permute-done.4.in_ref.refs_4_), channel_id=1, source_target_pairs={{0,16},{8,24},{16,0},{24,8},{1,17},{9,25},{17,1},{25,9},{2,18},{10... | collective-permute-start | bytes 737288 | tf_op jit(solution)/shard_map/ppermute | solution.py:270
  13.4 5.6 %collective-permute-done.refs_2_ = bf16[240,512]{1,0:T(8,128)(2,1)S(1)} collective-permute-done((bf16[240,512]{1,0:T(8,128)(2,1)S(1)}, bf16[240,512]{1,0:T(8,128)(2,1)S(1)}, u32[]{:S(2)}, u32[]{:S(2)}) %collective-permute-start) | collective-permute-done | bytes 245792 | tf_op jit(solution)/shard_map/ppermute | solution.py:270
  19.0 0.0 collective-permute-start.6
  19.0 0.5 %collective-permute-start.7 = (bf16[112,512]{1,0:T(8,128)(2,1)S(1)}, bf16[112,512]{1,0:T(8,128)(2,1)S(1)}, u32[]{:S(2)}, u32[]{:S(2)}) collective-permute-start(bf16[112,512]{1,0:T(8,128)(2,1)S(1)} %get-tuple-element.36), channel_id=1, source_target_pairs={{0,8},{8,0},{16,24},{24,16},{1,9},{9,1},{17,25},{25,17},{2,10},{10... | collective-permute-start | bytes 344072 | tf_op jit(solution)/shard_map/ppermute | solution.py:270
  19.5 1.5 %collective-permute-start.1 = (bf16[240,512]{1,0:T(8,128)(2,1)S(1)}, bf16[240,512]{1,0:T(8,128)(2,1)S(1)}, u32[]{:S(2)}, u32[]{:S(2)}) collective-permute-start(bf16[240,512]{1,0:T(8,128)(2,1)S(1)} %collective-permute-done.refs_2_), channel_id=1, source_target_pairs={{0,1},{1,0},{2,3},{3,2},{4,5},{5,4},{6,7},{7,6},{8,9},{9,8},{10,11... | collective-permute-start | bytes 737288 | tf_op jit(solution)/shard_map/ppermute | solution.py:270
  21.0 0.0 collective-permute-done.2.refs_1_
  21.0 0.1 collective-permute-start.8
  21.1 0.6 %collective-permute-start.9 = (bf16[112,512]{1,0:T(8,128)(2,1)S(1)}, bf16[112,512]{1,0:T(8,128)(2,1)S(1)}, u32[]{:S(2)}, u32[]{:S(2)}) collective-permute-start(bf16[112,512]{1,0:T(8,128)(2,1)S(1)} %get-tuple-element.44), channel_id=1, source_target_pairs={{0,8},{8,0},{16,24},{24,16},{1,9},{9,1},{17,25},{25,17},{2,10},{10... | collective-permute-start | bytes 344072 | tf_op jit(solution)/shard_map/ppermute | solution.py:270
  21.7 0.1 collective-permute-start.11
  21.8 0.0 collective-permute-done.5.in_ref.refs_6_
  21.8 0.4 collective-permute-start.10
  22.2 0.4 %collective-permute-done.9.refs_10_ = bf16[112,512]{1,0:T(8,128)(2,1)S(1)} collective-permute-done((bf16[112,512]{1,0:T(8,128)(2,1)S(1)}, bf16[112,512]{1,0:T(8,128)(2,1)S(1)}, u32[]{:S(2)}, u32[]{:S(2)}) %collective-permute-start.9) | collective-permute-done | bytes 114720 | tf_op jit(solution)/shard_map/ppermute | solution.py:270
  22.7 0.4 collective-permute-start.12
  23.0 0.0 collective-permute-done.11.refs_12_
  23.0 0.2 collective-permute-start.13
  23.2 0.0 collective-permute-done.8.refs_9_
  23.2 0.4 collective-permute-start.14
  23.5 0.0 collective-permute-done.10.refs_11_
  23.5 0.2 collective-permute-start.15
  23.7 1.1 %collective-permute-done.15.refs_16_ = bf16[48,512]{1,0:T(8,128)(2,1)S(1)} collective-permute-done((bf16[48,512]{1,0:T(8,128)(2,1)S(1)}, bf16[48,512]{1,0:T(8,128)(2,1)S(1)}, u32[]{:S(2)}, u32[]{:S(2)}) %collective-permute-start.15) | collective-permute-done | bytes 49184 | tf_op jit(solution)/shard_map/ppermute | solution.py:270
  24.8 0.0 collective-permute-done.12.refs_13_
  24.8 2.4 %first_scores.1 = (bf16[8,16,16,512]{3,2,1,0:T(8,128)(2,1)S(1)}, f32[8,256]{1,0:T(8,128)S(1)}, f32[6,16,128]{2,1,0:T(8,128)S(1)}) custom-call(bf16[240,512]{1,0:T(8,128)(2,1)S(1)} %embed.1.in_ref.refs_0_.refs_3_, bf16[240,512]{1,0:T(8,128)(2,1)S(1)} %collective-permute-done.2.refs_1_, bf16[240,512]{1,0:T(8,128)(2,1)S(1)} %collective-permute-done.refs_2_, ...), custom_call_target="tpu_custom_call" | custom-call | tf_op jit(solution)/shard_map/first_scores/pallas_call | solution.py:165
  27.2 0.2 collective-permute-done.1.refs_0_
  27.4 1.0 %finish.1 = f32[8,8,4,128]{3,2,1,0:T(4,128)S(1)} custom-call(bf16[240,512]{1,0:T(8,128)(2,1)S(1)} %collective-permute-done.1.refs_0_, bf16[8,16,16,512]{3,2,1,0:T(8,128)(2,1)S(1)} %get-tuple-element.51.refs_1_, f32[8,256]{1,0:T(8,128)S(1)} %get-tuple-element.52.refs_2_, f32[6,16,128]{2,1,0:T(8,128)S(1)} %get-tuple-element.53.refs_3_), custom_call_target="tpu_custom_call" | custom-call | tf_op jit(solution)/shard_map/finish/pallas_call | solution.py:223
  28.3 13.6 %all_to_all.5.parts = f32[8,8,4,128]{3,2,1,0:T(4,128)S(1)} all-to-all(f32[8,8,4,128]{3,2,1,0:T(4,128)S(1)} %finish.1), channel_id=1, replica_groups=mesh['grp'=4,'dev'=8] {'dev'}, dimensions={0} | all-to-all | bytes 262144 | tf_op jit(solution)/shard_map/all_to_all | solution.py:343
  42.0 0.7 %gather_results.1 = (f32[16,8,128]{2,1,0:T(8,128)}, f32[8,16]{1,0:T(8,128)}) custom-call(f32[8,8,4,128]{3,2,1,0:T(4,128)S(1)} %all_to_all.5.parts), custom_call_target="tpu_custom_call" | custom-call | tf_op jit(solution)/shard_map/gather_results/pallas_call | solution.py:256
  (9 shorter events, 0.1 us)
Async XLA Ops:
  2.4 9.4 %collective-permute-start.4 = (bf16[240,512]{1,0:T(8,128)(2,1)S(1)}, bf16[240,512]{1,0:T(8,128)(2,1)S(1)}, u32[]{:S(2)}, u32[]{:S(2)}) collective-permute-start(bf16[240,512]{1,0:T(8,128)(2,1)S(1)} %embed.1.in_ref.refs_0_.refs_3_), channel_id=1, source_target_pairs={{0,2},{1,3},{2,0},{3,1},{4,6},{5,7},{6,4},{7,5},{8,10},{9,11},{10,... | collective-permute-start | bytes 737288 | tf_op jit(solution)/shard_map/ppermute | solution.py:270
  5.5 13.5 %collective-permute-start = (bf16[240,512]{1,0:T(8,128)(2,1)S(1)}, bf16[240,512]{1,0:T(8,128)(2,1)S(1)}, u32[]{:S(2)}, u32[]{:S(2)}) collective-permute-start(bf16[240,512]{1,0:T(8,128)(2,1)S(1)} %embed.1.in_ref.refs_0_.refs_3_), channel_id=1, source_target_pairs={{0,6},{1,7},{2,4},{3,5},{4,2},{5,3},{6,0},{7,1},{8,14},{9,15},{10,... | collective-permute-start | bytes 737288 | tf_op jit(solution)/shard_map/ppermute | solution.py:270
  7.9 11.6 %collective-permute-start.3 = (bf16[240,512]{1,0:T(8,128)(2,1)S(1)}, bf16[240,512]{1,0:T(8,128)(2,1)S(1)}, u32[]{:S(2)}, u32[]{:S(2)}) collective-permute-start(bf16[240,512]{1,0:T(8,128)(2,1)S(1)} %embed.1.in_ref.refs_0_.refs_3_), channel_id=1, source_target_pairs={{0,16},{8,24},{16,0},{24,8},{1,17},{9,25},{17,1},{25,9},{2,18},{10... | collective-permute-start | bytes 737288 | tf_op jit(solution)/shard_map/ppermute | solution.py:270
  9.5 11.6 %collective-permute-start.2 = (bf16[240,512]{1,0:T(8,128)(2,1)S(1)}, bf16[240,512]{1,0:T(8,128)(2,1)S(1)}, u32[]{:S(2)}, u32[]{:S(2)}) collective-permute-start(bf16[240,512]{1,0:T(8,128)(2,1)S(1)} %embed.1.in_ref.refs_0_.refs_3_), channel_id=1, source_target_pairs={{0,1},{1,0},{2,3},{3,2},{4,5},{5,4},{6,7},{7,6},{8,9},{9,8},{10,11... | collective-permute-start | bytes 737288 | tf_op jit(solution)/shard_map/ppermute | solution.py:270
  11.8 10.0 %collective-permute-start.5 = (bf16[240,512]{1,0:T(8,128)(2,1)S(1)}, bf16[240,512]{1,0:T(8,128)(2,1)S(1)}, u32[]{:S(2)}, u32[]{:S(2)}) collective-permute-start(bf16[240,512]{1,0:T(8,128)(2,1)S(1)} %collective-permute-done.4.in_ref.refs_4_), channel_id=1, source_target_pairs={{0,16},{8,24},{16,0},{24,8},{1,17},{9,25},{17,1},{25,9},{2,18},{10... | collective-permute-start | bytes 737288 | tf_op jit(solution)/shard_map/ppermute | solution.py:270
  19.0 2.7 %collective-permute-start.6 = (bf16[128,512]{1,0:T(8,128)(2,1)S(1)}, bf16[128,512]{1,0:T(8,128)(2,1)S(1)}, u32[]{:S(2)}, u32[]{:S(2)}) collective-permute-start(bf16[128,512]{1,0:T(8,128)(2,1)S(1)} %get-tuple-element.35), channel_id=1, source_target_pairs={{0,8},{8,0},{16,24},{24,16},{1,9},{9,1},{17,25},{25,17},{2,10},{10... | collective-permute-start | bytes 393224 | tf_op jit(solution)/shard_map/ppermute | solution.py:270
  19.0 2.1 %collective-permute-start.7 = (bf16[112,512]{1,0:T(8,128)(2,1)S(1)}, bf16[112,512]{1,0:T(8,128)(2,1)S(1)}, u32[]{:S(2)}, u32[]{:S(2)}) collective-permute-start(bf16[112,512]{1,0:T(8,128)(2,1)S(1)} %get-tuple-element.36), channel_id=1, source_target_pairs={{0,8},{8,0},{16,24},{24,16},{1,9},{9,1},{17,25},{25,17},{2,10},{10... | collective-permute-start | bytes 344072 | tf_op jit(solution)/shard_map/ppermute | solution.py:270
  19.5 7.9 %collective-permute-start.1 = (bf16[240,512]{1,0:T(8,128)(2,1)S(1)}, bf16[240,512]{1,0:T(8,128)(2,1)S(1)}, u32[]{:S(2)}, u32[]{:S(2)}) collective-permute-start(bf16[240,512]{1,0:T(8,128)(2,1)S(1)} %collective-permute-done.refs_2_), channel_id=1, source_target_pairs={{0,1},{1,0},{2,3},{3,2},{4,5},{5,4},{6,7},{7,6},{8,9},{9,8},{10,11... | collective-permute-start | bytes 737288 | tf_op jit(solution)/shard_map/ppermute | solution.py:270
  21.0 2.2 %collective-permute-start.8 = (bf16[128,512]{1,0:T(8,128)(2,1)S(1)}, bf16[128,512]{1,0:T(8,128)(2,1)S(1)}, u32[]{:S(2)}, u32[]{:S(2)}) collective-permute-start(bf16[128,512]{1,0:T(8,128)(2,1)S(1)} %get-tuple-element.43), channel_id=1, source_target_pairs={{0,8},{8,0},{16,24},{24,16},{1,9},{9,1},{17,25},{25,17},{2,10},{10... | collective-permute-start | bytes 393224 | tf_op jit(solution)/shard_map/ppermute | solution.py:270
  21.1 1.5 %collective-permute-start.9 = (bf16[112,512]{1,0:T(8,128)(2,1)S(1)}, bf16[112,512]{1,0:T(8,128)(2,1)S(1)}, u32[]{:S(2)}, u32[]{:S(2)}) collective-permute-start(bf16[112,512]{1,0:T(8,128)(2,1)S(1)} %get-tuple-element.44), channel_id=1, source_target_pairs={{0,8},{8,0},{16,24},{24,16},{1,9},{9,1},{17,25},{25,17},{2,10},{10... | collective-permute-start | bytes 344072 | tf_op jit(solution)/shard_map/ppermute | solution.py:270
  21.7 1.3 %collective-permute-start.11 = (bf16[112,512]{1,0:T(8,128)(2,1)S(1)}, bf16[112,512]{1,0:T(8,128)(2,1)S(1)}, u32[]{:S(2)}, u32[]{:S(2)}) collective-permute-start(bf16[112,512]{1,0:T(8,128)(2,1)S(1)} %get-tuple-element.46), channel_id=1, source_target_pairs={{0,8},{8,0},{16,24},{24,16},{1,9},{9,1},{17,25},{25,17},{2,10},{10... | collective-permute-start | bytes 344072 | tf_op jit(solution)/shard_map/ppermute | solution.py:270
  21.8 1.8 %collective-permute-start.10 = (bf16[128,512]{1,0:T(8,128)(2,1)S(1)}, bf16[128,512]{1,0:T(8,128)(2,1)S(1)}, u32[]{:S(2)}, u32[]{:S(2)}) collective-permute-start(bf16[128,512]{1,0:T(8,128)(2,1)S(1)} %get-tuple-element.45), channel_id=1, source_target_pairs={{0,8},{8,0},{16,24},{24,16},{1,9},{9,1},{17,25},{25,17},{2,10},{10... | collective-permute-start | bytes 393224 | tf_op jit(solution)/shard_map/ppermute | solution.py:270
  22.7 2.1 %collective-permute-start.12 = (bf16[64,512]{1,0:T(8,128)(2,1)S(1)}, bf16[64,512]{1,0:T(8,128)(2,1)S(1)}, u32[]{:S(2)}, u32[]{:S(2)}) collective-permute-start(bf16[64,512]{1,0:T(8,128)(2,1)S(1)} %get-tuple-element.47), channel_id=1, source_target_pairs={{0,8},{8,0},{16,24},{24,16},{1,9},{9,1},{17,25},{25,17},{2,10},{10... | collective-permute-start | bytes 196616 | tf_op jit(solution)/shard_map/ppermute | solution.py:270
  23.0 1.8 %collective-permute-start.13 = (bf16[64,512]{1,0:T(8,128)(2,1)S(1)}, bf16[64,512]{1,0:T(8,128)(2,1)S(1)}, u32[]{:S(2)}, u32[]{:S(2)}) collective-permute-start(bf16[64,512]{1,0:T(8,128)(2,1)S(1)} %get-tuple-element.48), channel_id=1, source_target_pairs={{0,8},{8,0},{16,24},{24,16},{1,9},{9,1},{17,25},{25,17},{2,10},{10... | collective-permute-start | bytes 196616 | tf_op jit(solution)/shard_map/ppermute | solution.py:270
  23.2 1.6 %collective-permute-start.14 = (bf16[64,512]{1,0:T(8,128)(2,1)S(1)}, bf16[64,512]{1,0:T(8,128)(2,1)S(1)}, u32[]{:S(2)}, u32[]{:S(2)}) collective-permute-start(bf16[64,512]{1,0:T(8,128)(2,1)S(1)} %get-tuple-element.49), channel_id=1, source_target_pairs={{0,8},{8,0},{16,24},{24,16},{1,9},{9,1},{17,25},{25,17},{2,10},{10... | collective-permute-start | bytes 196616 | tf_op jit(solution)/shard_map/ppermute | solution.py:270
  23.5 1.2 %collective-permute-start.15 = (bf16[48,512]{1,0:T(8,128)(2,1)S(1)}, bf16[48,512]{1,0:T(8,128)(2,1)S(1)}, u32[]{:S(2)}, u32[]{:S(2)}) collective-permute-start(bf16[48,512]{1,0:T(8,128)(2,1)S(1)} %get-tuple-element.50), channel_id=1, source_target_pairs={{0,8},{8,0},{16,24},{24,16},{1,9},{9,1},{17,25},{25,17},{2,10},{10... | collective-permute-start | bytes 147464 | tf_op jit(solution)/shard_map/ppermute | solution.py:270

commit v3 on v2

--- a/solution.py
+++ b/solution.py
@@ -319,10 +319,9 @@
         bit //= 2
     cut = [2, 2, 2, 4]
     cut = [split_block(block, count) for block, count in zip(columns, cut + [2] * len(columns))]
-    mirror, cut[0] = lax.optimization_barrier((mirror, cut[0]))
     swapped = [flip(part, "grp", 1) for part in cut[0]]
     swapped, cut[-1] = lax.optimization_barrier((swapped, cut[-1]))
-    across, cut[-2] = lax.optimization_barrier((across, cut[-2]))
+    mirror, across, cut[-2] = lax.optimization_barrier((mirror, across, cut[-2]))
     ends = [
         (part, (mask, pair, sum(other.shape[0] for other in parts[:n])))
         for parts, (mask, pair, _) in zip(cut, labels)

time: 42.8 us -> 42.8 us (level)
  waiting for transfers between devices: 8.19 us -> 7.01 us
  blocking collectives: 13.6 us -> 14.4 us
    ppermute x16, waiting for transfers between devices: 8.19 us -> 7.01 us  [flip(): lax.ppermute(value, axis, [(i, i ^ mask) for i in range(lax.axis_size(axi...]
    all_to_all x1, blocking collectives: 13.6 us -> 14.4 us  [on_device(): lax.all_to_all(results, 'dev', split_axis=0, concat_axis=0, tiled=True)]
where the time goes in v3:
time: 42.8 us; the launch traced here: 42.7 us
  starting transfers between devices  14.7 us (34%)
  blocking collectives  14.4 us (34%)
  waiting for transfers between devices  7.01 us (16%)
  Pallas kernels  5.87 us (14%)
  between operations  0.7 us (2%)
    ppermute x16, starting transfers between devices, flip(): lax.ppermute(value, axis, [(i, i ^ mask) for i in range(lax.axis_size(axi...  14.7 us
    all_to_all x1, blocking collectives, on_device(): lax.all_to_all(results, 'dev', split_axis=0, concat_axis=0, tiled=True)  14.4 us
    ppermute x16, waiting for transfers between devices, flip(): lax.ppermute(value, axis, [(i, i ^ mask) for i in range(lax.axis_size(axi...  7.01 us
    pallas_call x1, Pallas kernels, first_step(): pl.pallas_call(functools.partial(first_kernel, len(pieces), labels, per,...  2.4 us
    pallas_call x1, Pallas kernels, embed_tiles(): pl.pallas_call(embed_kernel, out_shape=jax.ShapeDtypeStruct((slides * USE...  1.73 us
    pallas_call x1, Pallas kernels, finish_step(): pl.pallas_call(functools.partial(finish_kernel, size, groups, len(pieces)...  0.97 us
  transfers between devices with their start and end apart: 16, of which 5 were waited for; matrix products, arithmetic and copies ran while one was open for 0% of the time, Pallas kernels for 6%

profile of v3, /device:TPU:0, one launch (start us, length us, event | category | flops | bytes accessed | tf_op | source)
XLA Modules:
  0.0 42.7 jit_solution(1562396102958856881)
XLA Ops:
  0.6 1.7 %embed.1.in_ref.refs_0_.refs_3_ = bf16[240,512]{1,0:T(8,128)(2,1)S(1)} custom-call(bf16[2,128,768]{2,1,0:T(8,128)(2,1)} %features_in.1, s32[2]{0:T(128)} %counts_in.1, bf16[768,512]{1,0:T(8,128)(2,1)} %projection_in.1), custom_call_target="tpu_custom_call" | custom-call | tf_op jit(solution)/shard_map/embed/pallas_call | solution.py:52
  2.4 3.1 %collective-permute-start.4 = (bf16[240,512]{1,0:T(8,128)(2,1)S(1)}, bf16[240,512]{1,0:T(8,128)(2,1)S(1)}, u32[]{:S(2)}, u32[]{:S(2)}) collective-permute-start(bf16[240,512]{1,0:T(8,128)(2,1)S(1)} %embed.1.in_ref.refs_0_.refs_3_), channel_id=1, source_target_pairs={{0,2},{1,3},{2,0},{3,1},{4,6},{5,7},{6,4},{7,5},{8,10},{9,11},{10,... | collective-permute-start | bytes 737288 | tf_op jit(solution)/shard_map/ppermute | solution.py:270
  5.5 1.5 %collective-permute-start.2 = (bf16[240,512]{1,0:T(8,128)(2,1)S(1)}, bf16[240,512]{1,0:T(8,128)(2,1)S(1)}, u32[]{:S(2)}, u32[]{:S(2)}) collective-permute-start(bf16[240,512]{1,0:T(8,128)(2,1)S(1)} %embed.1.in_ref.refs_0_.refs_3_), channel_id=1, source_target_pairs={{0,16},{8,24},{16,0},{24,8},{1,17},{9,25},{17,1},{25,9},{2,18},{10... | collective-permute-start | bytes 737288 | tf_op jit(solution)/shard_map/ppermute | solution.py:270
  7.0 1.5 %collective-permute-start.1 = (bf16[240,512]{1,0:T(8,128)(2,1)S(1)}, bf16[240,512]{1,0:T(8,128)(2,1)S(1)}, u32[]{:S(2)}, u32[]{:S(2)}) collective-permute-start(bf16[240,512]{1,0:T(8,128)(2,1)S(1)} %embed.1.in_ref.refs_0_.refs_3_), channel_id=1, source_target_pairs={{0,1},{1,0},{2,3},{3,2},{4,5},{5,4},{6,7},{7,6},{8,9},{9,8},{10,11... | collective-permute-start | bytes 737288 | tf_op jit(solution)/shard_map/ppermute | solution.py:270
  8.5 2.5 %collective-permute-start = (bf16[240,512]{1,0:T(8,128)(2,1)S(1)}, bf16[240,512]{1,0:T(8,128)(2,1)S(1)}, u32[]{:S(2)}, u32[]{:S(2)}) collective-permute-start(bf16[240,512]{1,0:T(8,128)(2,1)S(1)} %embed.1.in_ref.refs_0_.refs_3_), channel_id=1, source_target_pairs={{0,6},{1,7},{2,4},{3,5},{4,2},{5,3},{6,0},{7,1},{8,14},{9,15},{10,... | collective-permute-start | bytes 737288 | tf_op jit(solution)/shard_map/ppermute | solution.py:270
  10.9 0.5 %collective-permute-done.4.in_ref.refs_4_ = bf16[240,512]{1,0:T(8,128)(2,1)S(1)} collective-permute-done((bf16[240,512]{1,0:T(8,128)(2,1)S(1)}, bf16[240,512]{1,0:T(8,128)(2,1)S(1)}, u32[]{:S(2)}, u32[]{:S(2)}) %collective-permute-start.4) | collective-permute-done | bytes 245792 | tf_op jit(solution)/shard_map/ppermute | solution.py:270
  11.4 1.9 %collective-permute-start.5 = (bf16[240,512]{1,0:T(8,128)(2,1)S(1)}, bf16[240,512]{1,0:T(8,128)(2,1)S(1)}, u32[]{:S(2)}, u32[]{:S(2)}) collective-permute-start(bf16[240,512]{1,0:T(8,128)(2,1)S(1)} %collective-permute-done.4.in_ref.refs_4_), channel_id=1, source_target_pairs={{0,16},{8,24},{16,0},{24,8},{1,17},{9,25},{17,1},{25,9},{2,18},{10... | collective-permute-start | bytes 737288 | tf_op jit(solution)/shard_map/ppermute | solution.py:270
  13.4 0.1 collective-permute-start.6
  13.4 0.0 collective-permute-done.2.in_ref.refs_5_
  13.5 0.5 %collective-permute-start.7 = (bf16[112,512]{1,0:T(8,128)(2,1)S(1)}, bf16[112,512]{1,0:T(8,128)(2,1)S(1)}, u32[]{:S(2)}, u32[]{:S(2)}) collective-permute-start(bf16[112,512]{1,0:T(8,128)(2,1)S(1)} %get-tuple-element.32), channel_id=1, source_target_pairs={{0,8},{8,0},{16,24},{24,16},{1,9},{9,1},{17,25},{25,17},{2,10},{10... | collective-permute-start | bytes 344072 | tf_op jit(solution)/shard_map/ppermute | solution.py:270
  14.0 0.1 collective-permute-done.1.refs_1_
  14.1 4.9 %collective-permute-done.refs_2_ = bf16[240,512]{1,0:T(8,128)(2,1)S(1)} collective-permute-done((bf16[240,512]{1,0:T(8,128)(2,1)S(1)}, bf16[240,512]{1,0:T(8,128)(2,1)S(1)}, u32[]{:S(2)}, u32[]{:S(2)}) %collective-permute-start) | collective-permute-done | bytes 245792 | tf_op jit(solution)/shard_map/ppermute | solution.py:270
  19.0 1.5 %collective-permute-start.3 = (bf16[240,512]{1,0:T(8,128)(2,1)S(1)}, bf16[240,512]{1,0:T(8,128)(2,1)S(1)}, u32[]{:S(2)}, u32[]{:S(2)}) collective-permute-start(bf16[240,512]{1,0:T(8,128)(2,1)S(1)} %collective-permute-done.refs_2_), channel_id=1, source_target_pairs={{0,1},{1,0},{2,3},{3,2},{4,5},{5,4},{6,7},{7,6},{8,9},{9,8},{10,11... | collective-permute-start | bytes 737288 | tf_op jit(solution)/shard_map/ppermute | solution.py:270
  20.5 0.1 collective-permute-start.8
  20.6 0.5 %collective-permute-start.9 = (bf16[112,512]{1,0:T(8,128)(2,1)S(1)}, bf16[112,512]{1,0:T(8,128)(2,1)S(1)}, u32[]{:S(2)}, u32[]{:S(2)}) collective-permute-start(bf16[112,512]{1,0:T(8,128)(2,1)S(1)} %get-tuple-element.40), channel_id=1, source_target_pairs={{0,8},{8,0},{16,24},{24,16},{1,9},{9,1},{17,25},{25,17},{2,10},{10... | collective-permute-start | bytes 344072 | tf_op jit(solution)/shard_map/ppermute | solution.py:270
  21.1 0.0 collective-permute-done.6.refs_7_
  21.1 0.1 collective-permute-start.11
  21.2 0.4 collective-permute-start.10
  21.6 0.5 %collective-permute-done.9.refs_10_ = bf16[112,512]{1,0:T(8,128)(2,1)S(1)} collective-permute-done((bf16[112,512]{1,0:T(8,128)(2,1)S(1)}, bf16[112,512]{1,0:T(8,128)(2,1)S(1)}, u32[]{:S(2)}, u32[]{:S(2)}) %collective-permute-start.9) | collective-permute-done | bytes 114720 | tf_op jit(solution)/shard_map/ppermute | solution.py:270
  22.1 0.3 collective-permute-start.12
  22.4 0.0 collective-permute-done.11.refs_12_
  22.4 0.2 collective-permute-start.13
  22.6 0.3 collective-permute-start.14
  22.9 0.0 collective-permute-done.10.refs_11_
  22.9 0.2 collective-permute-start.15
  23.1 1.0 %collective-permute-done.15.refs_16_ = bf16[48,512]{1,0:T(8,128)(2,1)S(1)} collective-permute-done((bf16[48,512]{1,0:T(8,128)(2,1)S(1)}, bf16[48,512]{1,0:T(8,128)(2,1)S(1)}, u32[]{:S(2)}, u32[]{:S(2)}) %collective-permute-start.15) | collective-permute-done | bytes 49184 | tf_op jit(solution)/shard_map/ppermute | solution.py:270
  24.2 0.0 collective-permute-done.13.refs_14_
  24.2 0.0 collective-permute-done.14.refs_15_
  24.2 2.4 %first_scores.1 = (bf16[8,16,16,512]{3,2,1,0:T(8,128)(2,1)S(1)}, f32[8,256]{1,0:T(8,128)S(1)}, f32[6,16,128]{2,1,0:T(8,128)S(1)}) custom-call(bf16[240,512]{1,0:T(8,128)(2,1)S(1)} %embed.1.in_ref.refs_0_.refs_3_, bf16[240,512]{1,0:T(8,128)(2,1)S(1)} %collective-permute-done.1.refs_1_, bf16[240,512]{1,0:T(8,128)(2,1)S(1)} %collective-permute-done.refs_2_, ...), custom_call_target="tpu_custom_call" | custom-call | tf_op jit(solution)/shard_map/first_scores/pallas_call | solution.py:165
  26.6 1.0 %finish.1 = f32[8,8,4,128]{3,2,1,0:T(4,128)S(1)} custom-call(bf16[240,512]{1,0:T(8,128)(2,1)S(1)} %collective-permute-done.3.refs_0_, bf16[8,16,16,512]{3,2,1,0:T(8,128)(2,1)S(1)} %get-tuple-element.47.refs_1_, f32[8,256]{1,0:T(8,128)S(1)} %get-tuple-element.48.refs_2_, f32[6,16,128]{2,1,0:T(8,128)S(1)} %get-tuple-element.49.refs_3_), custom_call_target="tpu_custom_call" | custom-call | tf_op jit(solution)/shard_map/finish/pallas_call | solution.py:223
  27.5 14.4 %all_to_all.5.parts = f32[8,8,4,128]{3,2,1,0:T(4,128)S(1)} all-to-all(f32[8,8,4,128]{3,2,1,0:T(4,128)S(1)} %finish.1), channel_id=1, replica_groups=mesh['grp'=4,'dev'=8] {'dev'}, dimensions={0} | all-to-all | bytes 262144 | tf_op jit(solution)/shard_map/all_to_all | solution.py:342
  42.0 0.7 %gather_results.1 = (f32[16,8,128]{2,1,0:T(8,128)}, f32[8,16]{1,0:T(8,128)}) custom-call(f32[8,8,4,128]{3,2,1,0:T(4,128)S(1)} %all_to_all.5.parts), custom_call_target="tpu_custom_call" | custom-call | tf_op jit(solution)/shard_map/gather_results/pallas_call | solution.py:256
  (9 shorter events, 0.1 us)
Async XLA Ops:
  2.4 9.0 %collective-permute-start.4 = (bf16[240,512]{1,0:T(8,128)(2,1)S(1)}, bf16[240,512]{1,0:T(8,128)(2,1)S(1)}, u32[]{:S(2)}, u32[]{:S(2)}) collective-permute-start(bf16[240,512]{1,0:T(8,128)(2,1)S(1)} %embed.1.in_ref.refs_0_.refs_3_), channel_id=1, source_target_pairs={{0,2},{1,3},{2,0},{3,1},{4,6},{5,7},{6,4},{7,5},{8,10},{9,11},{10,... | collective-permute-start | bytes 737288 | tf_op jit(solution)/shard_map/ppermute | solution.py:270
  5.5 8.0 %collective-permute-start.2 = (bf16[240,512]{1,0:T(8,128)(2,1)S(1)}, bf16[240,512]{1,0:T(8,128)(2,1)S(1)}, u32[]{:S(2)}, u32[]{:S(2)}) collective-permute-start(bf16[240,512]{1,0:T(8,128)(2,1)S(1)} %embed.1.in_ref.refs_0_.refs_3_), channel_id=1, source_target_pairs={{0,16},{8,24},{16,0},{24,8},{1,17},{9,25},{17,1},{25,9},{2,18},{10... | collective-permute-start | bytes 737288 | tf_op jit(solution)/shard_map/ppermute | solution.py:270
  7.0 7.1 %collective-permute-start.1 = (bf16[240,512]{1,0:T(8,128)(2,1)S(1)}, bf16[240,512]{1,0:T(8,128)(2,1)S(1)}, u32[]{:S(2)}, u32[]{:S(2)}) collective-permute-start(bf16[240,512]{1,0:T(8,128)(2,1)S(1)} %embed.1.in_ref.refs_0_.refs_3_), channel_id=1, source_target_pairs={{0,1},{1,0},{2,3},{3,2},{4,5},{5,4},{6,7},{7,6},{8,9},{9,8},{10,11... | collective-permute-start | bytes 737288 | tf_op jit(solution)/shard_map/ppermute | solution.py:270
  8.5 10.5 %collective-permute-start = (bf16[240,512]{1,0:T(8,128)(2,1)S(1)}, bf16[240,512]{1,0:T(8,128)(2,1)S(1)}, u32[]{:S(2)}, u32[]{:S(2)}) collective-permute-start(bf16[240,512]{1,0:T(8,128)(2,1)S(1)} %embed.1.in_ref.refs_0_.refs_3_), channel_id=1, source_target_pairs={{0,6},{1,7},{2,4},{3,5},{4,2},{5,3},{6,0},{7,1},{8,14},{9,15},{10,... | collective-permute-start | bytes 737288 | tf_op jit(solution)/shard_map/ppermute | solution.py:270
  11.4 9.7 %collective-permute-start.5 = (bf16[240,512]{1,0:T(8,128)(2,1)S(1)}, bf16[240,512]{1,0:T(8,128)(2,1)S(1)}, u32[]{:S(2)}, u32[]{:S(2)}) collective-permute-start(bf16[240,512]{1,0:T(8,128)(2,1)S(1)} %collective-permute-done.4.in_ref.refs_4_), channel_id=1, source_target_pairs={{0,16},{8,24},{16,0},{24,8},{1,17},{9,25},{17,1},{25,9},{2,18},{10... | collective-permute-start | bytes 737288 | tf_op jit(solution)/shard_map/ppermute | solution.py:270
  13.4 7.7 %collective-permute-start.6 = (bf16[128,512]{1,0:T(8,128)(2,1)S(1)}, bf16[128,512]{1,0:T(8,128)(2,1)S(1)}, u32[]{:S(2)}, u32[]{:S(2)}) collective-permute-start(bf16[128,512]{1,0:T(8,128)(2,1)S(1)} %get-tuple-element.31), channel_id=1, source_target_pairs={{0,8},{8,0},{16,24},{24,16},{1,9},{9,1},{17,25},{25,17},{2,10},{10... | collective-permute-start | bytes 393224 | tf_op jit(solution)/shard_map/ppermute | solution.py:270
  13.5 7.1 %collective-permute-start.7 = (bf16[112,512]{1,0:T(8,128)(2,1)S(1)}, bf16[112,512]{1,0:T(8,128)(2,1)S(1)}, u32[]{:S(2)}, u32[]{:S(2)}) collective-permute-start(bf16[112,512]{1,0:T(8,128)(2,1)S(1)} %get-tuple-element.32), channel_id=1, source_target_pairs={{0,8},{8,0},{16,24},{24,16},{1,9},{9,1},{17,25},{25,17},{2,10},{10... | collective-permute-start | bytes 344072 | tf_op jit(solution)/shard_map/ppermute | solution.py:270
  19.0 7.6 %collective-permute-start.3 = (bf16[240,512]{1,0:T(8,128)(2,1)S(1)}, bf16[240,512]{1,0:T(8,128)(2,1)S(1)}, u32[]{:S(2)}, u32[]{:S(2)}) collective-permute-start(bf16[240,512]{1,0:T(8,128)(2,1)S(1)} %collective-permute-done.refs_2_), channel_id=1, source_target_pairs={{0,1},{1,0},{2,3},{3,2},{4,5},{5,4},{6,7},{7,6},{8,9},{9,8},{10,11... | collective-permute-start | bytes 737288 | tf_op jit(solution)/shard_map/ppermute | solution.py:270
  20.5 2.1 %collective-permute-start.8 = (bf16[128,512]{1,0:T(8,128)(2,1)S(1)}, bf16[128,512]{1,0:T(8,128)(2,1)S(1)}, u32[]{:S(2)}, u32[]{:S(2)}) collective-permute-start(bf16[128,512]{1,0:T(8,128)(2,1)S(1)} %get-tuple-element.39), channel_id=1, source_target_pairs={{0,8},{8,0},{16,24},{24,16},{1,9},{9,1},{17,25},{25,17},{2,10},{10... | collective-permute-start | bytes 393224 | tf_op jit(solution)/shard_map/ppermute | solution.py:270
  20.6 1.5 %collective-permute-start.9 = (bf16[112,512]{1,0:T(8,128)(2,1)S(1)}, bf16[112,512]{1,0:T(8,128)(2,1)S(1)}, u32[]{:S(2)}, u32[]{:S(2)}) collective-permute-start(bf16[112,512]{1,0:T(8,128)(2,1)S(1)} %get-tuple-element.40), channel_id=1, source_target_pairs={{0,8},{8,0},{16,24},{24,16},{1,9},{9,1},{17,25},{25,17},{2,10},{10... | collective-permute-start | bytes 344072 | tf_op jit(solution)/shard_map/ppermute | solution.py:270
  21.1 1.3 %collective-permute-start.11 = (bf16[112,512]{1,0:T(8,128)(2,1)S(1)}, bf16[112,512]{1,0:T(8,128)(2,1)S(1)}, u32[]{:S(2)}, u32[]{:S(2)}) collective-permute-start(bf16[112,512]{1,0:T(8,128)(2,1)S(1)} %get-tuple-element.42), channel_id=1, source_target_pairs={{0,8},{8,0},{16,24},{24,16},{1,9},{9,1},{17,25},{25,17},{2,10},{10... | collective-permute-start | bytes 344072 | tf_op jit(solution)/shard_map/ppermute | solution.py:270
  21.2 1.8 %collective-permute-start.10 = (bf16[128,512]{1,0:T(8,128)(2,1)S(1)}, bf16[128,512]{1,0:T(8,128)(2,1)S(1)}, u32[]{:S(2)}, u32[]{:S(2)}) collective-permute-start(bf16[128,512]{1,0:T(8,128)(2,1)S(1)} %get-tuple-element.41), channel_id=1, source_target_pairs={{0,8},{8,0},{16,24},{24,16},{1,9},{9,1},{17,25},{25,17},{2,10},{10... | collective-permute-start | bytes 393224 | tf_op jit(solution)/shard_map/ppermute | solution.py:270
  22.1 2.1 %collective-permute-start.12 = (bf16[64,512]{1,0:T(8,128)(2,1)S(1)}, bf16[64,512]{1,0:T(8,128)(2,1)S(1)}, u32[]{:S(2)}, u32[]{:S(2)}) collective-permute-start(bf16[64,512]{1,0:T(8,128)(2,1)S(1)} %get-tuple-element.43), channel_id=1, source_target_pairs={{0,8},{8,0},{16,24},{24,16},{1,9},{9,1},{17,25},{25,17},{2,10},{10... | collective-permute-start | bytes 196616 | tf_op jit(solution)/shard_map/ppermute | solution.py:270
  22.4 1.8 %collective-permute-start.13 = (bf16[64,512]{1,0:T(8,128)(2,1)S(1)}, bf16[64,512]{1,0:T(8,128)(2,1)S(1)}, u32[]{:S(2)}, u32[]{:S(2)}) collective-permute-start(bf16[64,512]{1,0:T(8,128)(2,1)S(1)} %get-tuple-element.44), channel_id=1, source_target_pairs={{0,8},{8,0},{16,24},{24,16},{1,9},{9,1},{17,25},{25,17},{2,10},{10... | collective-permute-start | bytes 196616 | tf_op jit(solution)/shard_map/ppermute | solution.py:270
  22.6 1.6 %collective-permute-start.14 = (bf16[64,512]{1,0:T(8,128)(2,1)S(1)}, bf16[64,512]{1,0:T(8,128)(2,1)S(1)}, u32[]{:S(2)}, u32[]{:S(2)}) collective-permute-start(bf16[64,512]{1,0:T(8,128)(2,1)S(1)} %get-tuple-element.45), channel_id=1, source_target_pairs={{0,8},{8,0},{16,24},{24,16},{1,9},{9,1},{17,25},{25,17},{2,10},{10... | collective-permute-start | bytes 196616 | tf_op jit(solution)/shard_map/ppermute | solution.py:270
  22.9 1.2 %collective-permute-start.15 = (bf16[48,512]{1,0:T(8,128)(2,1)S(1)}, bf16[48,512]{1,0:T(8,128)(2,1)S(1)}, u32[]{:S(2)}, u32[]{:S(2)}) collective-permute-start(bf16[48,512]{1,0:T(8,128)(2,1)S(1)} %get-tuple-element.46), channel_id=1, source_target_pairs={{0,8},{8,0},{16,24},{24,16},{1,9},{9,1},{17,25},{25,17},{2,10},{10... | collective-permute-start | bytes 147464 | tf_op jit(solution)/shard_map/ppermute | solution.py:270

commit v4 on v3

--- a/solution.py
+++ b/solution.py
@@ -310,18 +310,25 @@
     slots = features.shape[1]
     whole = embed_tiles(features, tile_counts, projection)
     per = features.shape[0]
-    mirror, across, beside = flip(whole, "dev", 6), flip(whole, "dev", 1), flip(whole, "dev", 2)
+    across, beside = flip(whole, "dev", 1), flip(whole, "dev", 2)
+    inner = [d for d in range(size) if (d >> 1 ^ d >> 2) & 1]
+    outer = [d for d in range(size) if d not in inner]
+    here = lax.axis_index("dev")
+    within = (here >> 1 ^ here >> 2) & 1 == 1
+    middle = lax.ppermute(whole, "dev", [(d, d ^ 6) for d in inner])
+    beside, later = lax.optimization_barrier((beside, whole))
+    edge = lax.ppermute(later, "dev", [(d, d ^ 6) for d in outer])
     labels, columns = [(0, 0, 0), (0, 1, 0)], [whole, beside]
     bit = groups // 2
     while bit > 1:
         columns += [flip(block, "grp", bit) for block in columns]
         labels += [(mask ^ bit, pair, 0) for mask, pair, _ in labels]
         bit //= 2
-    cut = [2, 2, 2, 4]
+    cut = [2, 2, 1, 4]
     cut = [split_block(block, count) for block, count in zip(columns, cut + [2] * len(columns))]
     swapped = [flip(part, "grp", 1) for part in cut[0]]
     swapped, cut[-1] = lax.optimization_barrier((swapped, cut[-1]))
-    mirror, across, cut[-2] = lax.optimization_barrier((mirror, across, cut[-2]))
+    middle, across, cut[-2] = lax.optimization_barrier((middle, across, cut[-2]))
     ends = [
         (part, (mask, pair, sum(other.shape[0] for other in parts[:n])))
         for parts, (mask, pair, _) in zip(cut, labels)
@@ -329,6 +336,7 @@
     ]
     columns += swapped + [flip(part, "grp", 1) for part, _ in ends[len(swapped) :]]
     labels += [(mask ^ 1, pair, offset) for _, (mask, pair, offset) in ends]
+    mirror = jnp.where(within, middle, edge)
     rows = [(whole, 0), (across, 1), (mirror, 6), (flip(mirror, "dev", 1), 7)]
     bit = 8
     while bit < size:

time: 42.8 us -> 43.7 us (1.021)
  blocking collectives: 14.4 us -> 10.7 us
  starting transfers between devices: 14.7 us -> 17.7 us
  waiting for transfers between devices: 7.01 us -> 8.44 us
    ppermute x0 -> x2, starting transfers between devices: none -> 6.33 us  [the longest x1 5.67 us: on_device(): edge = lax.ppermute(later, 'dev', [(d, d ^ 6) for d in outer])]
    all_to_all x1, blocking collectives: 14.4 us -> 10.7 us  [on_device(): lax.all_to_all(results, 'dev', split_axis=0, concat_axis=0, tiled=True)]
    ppermute x16 -> x14, starting transfers between devices: 14.7 us -> 11.3 us  [flip(): lax.ppermute(value, axis, [(i, i ^ mask) for i in range(lax.axis_size(axi...]
    ppermute x0 -> x2, waiting for transfers between devices: none -> 3.19 us  [the longest x1 3.18 us: on_device(): edge = lax.ppermute(later, 'dev', [(d, d ^ 6) for d in outer])]
    ppermute x16 -> x14, waiting for transfers between devices: 7.01 us -> 5.25 us  [flip(): lax.ppermute(value, axis, [(i, i ^ mask) for i in range(lax.axis_size(axi...]
where the time goes in v4:
time: 43.7 us; the launch traced here: 43.5 us
  starting transfers between devices  17.7 us (41%)
  blocking collectives  10.7 us (24%)
  waiting for transfers between devices  8.44 us (19%)
  Pallas kernels  5.87 us (13%)
  between operations  0.75 us (2%)
    ppermute x14, starting transfers between devices, flip(): lax.ppermute(value, axis, [(i, i ^ mask) for i in range(lax.axis_size(axi...  11.3 us
    all_to_all x1, blocking collectives, on_device(): lax.all_to_all(results, 'dev', split_axis=0, concat_axis=0, tiled=True)  10.7 us
    ppermute x1, starting transfers between devices, on_device(): edge = lax.ppermute(later, 'dev', [(d, d ^ 6) for d in outer])  5.67 us
    ppermute x14, waiting for transfers between devices, flip(): lax.ppermute(value, axis, [(i, i ^ mask) for i in range(lax.axis_size(axi...  5.25 us
    ppermute x1, waiting for transfers between devices, on_device(): edge = lax.ppermute(later, 'dev', [(d, d ^ 6) for d in outer])  3.18 us
    pallas_call x1, Pallas kernels, first_step(): pl.pallas_call(functools.partial(first_kernel, len(pieces), labels, per,...  2.4 us
    pallas_call x1, Pallas kernels, embed_tiles(): pl.pallas_call(embed_kernel, out_shape=jax.ShapeDtypeStruct((slides * USE...  1.73 us
    pallas_call x1, Pallas kernels, finish_step(): pl.pallas_call(functools.partial(finish_kernel, size, groups, len(pieces)...  0.96 us
  transfers between devices with their start and end apart: 16, of which 5 were waited for; matrix products, arithmetic and copies ran while one was open for 0% of the time, Pallas kernels for 6%

profile of v4, /device:TPU:0, one launch (start us, length us, event | category | flops | bytes accessed | tf_op | source)
XLA Modules:
  0.0 43.5 jit_solution(11236148470205790360)
XLA Ops:
  0.6 1.7 %embed.1.in_ref.refs_0_.refs_3_ = bf16[240,512]{1,0:T(8,128)(2,1)S(1)} custom-call(bf16[2,128,768]{2,1,0:T(8,128)(2,1)} %features_in.1, s32[2]{0:T(128)} %counts_in.1, bf16[768,512]{1,0:T(8,128)(2,1)} %projection_in.1), custom_call_target="tpu_custom_call" | custom-call | tf_op jit(solution)/shard_map/embed/pallas_call | solution.py:52
  2.4 3.1 %collective-permute-start.3 = (bf16[240,512]{1,0:T(8,128)(2,1)S(1)}, bf16[240,512]{1,0:T(8,128)(2,1)S(1)}, u32[]{:S(2)}, u32[]{:S(2)}) collective-permute-start(bf16[240,512]{1,0:T(8,128)(2,1)S(1)} %embed.1.in_ref.refs_0_.refs_3_), channel_id=1, source_target_pairs={{0,2},{1,3},{2,0},{3,1},{4,6},{5,7},{6,4},{7,5},{8,10},{9,11},{10,... | collective-permute-start | bytes 737288 | tf_op jit(solution)/shard_map/ppermute | solution.py:270
  5.5 1.5 %collective-permute-start.2 = (bf16[240,512]{1,0:T(8,128)(2,1)S(1)}, bf16[240,512]{1,0:T(8,128)(2,1)S(1)}, u32[]{:S(2)}, u32[]{:S(2)}) collective-permute-start(bf16[240,512]{1,0:T(8,128)(2,1)S(1)} %embed.1.in_ref.refs_0_.refs_3_), channel_id=1, source_target_pairs={{0,16},{8,24},{16,0},{24,8},{1,17},{9,25},{17,1},{25,9},{2,18},{10... | collective-permute-start | bytes 737288 | tf_op jit(solution)/shard_map/ppermute | solution.py:270
  7.0 0.7 %collective-permute-start = (bf16[240,512]{1,0:T(8,128)(2,1)S(1)}, bf16[240,512]{1,0:T(8,128)(2,1)S(1)}, u32[]{:S(2)}, u32[]{:S(2)}) collective-permute-start(bf16[240,512]{1,0:T(8,128)(2,1)S(1)} %embed.1.in_ref.refs_0_.refs_3_), channel_id=1, source_target_pairs={{2,4},{3,5},{4,2},{5,3},{10,12},{11,13},{12,10},{13,11},{18,20},{1... | collective-permute-start | bytes 737288 | tf_op jit(solution)/shard_map/ppermute | solution.py:318
  7.7 1.6 %collective-permute-start.1 = (bf16[240,512]{1,0:T(8,128)(2,1)S(1)}, bf16[240,512]{1,0:T(8,128)(2,1)S(1)}, u32[]{:S(2)}, u32[]{:S(2)}) collective-permute-start(bf16[240,512]{1,0:T(8,128)(2,1)S(1)} %embed.1.in_ref.refs_0_.refs_3_), channel_id=1, source_target_pairs={{0,1},{1,0},{2,3},{3,2},{4,5},{5,4},{6,7},{7,6},{8,9},{9,8},{10,11... | collective-permute-start | bytes 737288 | tf_op jit(solution)/shard_map/ppermute | solution.py:270
  9.2 2.2 %collective-permute-done.3.in_ref.refs_4_ = bf16[240,512]{1,0:T(8,128)(2,1)S(1)} collective-permute-done((bf16[240,512]{1,0:T(8,128)(2,1)S(1)}, bf16[240,512]{1,0:T(8,128)(2,1)S(1)}, u32[]{:S(2)}, u32[]{:S(2)}) %collective-permute-start.3) | collective-permute-done | bytes 245792 | tf_op jit(solution)/shard_map/ppermute | solution.py:270
  11.4 5.7 %collective-permute-start.4 = (bf16[240,512]{1,0:T(8,128)(2,1)S(1)}, bf16[240,512]{1,0:T(8,128)(2,1)S(1)}, u32[]{:S(2)}, u32[]{:S(2)}) collective-permute-start(bf16[240,512]{1,0:T(8,128)(2,1)S(1)} %embed.1.in_ref.refs_0_.refs_3_), channel_id=1, source_target_pairs={{0,6},{1,7},{6,0},{7,1},{8,14},{9,15},{14,8},{15,9},{16,22},{17,23... | collective-permute-start | bytes 737288 | tf_op jit(solution)/shard_map/ppermute | solution.py:320
  17.1 0.1 collective-permute-start.8
  17.2 1.6 %collective-permute-start.6 = (bf16[240,512]{1,0:T(8,128)(2,1)S(1)}, bf16[240,512]{1,0:T(8,128)(2,1)S(1)}, u32[]{:S(2)}, u32[]{:S(2)}) collective-permute-start(bf16[240,512]{1,0:T(8,128)(2,1)S(1)} %collective-permute-done.3.in_ref.refs_4_), channel_id=1, source_target_pairs={{0,16},{8,24},{16,0},{24,8},{1,17},{9,25},{17,1},{25,9},{2,18},{10... | collective-permute-start | bytes 737288 | tf_op jit(solution)/shard_map/ppermute | solution.py:270
  18.8 0.0 collective-permute-done
  18.8 0.0 collective-permute-done.1.refs_1_
  18.8 0.2 collective-permute-start.11
  19.1 3.2 %collective-permute-done.4 = bf16[240,512]{1,0:T(8,128)(2,1)S(1)} collective-permute-done((bf16[240,512]{1,0:T(8,128)(2,1)S(1)}, bf16[240,512]{1,0:T(8,128)(2,1)S(1)}, u32[]{:S(2)}, u32[]{:S(2)}) %collective-permute-start.4) | collective-permute-done | bytes 245792 | tf_op jit(solution)/shard_map/ppermute | solution.py:320
  22.3 1.5 %collective-permute-start.5 = (bf16[240,512]{1,0:T(8,128)(2,1)S(1)}, bf16[240,512]{1,0:T(8,128)(2,1)S(1)}, u32[]{:S(2)}, u32[]{:S(2)}) collective-permute-start(bf16[240,512]{1,0:T(8,128)(2,1)S(1)} %broadcast_select_fusion.refs_2_), channel_id=1, source_target_pairs={{0,1},{1,0},{2,3},{3,2},{4,5},{5,4},{6,7},{7,6},{8,9},{9,8},{10,11... | collective-permute-start | bytes 737288 | tf_op jit(solution)/shard_map/ppermute | solution.py:270
  23.8 0.0 collective-permute-done.8.refs_8_
  23.8 0.6 %collective-permute-start.9 = (bf16[128,512]{1,0:T(8,128)(2,1)S(1)}, bf16[128,512]{1,0:T(8,128)(2,1)S(1)}, u32[]{:S(2)}, u32[]{:S(2)}) collective-permute-start(bf16[128,512]{1,0:T(8,128)(2,1)S(1)} %get-tuple-element.38), channel_id=1, source_target_pairs={{0,8},{8,0},{16,24},{24,16},{1,9},{9,1},{17,25},{25,17},{2,10},{10... | collective-permute-start | bytes 393224 | tf_op jit(solution)/shard_map/ppermute | solution.py:270
  24.3 1.2 %collective-permute-done.6.in_ref.refs_6_ = bf16[240,512]{1,0:T(8,128)(2,1)S(1)} collective-permute-done((bf16[240,512]{1,0:T(8,128)(2,1)S(1)}, bf16[240,512]{1,0:T(8,128)(2,1)S(1)}, u32[]{:S(2)}, u32[]{:S(2)}) %collective-permute-start.6) | collective-permute-done | bytes 245792 | tf_op jit(solution)/shard_map/ppermute | solution.py:270
  25.6 0.0 collective-permute-start.10
  25.6 0.0 collective-permute-done.7.refs_7_
  25.6 0.6 %collective-permute-start.12 = (bf16[64,512]{1,0:T(8,128)(2,1)S(1)}, bf16[64,512]{1,0:T(8,128)(2,1)S(1)}, u32[]{:S(2)}, u32[]{:S(2)}) collective-permute-start(bf16[64,512]{1,0:T(8,128)(2,1)S(1)} %get-tuple-element.41), channel_id=1, source_target_pairs={{0,8},{8,0},{16,24},{24,16},{1,9},{9,1},{17,25},{25,17},{2,10},{10... | collective-permute-start | bytes 196616 | tf_op jit(solution)/shard_map/ppermute | solution.py:270
  26.2 0.7 %collective-permute-done.10.refs_10_ = bf16[112,512]{1,0:T(8,128)(2,1)S(1)} collective-permute-done((bf16[112,512]{1,0:T(8,128)(2,1)S(1)}, bf16[112,512]{1,0:T(8,128)(2,1)S(1)}, u32[]{:S(2)}, u32[]{:S(2)}) %collective-permute-start.10) | collective-permute-done | bytes 114720 | tf_op jit(solution)/shard_map/ppermute | solution.py:270
  26.9 0.2 collective-permute-start.13
  27.1 0.4 collective-permute-start.14
  27.4 0.0 collective-permute-done.11.refs_11_
  27.4 0.2 collective-permute-start.15
  27.6 1.1 %collective-permute-done.15.refs_15_ = bf16[48,512]{1,0:T(8,128)(2,1)S(1)} collective-permute-done((bf16[48,512]{1,0:T(8,128)(2,1)S(1)}, bf16[48,512]{1,0:T(8,128)(2,1)S(1)}, u32[]{:S(2)}, u32[]{:S(2)}) %collective-permute-start.15) | collective-permute-done | bytes 49184 | tf_op jit(solution)/shard_map/ppermute | solution.py:270
  28.7 0.0 collective-permute-done.14.refs_14_
  28.7 2.4 %first_scores.1 = (bf16[8,16,16,512]{3,2,1,0:T(8,128)(2,1)S(1)}, f32[8,256]{1,0:T(8,128)S(1)}, f32[6,16,128]{2,1,0:T(8,128)S(1)}) custom-call(bf16[240,512]{1,0:T(8,128)(2,1)S(1)} %embed.1.in_ref.refs_0_.refs_3_, bf16[240,512]{1,0:T(8,128)(2,1)S(1)} %collective-permute-done.1.refs_1_, bf16[240,512]{1,0:T(8,128)(2,1)S(1)} %broadcast_select_fusion.refs_2_, ...), custom_call_target="tpu_custom_call" | custom-call | tf_op jit(solution)/shard_map/first_scores/pallas_call | solution.py:165
  31.1 0.0 collective-permute-done.5.refs_0_
  31.1 1.0 %finish.1 = f32[8,8,4,128]{3,2,1,0:T(4,128)S(1)} custom-call(bf16[240,512]{1,0:T(8,128)(2,1)S(1)} %collective-permute-done.5.refs_0_, bf16[8,16,16,512]{3,2,1,0:T(8,128)(2,1)S(1)} %get-tuple-element.45.refs_1_, f32[8,256]{1,0:T(8,128)S(1)} %get-tuple-element.46.refs_2_, f32[6,16,128]{2,1,0:T(8,128)S(1)} %get-tuple-element.47.refs_3_), custom_call_target="tpu_custom_call" | custom-call | tf_op jit(solution)/shard_map/finish/pallas_call | solution.py:223
  32.0 10.7 %all_to_all.5.parts = f32[8,8,4,128]{3,2,1,0:T(4,128)S(1)} all-to-all(f32[8,8,4,128]{3,2,1,0:T(4,128)S(1)} %finish.1), channel_id=1, replica_groups=mesh['grp'=4,'dev'=8] {'dev'}, dimensions={0} | all-to-all | bytes 262144 | tf_op jit(solution)/shard_map/all_to_all | solution.py:350
  42.8 0.7 %gather_results.1 = (f32[16,8,128]{2,1,0:T(8,128)}, f32[8,16]{1,0:T(8,128)}) custom-call(f32[8,8,4,128]{3,2,1,0:T(4,128)S(1)} %all_to_all.5.parts), custom_call_target="tpu_custom_call" | custom-call | tf_op jit(solution)/shard_map/gather_results/pallas_call | solution.py:256
  (10 shorter events, 0.1 us)
Async XLA Ops:
  2.4 9.0 %collective-permute-start.3 = (bf16[240,512]{1,0:T(8,128)(2,1)S(1)}, bf16[240,512]{1,0:T(8,128)(2,1)S(1)}, u32[]{:S(2)}, u32[]{:S(2)}) collective-permute-start(bf16[240,512]{1,0:T(8,128)(2,1)S(1)} %embed.1.in_ref.refs_0_.refs_3_), channel_id=1, source_target_pairs={{0,2},{1,3},{2,0},{3,1},{4,6},{5,7},{6,4},{7,5},{8,10},{9,11},{10,... | collective-permute-start | bytes 737288 | tf_op jit(solution)/shard_map/ppermute | solution.py:270
  5.5 11.7 %collective-permute-start.2 = (bf16[240,512]{1,0:T(8,128)(2,1)S(1)}, bf16[240,512]{1,0:T(8,128)(2,1)S(1)}, u32[]{:S(2)}, u32[]{:S(2)}) collective-permute-start(bf16[240,512]{1,0:T(8,128)(2,1)S(1)} %embed.1.in_ref.refs_0_.refs_3_), channel_id=1, source_target_pairs={{0,16},{8,24},{16,0},{24,8},{1,17},{9,25},{17,1},{25,9},{2,18},{10... | collective-permute-start | bytes 737288 | tf_op jit(solution)/shard_map/ppermute | solution.py:270
  7.0 11.8 %collective-permute-start = (bf16[240,512]{1,0:T(8,128)(2,1)S(1)}, bf16[240,512]{1,0:T(8,128)(2,1)S(1)}, u32[]{:S(2)}, u32[]{:S(2)}) collective-permute-start(bf16[240,512]{1,0:T(8,128)(2,1)S(1)} %embed.1.in_ref.refs_0_.refs_3_), channel_id=1, source_target_pairs={{2,4},{3,5},{4,2},{5,3},{10,12},{11,13},{12,10},{13,11},{18,20},{1... | collective-permute-start | bytes 737288 | tf_op jit(solution)/shard_map/ppermute | solution.py:318
  7.7 11.2 %collective-permute-start.1 = (bf16[240,512]{1,0:T(8,128)(2,1)S(1)}, bf16[240,512]{1,0:T(8,128)(2,1)S(1)}, u32[]{:S(2)}, u32[]{:S(2)}) collective-permute-start(bf16[240,512]{1,0:T(8,128)(2,1)S(1)} %embed.1.in_ref.refs_0_.refs_3_), channel_id=1, source_target_pairs={{0,1},{1,0},{2,3},{3,2},{4,5},{5,4},{6,7},{7,6},{8,9},{9,8},{10,11... | collective-permute-start | bytes 737288 | tf_op jit(solution)/shard_map/ppermute | solution.py:270
  11.4 10.8 %collective-permute-start.4 = (bf16[240,512]{1,0:T(8,128)(2,1)S(1)}, bf16[240,512]{1,0:T(8,128)(2,1)S(1)}, u32[]{:S(2)}, u32[]{:S(2)}) collective-permute-start(bf16[240,512]{1,0:T(8,128)(2,1)S(1)} %embed.1.in_ref.refs_0_.refs_3_), channel_id=1, source_target_pairs={{0,6},{1,7},{6,0},{7,1},{8,14},{9,15},{14,8},{15,9},{16,22},{17,23... | collective-permute-start | bytes 737288 | tf_op jit(solution)/shard_map/ppermute | solution.py:320
  17.1 6.6 %collective-permute-start.8 = (bf16[112,512]{1,0:T(8,128)(2,1)S(1)}, bf16[112,512]{1,0:T(8,128)(2,1)S(1)}, u32[]{:S(2)}, u32[]{:S(2)}) collective-permute-start(bf16[112,512]{1,0:T(8,128)(2,1)S(1)} %get-tuple-element.31), channel_id=1, source_target_pairs={{0,8},{8,0},{16,24},{24,16},{1,9},{9,1},{17,25},{25,17},{2,10},{10... | collective-permute-start | bytes 344072 | tf_op jit(solution)/shard_map/ppermute | solution.py:270
  17.2 8.4 %collective-permute-start.6 = (bf16[240,512]{1,0:T(8,128)(2,1)S(1)}, bf16[240,512]{1,0:T(8,128)(2,1)S(1)}, u32[]{:S(2)}, u32[]{:S(2)}) collective-permute-start(bf16[240,512]{1,0:T(8,128)(2,1)S(1)} %collective-permute-done.3.in_ref.refs_4_), channel_id=1, source_target_pairs={{0,16},{8,24},{16,0},{24,8},{1,17},{9,25},{17,1},{25,9},{2,18},{10... | collective-permute-start | bytes 737288 | tf_op jit(solution)/shard_map/ppermute | solution.py:270
  18.8 8.6 %collective-permute-start.11 = (bf16[240,512]{1,0:T(8,128)(2,1)S(1)}, bf16[240,512]{1,0:T(8,128)(2,1)S(1)}, u32[]{:S(2)}, u32[]{:S(2)}) collective-permute-start(bf16[240,512]{1,0:T(8,128)(2,1)S(1)} %split_block.4), channel_id=1, source_target_pairs={{0,8},{8,0},{16,24},{24,16},{1,9},{9,1},{17,25},{25,17},{2,10},{10... | collective-permute-start | bytes 737288 | tf_op jit(solution)/shard_map/ppermute | solution.py:270
  22.3 8.8 %collective-permute-start.5 = (bf16[240,512]{1,0:T(8,128)(2,1)S(1)}, bf16[240,512]{1,0:T(8,128)(2,1)S(1)}, u32[]{:S(2)}, u32[]{:S(2)}) collective-permute-start(bf16[240,512]{1,0:T(8,128)(2,1)S(1)} %broadcast_select_fusion.refs_2_), channel_id=1, source_target_pairs={{0,1},{1,0},{2,3},{3,2},{4,5},{5,4},{6,7},{7,6},{8,9},{9,8},{10,11... | collective-permute-start | bytes 737288 | tf_op jit(solution)/shard_map/ppermute | solution.py:270
  23.7 1.9 %collective-permute-start.7 = (bf16[128,512]{1,0:T(8,128)(2,1)S(1)}, bf16[128,512]{1,0:T(8,128)(2,1)S(1)}, u32[]{:S(2)}, u32[]{:S(2)}) collective-permute-start(bf16[128,512]{1,0:T(8,128)(2,1)S(1)} %get-tuple-element.30), channel_id=1, source_target_pairs={{0,8},{8,0},{16,24},{24,16},{1,9},{9,1},{17,25},{25,17},{2,10},{10... | collective-permute-start | bytes 393224 | tf_op jit(solution)/shard_map/ppermute | solution.py:270
  23.8 3.3 %collective-permute-start.9 = (bf16[128,512]{1,0:T(8,128)(2,1)S(1)}, bf16[128,512]{1,0:T(8,128)(2,1)S(1)}, u32[]{:S(2)}, u32[]{:S(2)}) collective-permute-start(bf16[128,512]{1,0:T(8,128)(2,1)S(1)} %get-tuple-element.38), channel_id=1, source_target_pairs={{0,8},{8,0},{16,24},{24,16},{1,9},{9,1},{17,25},{25,17},{2,10},{10... | collective-permute-start | bytes 393224 | tf_op jit(solution)/shard_map/ppermute | solution.py:270
  25.6 1.3 %collective-permute-start.10 = (bf16[112,512]{1,0:T(8,128)(2,1)S(1)}, bf16[112,512]{1,0:T(8,128)(2,1)S(1)}, u32[]{:S(2)}, u32[]{:S(2)}) collective-permute-start(bf16[112,512]{1,0:T(8,128)(2,1)S(1)} %get-tuple-element.39), channel_id=1, source_target_pairs={{0,8},{8,0},{16,24},{24,16},{1,9},{9,1},{17,25},{25,17},{2,10},{10... | collective-permute-start | bytes 344072 | tf_op jit(solution)/shard_map/ppermute | solution.py:270
  25.6 3.0 %collective-permute-start.12 = (bf16[64,512]{1,0:T(8,128)(2,1)S(1)}, bf16[64,512]{1,0:T(8,128)(2,1)S(1)}, u32[]{:S(2)}, u32[]{:S(2)}) collective-permute-start(bf16[64,512]{1,0:T(8,128)(2,1)S(1)} %get-tuple-element.41), channel_id=1, source_target_pairs={{0,8},{8,0},{16,24},{24,16},{1,9},{9,1},{17,25},{25,17},{2,10},{10... | collective-permute-start | bytes 196616 | tf_op jit(solution)/shard_map/ppermute | solution.py:270
  26.9 1.8 %collective-permute-start.13 = (bf16[64,512]{1,0:T(8,128)(2,1)S(1)}, bf16[64,512]{1,0:T(8,128)(2,1)S(1)}, u32[]{:S(2)}, u32[]{:S(2)}) collective-permute-start(bf16[64,512]{1,0:T(8,128)(2,1)S(1)} %get-tuple-element.42), channel_id=1, source_target_pairs={{0,8},{8,0},{16,24},{24,16},{1,9},{9,1},{17,25},{25,17},{2,10},{10... | collective-permute-start | bytes 196616 | tf_op jit(solution)/shard_map/ppermute | solution.py:270
  27.1 1.6 %collective-permute-start.14 = (bf16[64,512]{1,0:T(8,128)(2,1)S(1)}, bf16[64,512]{1,0:T(8,128)(2,1)S(1)}, u32[]{:S(2)}, u32[]{:S(2)}) collective-permute-start(bf16[64,512]{1,0:T(8,128)(2,1)S(1)} %get-tuple-element.43), channel_id=1, source_target_pairs={{0,8},{8,0},{16,24},{24,16},{1,9},{9,1},{17,25},{25,17},{2,10},{10... | collective-permute-start | bytes 196616 | tf_op jit(solution)/shard_map/ppermute | solution.py:270
  27.4 1.2 %collective-permute-start.15 = (bf16[48,512]{1,0:T(8,128)(2,1)S(1)}, bf16[48,512]{1,0:T(8,128)(2,1)S(1)}, u32[]{:S(2)}, u32[]{:S(2)}) collective-permute-start(bf16[48,512]{1,0:T(8,128)(2,1)S(1)} %get-tuple-element.44), channel_id=1, source_target_pairs={{0,8},{8,0},{16,24},{24,16},{1,9},{9,1},{17,25},{25,17},{2,10},{10... | collective-permute-start | bytes 147464 | tf_op jit(solution)/shard_map/ppermute | solution.py:270

commit v5 on v3

--- a/solution.py
+++ b/solution.py
@@ -78,15 +78,14 @@
 def lay_columns(blocks, labels, per, cols, weight_ref):
     chunks, col_slides, _, _ = cols.shape
     span = col_slides * CHUNK
-    mine = lax.axis_index("grp")
     lane = lax.broadcasted_iota(jnp.int32, (1, span), 1)
     counts = jnp.ones((1, span), jnp.float32)
     whole = {}
     for (mask, pair, offset), block in zip(labels, blocks):
         for start in range(0, block.shape[0], CHUNK):
             whole.setdefault((mask, pair), {})[offset + start] = block, start
-    for (mask, pair), parts in whole.items():
-        first = ((mine ^ mask) * 2 + pair) * per
+    for place, parts in enumerate(whole.values()):
+        first = place * per
         heads = {spot: ref[pl.ds(start, CHUNK), :LANES].astype(jnp.float32) for spot, (ref, start) in parts.items()}
         tops = [heads[s * MAIN][:1] for s in range(per)]
         for spot, (ref, start) in parts.items():
@@ -197,32 +196,34 @@
     )(*pieces, cols, weight)
 
 
-def finish_kernel(size, groups, count, per, slots, *refs):
-    pieces, (cols, weight_ref), refs = refs[:count], refs[count : count + 2], refs[count + 2 :]
+def finish_kernel(size, groups, count, per, slots, labels, *refs):
+    pieces, refs = refs[:count], refs[count:]
+    sets, refs = [refs[2 * n : 2 * n + 2] for n in range(len(labels))], refs[2 * len(labels) :]
     done, out_ref = refs[:-1], refs[-1]
-    wide = out_ref.shape[2]
     block = lax.axis_index("dev") // groups
-    first = sum(ref.shape[0] for ref in done)
-
-    def keep(r, best):
-        for g in range(groups):
-            out_ref[g * (size // groups) + block, r] = best[g * wide : (g + 1) * wide]
-
-    r = 0
-    for ref in done:
-        for n in range(ref.shape[0]):
-            keep(r, ref[n])
-            r += 1
-    score_pieces(pieces, cols, weight_ref, per, slots, lambda t, best: keep(first + t, best))
-
-
-def finish_step(pieces, cols, weight, done, size, groups, per, slots):
-    count = len(pieces) * per + sum(part.shape[0] for part in done)
-    wide = done[0].shape[1] // groups
-    operands = [*pieces, cols, weight, *done]
-    return pl.pallas_call(
-        functools.partial(finish_kernel, size, groups, len(pieces), per, slots),
-        out_shape=jax.ShapeDtypeStruct((size, count, wide, slots), jnp.float32),
+    mine = lax.axis_index("grp")
+
+    def keep(n, r, best):
+        for place, (mask, pair) in enumerate(labels[n]):
+            part = best[place * per : (place + 1) * per]
+            out_ref[(mine ^ mask) * (size // groups) + block, r, pl.ds(pair * per, per), :] = part
+
+    for n in range(len(labels)):
+        first = 0
+        for ref in done[n :: len(labels)]:
+            for r in range(ref.shape[0]):
+                keep(n, first + r, ref[r])
+            first += ref.shape[0]
+        cols, weight_ref = sets[n]
+        score_pieces(pieces, cols, weight_ref, per, slots, lambda t, best: keep(n, first + t, best))
+
+
+def finish_step(pieces, sets, done, labels, size, groups, per, slots):
+    count = len(pieces) * per + sum(part.shape[0] for part in done[:: len(labels)])
+    operands = [*pieces, *[part for both in sets for part in both], *done]
+    return pl.pallas_call(
+        functools.partial(finish_kernel, size, groups, len(pieces), per, slots, labels),
+        out_shape=jax.ShapeDtypeStruct((size, count, 2 * per, slots), jnp.float32),
         in_specs=[VMEM] * len(operands),
         out_specs=VMEM,
         compiler_params=PARAMS,
@@ -319,26 +320,36 @@
         bit //= 2
     cut = [2, 2, 2, 4]
     cut = [split_block(block, count) for block, count in zip(columns, cut + [2] * len(columns))]
-    swapped = [flip(part, "grp", 1) for part in cut[0]]
-    swapped, cut[-1] = lax.optimization_barrier((swapped, cut[-1]))
-    mirror, across, cut[-2] = lax.optimization_barrier((mirror, across, cut[-2]))
-    ends = [
-        (part, (mask, pair, sum(other.shape[0] for other in parts[:n])))
-        for parts, (mask, pair, _) in zip(cut, labels)
-        for n, part in enumerate(parts)
-    ]
-    columns += swapped + [flip(part, "grp", 1) for part, _ in ends[len(swapped) :]]
-    labels += [(mask ^ 1, pair, offset) for _, (mask, pair, offset) in ends]
+    swapped = [[flip(part, "grp", 1) for part in cut[n]] for n in range(2)]
     rows = [(whole, 0), (across, 1), (mirror, 6), (flip(mirror, "dev", 1), 7)]
     bit = 8
     while bit < size:
         rows += [(flip(block, "dev", bit), mask ^ bit) for block, mask in rows]
         bit *= 2
-    blocks = [block for block, _ in rows]
-    early, late = blocks[:-1], blocks[-1:]
-    cols, weight, scored = first_step(early[:3], columns, labels, per, slots)
-    done = [scored, *[score_step(early[i : i + 3], cols, weight, per, slots) for i in range(3, len(early), 3)]]
-    results = finish_step(late, cols, weight, done, size, groups, per, slots)
+    early, late = [block for block, _ in rows[:-1]], [block for block, _ in rows[-1:]]
+
+    def column_set(which):
+        blocks, names = [columns[n] for n in which], [labels[n] for n in which]
+        for n in which:
+            mask, pair, _ = labels[n]
+            since = 0
+            for part in swapped[n]:
+                blocks.append(part)
+                names.append((mask ^ 1, pair, since))
+                since += part.shape[0]
+        return blocks, tuple(names)
+
+    near, near_names = column_set(range(2))
+    *near_set, scored = first_step(early[:3], near, near_names, per, slots)
+    scored, cut[-1] = lax.optimization_barrier((scored, cut[-1]))
+    swapped += [[flip(part, "grp", 1) for part in parts] for parts in cut[2:]]
+    far, far_names = column_set(range(2, len(columns)))
+    *far_set, rest = first_step(early[:3], far, far_names, per, slots)
+    sets, done = [near_set, far_set], [scored, rest]
+    for i in range(3, len(early), 3):
+        done += [score_step(early[i : i + 3], *both, per, slots) for both in sets]
+    places = [tuple(dict.fromkeys((mask, pair) for mask, pair, _ in names)) for names in (near_names, far_names)]
+    results = finish_step(late, sets, done, places, size, groups, per, slots)
     parts = lax.all_to_all(results, "dev", split_axis=0, concat_axis=0, tiled=True)
     names = tuple((mask, s) for _, mask in rows for s in range(per))
     best, chamfer = gather_results(parts, names, size, groups)

time: 42.8 us -> 41.6 us (0.972)
  starting transfers between devices: 14.7 us -> 13.5 us
  blocking collectives: 14.4 us -> 13.4 us
  waiting for transfers between devices: 7.01 us -> 7.79 us
    ppermute x16, starting transfers between devices: 14.7 us -> 13.5 us  [flip(): lax.ppermute(value, axis, [(i, i ^ mask) for i in range(lax.axis_size(axi...]
    all_to_all x1, blocking collectives: 14.4 us -> 13.4 us  [on_device(): lax.all_to_all(results, 'dev', split_axis=0, concat_axis=0, tiled=True)]
    ppermute x16, waiting for transfers between devices: 7.01 us -> 7.79 us  [flip(): lax.ppermute(value, axis, [(i, i ^ mask) for i in range(lax.axis_size(axi...]
    pallas_call x1 -> x2, Pallas kernels: 2.4 us -> 2.54 us  [first_step(): pl.pallas_call(functools.partial(first_kernel, len(pieces), labels, per,...]
  transfers between devices with their start and end apart: 16 -> 16, of which waited for: 5 -> 4; matrix products, arithmetic and copies ran while one was open for 0% -> 0% of each run, Pallas kernels for 6% -> 6%
where the time goes in v5:
time: 41.6 us; the launch traced here: 41.4 us
  starting transfers between devices  13.5 us (32%)
  blocking collectives  13.4 us (32%)
  waiting for transfers between devices  7.79 us (19%)
  Pallas kernels  5.97 us (14%)
  between operations  0.71 us (2%)
    ppermute x16, starting transfers between devices, flip(): lax.ppermute(value, axis, [(i, i ^ mask) for i in range(lax.axis_size(axi...  13.5 us
    all_to_all x1, blocking collectives, on_device(): lax.all_to_all(results, 'dev', split_axis=0, concat_axis=0, tiled=True)  13.4 us
    ppermute x16, waiting for transfers between devices, flip(): lax.ppermute(value, axis, [(i, i ^ mask) for i in range(lax.axis_size(axi...  7.79 us
    pallas_call x2, Pallas kernels, first_step(): pl.pallas_call(functools.partial(first_kernel, len(pieces), labels, per,...  2.54 us
    pallas_call x1, Pallas kernels, embed_tiles(): pl.pallas_call(embed_kernel, out_shape=jax.ShapeDtypeStruct((slides * USE...  1.73 us
    pallas_call x1, Pallas kernels, finish_step(): pl.pallas_call(functools.partial(finish_kernel, size, groups, len(pieces)...  0.93 us
  transfers between devices with their start and end apart: 16, of which 4 were waited for; matrix products, arithmetic and copies ran while one was open for 0% of the time, Pallas kernels for 6%

profile of v5, /device:TPU:0, one launch (start us, length us, event | category | flops | bytes accessed | tf_op | source)
XLA Modules:
  0.0 41.4 jit_solution(12561890872112770473)
XLA Ops:
  0.6 1.7 %embed.1.in_ref.refs_0_.refs_3_ = bf16[240,512]{1,0:T(8,128)(2,1)S(1)} custom-call(bf16[2,128,768]{2,1,0:T(8,128)(2,1)} %features_in.1, s32[2]{0:T(128)} %counts_in.1, bf16[768,512]{1,0:T(8,128)(2,1)} %projection_in.1), custom_call_target="tpu_custom_call" | custom-call | tf_op jit(solution)/shard_map/embed/pallas_call | solution.py:52
  2.4 3.1 %collective-permute-start.3 = (bf16[240,512]{1,0:T(8,128)(2,1)S(1)}, bf16[240,512]{1,0:T(8,128)(2,1)S(1)}, u32[]{:S(2)}, u32[]{:S(2)}) collective-permute-start(bf16[240,512]{1,0:T(8,128)(2,1)S(1)} %embed.1.in_ref.refs_0_.refs_3_), channel_id=1, source_target_pairs={{0,2},{1,3},{2,0},{3,1},{4,6},{5,7},{6,4},{7,5},{8,10},{9,11},{10,... | collective-permute-start | bytes 737288 | tf_op jit(solution)/shard_map/ppermute | solution.py:271
  5.5 0.1 collective-permute-start.5
  5.6 2.5 %collective-permute-start = (bf16[240,512]{1,0:T(8,128)(2,1)S(1)}, bf16[240,512]{1,0:T(8,128)(2,1)S(1)}, u32[]{:S(2)}, u32[]{:S(2)}) collective-permute-start(bf16[240,512]{1,0:T(8,128)(2,1)S(1)} %embed.1.in_ref.refs_0_.refs_3_), channel_id=1, source_target_pairs={{0,6},{1,7},{2,4},{3,5},{4,2},{5,3},{6,0},{7,1},{8,14},{9,15},{10,... | collective-permute-start | bytes 737288 | tf_op jit(solution)/shard_map/ppermute | solution.py:271
  8.1 1.5 %collective-permute-start.8 = (bf16[240,512]{1,0:T(8,128)(2,1)S(1)}, bf16[240,512]{1,0:T(8,128)(2,1)S(1)}, u32[]{:S(2)}, u32[]{:S(2)}) collective-permute-start(bf16[240,512]{1,0:T(8,128)(2,1)S(1)} %embed.1.in_ref.refs_0_.refs_3_), channel_id=1, source_target_pairs={{0,16},{8,24},{16,0},{24,8},{1,17},{9,25},{17,1},{25,9},{2,18},{10... | collective-permute-start | bytes 737288 | tf_op jit(solution)/shard_map/ppermute | solution.py:271
  9.6 1.5 %collective-permute-start.2 = (bf16[240,512]{1,0:T(8,128)(2,1)S(1)}, bf16[240,512]{1,0:T(8,128)(2,1)S(1)}, u32[]{:S(2)}, u32[]{:S(2)}) collective-permute-start(bf16[240,512]{1,0:T(8,128)(2,1)S(1)} %embed.1.in_ref.refs_0_.refs_3_), channel_id=1, source_target_pairs={{0,1},{1,0},{2,3},{3,2},{4,5},{5,4},{6,7},{7,6},{8,9},{9,8},{10,11... | collective-permute-start | bytes 737288 | tf_op jit(solution)/shard_map/ppermute | solution.py:271
  11.1 0.0 collective-permute-done.5.refs_6_
  11.1 0.0 collective-permute-start.4
  11.1 0.7 %collective-permute-done.3.in_ref.refs_4_ = bf16[240,512]{1,0:T(8,128)(2,1)S(1)} collective-permute-done((bf16[240,512]{1,0:T(8,128)(2,1)S(1)}, bf16[240,512]{1,0:T(8,128)(2,1)S(1)}, u32[]{:S(2)}, u32[]{:S(2)}) %collective-permute-start.3) | collective-permute-done | bytes 245792 | tf_op jit(solution)/shard_map/ppermute | solution.py:271
  11.8 1.5 %collective-permute-start.9 = (bf16[240,512]{1,0:T(8,128)(2,1)S(1)}, bf16[240,512]{1,0:T(8,128)(2,1)S(1)}, u32[]{:S(2)}, u32[]{:S(2)}) collective-permute-start(bf16[240,512]{1,0:T(8,128)(2,1)S(1)} %collective-permute-done.3.in_ref.refs_4_), channel_id=1, source_target_pairs={{0,16},{8,24},{16,0},{24,8},{1,17},{9,25},{17,1},{25,9},{2,18},{10... | collective-permute-start | bytes 737288 | tf_op jit(solution)/shard_map/ppermute | solution.py:271
  13.4 0.1 collective-permute-start.7
  13.5 5.5 %collective-permute-done.refs_2_ = bf16[240,512]{1,0:T(8,128)(2,1)S(1)} collective-permute-done((bf16[240,512]{1,0:T(8,128)(2,1)S(1)}, bf16[240,512]{1,0:T(8,128)(2,1)S(1)}, u32[]{:S(2)}, u32[]{:S(2)}) %collective-permute-start) | collective-permute-done | bytes 245792 | tf_op jit(solution)/shard_map/ppermute | solution.py:271
  19.0 1.5 %collective-permute-start.1 = (bf16[240,512]{1,0:T(8,128)(2,1)S(1)}, bf16[240,512]{1,0:T(8,128)(2,1)S(1)}, u32[]{:S(2)}, u32[]{:S(2)}) collective-permute-start(bf16[240,512]{1,0:T(8,128)(2,1)S(1)} %collective-permute-done.refs_2_), channel_id=1, source_target_pairs={{0,1},{1,0},{2,3},{3,2},{4,5},{5,4},{6,7},{7,6},{8,9},{9,8},{10,11... | collective-permute-start | bytes 737288 | tf_op jit(solution)/shard_map/ppermute | solution.py:271
  20.5 0.0 collective-permute-done.8.in_ref.refs_3_
  20.5 0.0 collective-permute-start.6
  20.5 0.0 collective-permute-done.2.refs_1_
  20.5 0.6 %collective-permute-start.10 = (bf16[128,512]{1,0:T(8,128)(2,1)S(1)}, bf16[128,512]{1,0:T(8,128)(2,1)S(1)}, u32[]{:S(2)}, u32[]{:S(2)}) collective-permute-start(bf16[128,512]{1,0:T(8,128)(2,1)S(1)} %get-tuple-element.31), channel_id=1, source_target_pairs={{0,8},{8,0},{16,24},{24,16},{1,9},{9,1},{17,25},{25,17},{2,10},{10... | collective-permute-start | bytes 393224 | tf_op jit(solution)/shard_map/ppermute | solution.py:271
  21.1 0.1 collective-permute-start.11
  21.2 0.7 %collective-permute-done.6.refs_7_ = bf16[128,512]{1,0:T(8,128)(2,1)S(1)} collective-permute-done((bf16[128,512]{1,0:T(8,128)(2,1)S(1)}, bf16[128,512]{1,0:T(8,128)(2,1)S(1)}, u32[]{:S(2)}, u32[]{:S(2)}) %collective-permute-start.6) | collective-permute-done | bytes 131104 | tf_op jit(solution)/shard_map/ppermute | solution.py:271
  21.8 1.3 %first_scores.2 = (bf16[8,8,16,512]{3,2,1,0:T(8,128)(2,1)S(1)}, f32[8,128]{1,0:T(8,128)S(1)}, f32[6,8,128]{2,1,0:T(8,128)S(1)}) custom-call(bf16[240,512]{1,0:T(8,128)(2,1)S(1)} %embed.1.in_ref.refs_0_.refs_3_, bf16[240,512]{1,0:T(8,128)(2,1)S(1)} %collective-permute-done.2.refs_1_, bf16[240,512]{1,0:T(8,128)(2,1)S(1)} %collective-permute-done.refs_2_, ...), custom_call_target="tpu_custom_call" | custom-call | tf_op jit(solution)/shard_map/first_scores/pallas_call | solution.py:164
  23.1 0.2 collective-permute-start.12
  23.3 0.4 collective-permute-start.13
  23.7 0.0 collective-permute-done.11.refs_6_
  23.7 0.1 collective-permute-start.14
  23.8 0.4 collective-permute-start.15
  24.2 0.9 %collective-permute-done.15.refs_10_ = bf16[48,512]{1,0:T(8,128)(2,1)S(1)} collective-permute-done((bf16[48,512]{1,0:T(8,128)(2,1)S(1)}, bf16[48,512]{1,0:T(8,128)(2,1)S(1)}, u32[]{:S(2)}, u32[]{:S(2)}) %collective-permute-start.15) | collective-permute-done | bytes 49184 | tf_op jit(solution)/shard_map/ppermute | solution.py:271
  25.1 0.0 collective-permute-done.12.refs_7_
  25.1 0.0 collective-permute-done.13.refs_8_
  25.1 1.3 %first_scores.3 = (bf16[8,8,16,512]{3,2,1,0:T(8,128)(2,1)S(1)}, f32[8,128]{1,0:T(8,128)S(1)}, f32[6,8,128]{2,1,0:T(8,128)S(1)}) custom-call(bf16[240,512]{1,0:T(8,128)(2,1)S(1)} %embed.1.in_ref.refs_0_.refs_3_, bf16[240,512]{1,0:T(8,128)(2,1)S(1)} %collective-permute-done.2.refs_1_, bf16[240,512]{1,0:T(8,128)(2,1)S(1)} %collective-permute-done.refs_2_, ...), custom_call_target="tpu_custom_call" | custom-call | tf_op jit(solution)/shard_map/first_scores/pallas_call | solution.py:164
  26.4 0.9 %finish.1 = f32[8,8,4,128]{3,2,1,0:T(4,128)S(1)} custom-call(bf16[240,512]{1,0:T(8,128)(2,1)S(1)} %collective-permute-done.1.refs_0_, bf16[8,8,16,512]{3,2,1,0:T(8,128)(2,1)S(1)} %get-tuple-element.29.refs_1_, f32[8,128]{1,0:T(8,128)S(1)} %get-tuple-element.30.refs_2_, bf16[8,8,16,512]{3,2,1,0:T(8,128)(2,1)S(1)} %get-tuple-element.42.refs_3_, ...), custom_call_target="tpu_custom_call" | custom-call | tf_op jit(solution)/shard_map/finish/pallas_call | solution.py:224
  27.3 13.4 %all_to_all.5.parts = f32[8,8,4,128]{3,2,1,0:T(4,128)S(1)} all-to-all(f32[8,8,4,128]{3,2,1,0:T(4,128)S(1)} %finish.1), channel_id=1, replica_groups=mesh['grp'=4,'dev'=8] {'dev'}, dimensions={0} | all-to-all | bytes 262144 | tf_op jit(solution)/shard_map/all_to_all | solution.py:353
  40.7 0.7 %gather_results.1 = (f32[16,8,128]{2,1,0:T(8,128)}, f32[8,16]{1,0:T(8,128)}) custom-call(f32[8,8,4,128]{3,2,1,0:T(4,128)S(1)} %all_to_all.5.parts), custom_call_target="tpu_custom_call" | custom-call | tf_op jit(solution)/shard_map/gather_results/pallas_call | solution.py:257
  (10 shorter events, 0.1 us)
Async XLA Ops:
  2.4 9.4 %collective-permute-start.3 = (bf16[240,512]{1,0:T(8,128)(2,1)S(1)}, bf16[240,512]{1,0:T(8,128)(2,1)S(1)}, u32[]{:S(2)}, u32[]{:S(2)}) collective-permute-start(bf16[240,512]{1,0:T(8,128)(2,1)S(1)} %embed.1.in_ref.refs_0_.refs_3_), channel_id=1, source_target_pairs={{0,2},{1,3},{2,0},{3,1},{4,6},{5,7},{6,4},{7,5},{8,10},{9,11},{10,... | collective-permute-start | bytes 737288 | tf_op jit(solution)/shard_map/ppermute | solution.py:271
  5.5 5.6 %collective-permute-start.5 = (bf16[112,512]{1,0:T(8,128)(2,1)S(1)}, bf16[112,512]{1,0:T(8,128)(2,1)S(1)}, u32[]{:S(2)}, u32[]{:S(2)}) collective-permute-start(bf16[112,512]{1,0:T(8,128)(2,1)S(1)} %get-tuple-element.26), channel_id=1, source_target_pairs={{0,8},{8,0},{16,24},{24,16},{1,9},{9,1},{17,25},{25,17},{2,10},{10... | collective-permute-start | bytes 344072 | tf_op jit(solution)/shard_map/ppermute | solution.py:271
  5.6 13.4 %collective-permute-start = (bf16[240,512]{1,0:T(8,128)(2,1)S(1)}, bf16[240,512]{1,0:T(8,128)(2,1)S(1)}, u32[]{:S(2)}, u32[]{:S(2)}) collective-permute-start(bf16[240,512]{1,0:T(8,128)(2,1)S(1)} %embed.1.in_ref.refs_0_.refs_3_), channel_id=1, source_target_pairs={{0,6},{1,7},{2,4},{3,5},{4,2},{5,3},{6,0},{7,1},{8,14},{9,15},{10,... | collective-permute-start | bytes 737288 | tf_op jit(solution)/shard_map/ppermute | solution.py:271
  8.1 12.4 %collective-permute-start.8 = (bf16[240,512]{1,0:T(8,128)(2,1)S(1)}, bf16[240,512]{1,0:T(8,128)(2,1)S(1)}, u32[]{:S(2)}, u32[]{:S(2)}) collective-permute-start(bf16[240,512]{1,0:T(8,128)(2,1)S(1)} %embed.1.in_ref.refs_0_.refs_3_), channel_id=1, source_target_pairs={{0,16},{8,24},{16,0},{24,8},{1,17},{9,25},{17,1},{25,9},{2,18},{10... | collective-permute-start | bytes 737288 | tf_op jit(solution)/shard_map/ppermute | solution.py:271
  9.6 10.9 %collective-permute-start.2 = (bf16[240,512]{1,0:T(8,128)(2,1)S(1)}, bf16[240,512]{1,0:T(8,128)(2,1)S(1)}, u32[]{:S(2)}, u32[]{:S(2)}) collective-permute-start(bf16[240,512]{1,0:T(8,128)(2,1)S(1)} %embed.1.in_ref.refs_0_.refs_3_), channel_id=1, source_target_pairs={{0,1},{1,0},{2,3},{3,2},{4,5},{5,4},{6,7},{7,6},{8,9},{9,8},{10,11... | collective-permute-start | bytes 737288 | tf_op jit(solution)/shard_map/ppermute | solution.py:271
  11.1 2.3 %collective-permute-start.4 = (bf16[128,512]{1,0:T(8,128)(2,1)S(1)}, bf16[128,512]{1,0:T(8,128)(2,1)S(1)}, u32[]{:S(2)}, u32[]{:S(2)}) collective-permute-start(bf16[128,512]{1,0:T(8,128)(2,1)S(1)} %get-tuple-element.25), channel_id=1, source_target_pairs={{0,8},{8,0},{16,24},{24,16},{1,9},{9,1},{17,25},{25,17},{2,10},{10... | collective-permute-start | bytes 393224 | tf_op jit(solution)/shard_map/ppermute | solution.py:271
  11.8 11.3 %collective-permute-start.9 = (bf16[240,512]{1,0:T(8,128)(2,1)S(1)}, bf16[240,512]{1,0:T(8,128)(2,1)S(1)}, u32[]{:S(2)}, u32[]{:S(2)}) collective-permute-start(bf16[240,512]{1,0:T(8,128)(2,1)S(1)} %collective-permute-done.3.in_ref.refs_4_), channel_id=1, source_target_pairs={{0,16},{8,24},{16,0},{24,8},{1,17},{9,25},{17,1},{25,9},{2,18},{10... | collective-permute-start | bytes 737288 | tf_op jit(solution)/shard_map/ppermute | solution.py:271
  13.4 7.7 %collective-permute-start.7 = (bf16[112,512]{1,0:T(8,128)(2,1)S(1)}, bf16[112,512]{1,0:T(8,128)(2,1)S(1)}, u32[]{:S(2)}, u32[]{:S(2)}) collective-permute-start(bf16[112,512]{1,0:T(8,128)(2,1)S(1)} %get-tuple-element.28), channel_id=1, source_target_pairs={{0,8},{8,0},{16,24},{24,16},{1,9},{9,1},{17,25},{25,17},{2,10},{10... | collective-permute-start | bytes 344072 | tf_op jit(solution)/shard_map/ppermute | solution.py:271
  19.0 7.4 %collective-permute-start.1 = (bf16[240,512]{1,0:T(8,128)(2,1)S(1)}, bf16[240,512]{1,0:T(8,128)(2,1)S(1)}, u32[]{:S(2)}, u32[]{:S(2)}) collective-permute-start(bf16[240,512]{1,0:T(8,128)(2,1)S(1)} %collective-permute-done.refs_2_), channel_id=1, source_target_pairs={{0,1},{1,0},{2,3},{3,2},{4,5},{5,4},{6,7},{7,6},{8,9},{9,8},{10,11... | collective-permute-start | bytes 737288 | tf_op jit(solution)/shard_map/ppermute | solution.py:271
  20.5 1.3 %collective-permute-start.6 = (bf16[128,512]{1,0:T(8,128)(2,1)S(1)}, bf16[128,512]{1,0:T(8,128)(2,1)S(1)}, u32[]{:S(2)}, u32[]{:S(2)}) collective-permute-start(bf16[128,512]{1,0:T(8,128)(2,1)S(1)} %get-tuple-element.27), channel_id=1, source_target_pairs={{0,8},{8,0},{16,24},{24,16},{1,9},{9,1},{17,25},{25,17},{2,10},{10... | collective-permute-start | bytes 393224 | tf_op jit(solution)/shard_map/ppermute | solution.py:271
  20.5 3.3 %collective-permute-start.10 = (bf16[128,512]{1,0:T(8,128)(2,1)S(1)}, bf16[128,512]{1,0:T(8,128)(2,1)S(1)}, u32[]{:S(2)}, u32[]{:S(2)}) collective-permute-start(bf16[128,512]{1,0:T(8,128)(2,1)S(1)} %get-tuple-element.31), channel_id=1, source_target_pairs={{0,8},{8,0},{16,24},{24,16},{1,9},{9,1},{17,25},{25,17},{2,10},{10... | collective-permute-start | bytes 393224 | tf_op jit(solution)/shard_map/ppermute | solution.py:271
  21.1 2.6 %collective-permute-start.11 = (bf16[112,512]{1,0:T(8,128)(2,1)S(1)}, bf16[112,512]{1,0:T(8,128)(2,1)S(1)}, u32[]{:S(2)}, u32[]{:S(2)}) collective-permute-start(bf16[112,512]{1,0:T(8,128)(2,1)S(1)} %get-tuple-element.32), channel_id=1, source_target_pairs={{0,8},{8,0},{16,24},{24,16},{1,9},{9,1},{17,25},{25,17},{2,10},{10... | collective-permute-start | bytes 344072 | tf_op jit(solution)/shard_map/ppermute | solution.py:271
  23.1 2.0 %collective-permute-start.12 = (bf16[64,512]{1,0:T(8,128)(2,1)S(1)}, bf16[64,512]{1,0:T(8,128)(2,1)S(1)}, u32[]{:S(2)}, u32[]{:S(2)}) collective-permute-start(bf16[64,512]{1,0:T(8,128)(2,1)S(1)} %get-tuple-element.38), channel_id=1, source_target_pairs={{0,8},{8,0},{16,24},{24,16},{1,9},{9,1},{17,25},{25,17},{2,10},{10... | collective-permute-start | bytes 196616 | tf_op jit(solution)/shard_map/ppermute | solution.py:271
  23.3 1.8 %collective-permute-start.13 = (bf16[64,512]{1,0:T(8,128)(2,1)S(1)}, bf16[64,512]{1,0:T(8,128)(2,1)S(1)}, u32[]{:S(2)}, u32[]{:S(2)}) collective-permute-start(bf16[64,512]{1,0:T(8,128)(2,1)S(1)} %get-tuple-element.39), channel_id=1, source_target_pairs={{0,8},{8,0},{16,24},{24,16},{1,9},{9,1},{17,25},{25,17},{2,10},{10... | collective-permute-start | bytes 196616 | tf_op jit(solution)/shard_map/ppermute | solution.py:271
  23.7 1.4 %collective-permute-start.14 = (bf16[64,512]{1,0:T(8,128)(2,1)S(1)}, bf16[64,512]{1,0:T(8,128)(2,1)S(1)}, u32[]{:S(2)}, u32[]{:S(2)}) collective-permute-start(bf16[64,512]{1,0:T(8,128)(2,1)S(1)} %get-tuple-element.40), channel_id=1, source_target_pairs={{0,8},{8,0},{16,24},{24,16},{1,9},{9,1},{17,25},{25,17},{2,10},{10... | collective-permute-start | bytes 196616 | tf_op jit(solution)/shard_map/ppermute | solution.py:271
  23.8 1.2 %collective-permute-start.15 = (bf16[48,512]{1,0:T(8,128)(2,1)S(1)}, bf16[48,512]{1,0:T(8,128)(2,1)S(1)}, u32[]{:S(2)}, u32[]{:S(2)}) collective-permute-start(bf16[48,512]{1,0:T(8,128)(2,1)S(1)} %get-tuple-element.41), channel_id=1, source_target_pairs={{0,8},{8,0},{16,24},{24,16},{1,9},{9,1},{17,25},{25,17},{2,10},{10... | collective-permute-start | bytes 147464 | tf_op jit(solution)/shard_map/ppermute | solution.py:271

commit v6 on v5

--- a/solution.py
+++ b/solution.py
@@ -311,7 +311,7 @@
     slots = features.shape[1]
     whole = embed_tiles(features, tile_counts, projection)
     per = features.shape[0]
-    mirror, across, beside = flip(whole, "dev", 6), flip(whole, "dev", 1), flip(whole, "dev", 2)
+    opposite, across, beside = flip(whole, "dev", 4), flip(whole, "dev", 1), flip(whole, "dev", 2)
     labels, columns = [(0, 0, 0), (0, 1, 0)], [whole, beside]
     bit = groups // 2
     while bit > 1:
@@ -321,7 +321,7 @@
     cut = [2, 2, 2, 4]
     cut = [split_block(block, count) for block, count in zip(columns, cut + [2] * len(columns))]
     swapped = [[flip(part, "grp", 1) for part in cut[n]] for n in range(2)]
-    rows = [(whole, 0), (across, 1), (mirror, 6), (flip(mirror, "dev", 1), 7)]
+    rows = [(whole, 0), (across, 1), (opposite, 4), (flip(opposite, "dev", 1), 5)]
     bit = 8
     while bit < size:
         rows += [(flip(block, "dev", bit), mask ^ bit) for block, mask in rows]

time: 41.6 us -> 41.3 us (level)
  blocking collectives: 13.4 us -> 11.8 us
  waiting for transfers between devices: 7.79 us -> 8.79 us
    all_to_all x1, blocking collectives: 13.4 us -> 11.8 us  [on_device(): lax.all_to_all(results, 'dev', split_axis=0, concat_axis=0, tiled=True)]
    ppermute x16, waiting for transfers between devices: 7.79 us -> 8.79 us  [flip(): lax.ppermute(value, axis, [(i, i ^ mask) for i in range(lax.axis_size(axi...]
  transfers between devices with their start and end apart: 16 -> 16, of which waited for: 4 -> 5; matrix products, arithmetic and copies ran while one was open for 0% -> 0% of each run, Pallas kernels for 6% -> 6%
where the time goes in v6:
time: 41.3 us; the launch traced here: 41.1 us
  starting transfers between devices  13.8 us (33%)
  blocking collectives  11.8 us (29%)
  waiting for transfers between devices  8.79 us (21%)
  Pallas kernels  5.97 us (14%)
  between operations  0.71 us (2%)
    ppermute x16, starting transfers between devices, flip(): lax.ppermute(value, axis, [(i, i ^ mask) for i in range(lax.axis_size(axi...  13.8 us
    all_to_all x1, blocking collectives, on_device(): lax.all_to_all(results, 'dev', split_axis=0, concat_axis=0, tiled=True)  11.8 us
    ppermute x16, waiting for transfers between devices, flip(): lax.ppermute(value, axis, [(i, i ^ mask) for i in range(lax.axis_size(axi...  8.79 us
    pallas_call x2, Pallas kernels, first_step(): pl.pallas_call(functools.partial(first_kernel, len(pieces), labels, per,...  2.54 us
    pallas_call x1, Pallas kernels, embed_tiles(): pl.pallas_call(embed_kernel, out_shape=jax.ShapeDtypeStruct((slides * USE...  1.73 us
    pallas_call x1, Pallas kernels, finish_step(): pl.pallas_call(functools.partial(finish_kernel, size, groups, len(pieces)...  0.92 us
  transfers between devices with their start and end apart: 16, of which 5 were waited for; matrix products, arithmetic and copies ran while one was open for 0% of the time, Pallas kernels for 6%

profile of v6, /device:TPU:0, one launch (start us, length us, event | category | flops | bytes accessed | tf_op | source)
XLA Modules:
  0.0 41.1 jit_solution(253936782995548197)
XLA Ops:
  0.6 1.7 %embed.1.in_ref.refs_0_.refs_3_ = bf16[240,512]{1,0:T(8,128)(2,1)S(1)} custom-call(bf16[2,128,768]{2,1,0:T(8,128)(2,1)} %features_in.1, s32[2]{0:T(128)} %counts_in.1, bf16[768,512]{1,0:T(8,128)(2,1)} %projection_in.1), custom_call_target="tpu_custom_call" | custom-call | tf_op jit(solution)/shard_map/embed/pallas_call | solution.py:52
  2.4 3.1 %collective-permute-start.3 = (bf16[240,512]{1,0:T(8,128)(2,1)S(1)}, bf16[240,512]{1,0:T(8,128)(2,1)S(1)}, u32[]{:S(2)}, u32[]{:S(2)}) collective-permute-start(bf16[240,512]{1,0:T(8,128)(2,1)S(1)} %embed.1.in_ref.refs_0_.refs_3_), channel_id=1, source_target_pairs={{0,2},{1,3},{2,0},{3,1},{4,6},{5,7},{6,4},{7,5},{8,10},{9,11},{10,... | collective-permute-start | bytes 737288 | tf_op jit(solution)/shard_map/ppermute | solution.py:271
  5.5 0.1 collective-permute-start.5
  5.6 2.7 %collective-permute-start = (bf16[240,512]{1,0:T(8,128)(2,1)S(1)}, bf16[240,512]{1,0:T(8,128)(2,1)S(1)}, u32[]{:S(2)}, u32[]{:S(2)}) collective-permute-start(bf16[240,512]{1,0:T(8,128)(2,1)S(1)} %embed.1.in_ref.refs_0_.refs_3_), channel_id=1, source_target_pairs={{0,4},{1,5},{2,6},{3,7},{4,0},{5,1},{6,2},{7,3},{8,12},{9,13},{10,... | collective-permute-start | bytes 737288 | tf_op jit(solution)/shard_map/ppermute | solution.py:271
  8.2 1.5 %collective-permute-start.8 = (bf16[240,512]{1,0:T(8,128)(2,1)S(1)}, bf16[240,512]{1,0:T(8,128)(2,1)S(1)}, u32[]{:S(2)}, u32[]{:S(2)}) collective-permute-start(bf16[240,512]{1,0:T(8,128)(2,1)S(1)} %embed.1.in_ref.refs_0_.refs_3_), channel_id=1, source_target_pairs={{0,16},{8,24},{16,0},{24,8},{1,17},{9,25},{17,1},{25,9},{2,18},{10... | collective-permute-start | bytes 737288 | tf_op jit(solution)/shard_map/ppermute | solution.py:271
  9.7 1.5 %collective-permute-start.2 = (bf16[240,512]{1,0:T(8,128)(2,1)S(1)}, bf16[240,512]{1,0:T(8,128)(2,1)S(1)}, u32[]{:S(2)}, u32[]{:S(2)}) collective-permute-start(bf16[240,512]{1,0:T(8,128)(2,1)S(1)} %embed.1.in_ref.refs_0_.refs_3_), channel_id=1, source_target_pairs={{0,1},{1,0},{2,3},{3,2},{4,5},{5,4},{6,7},{7,6},{8,9},{9,8},{10,11... | collective-permute-start | bytes 737288 | tf_op jit(solution)/shard_map/ppermute | solution.py:271
  11.2 0.0 collective-permute-done.5.refs_6_
  11.2 0.0 collective-permute-start.4
  11.2 4.3 %collective-permute-done.3.in_ref.refs_4_ = bf16[240,512]{1,0:T(8,128)(2,1)S(1)} collective-permute-done((bf16[240,512]{1,0:T(8,128)(2,1)S(1)}, bf16[240,512]{1,0:T(8,128)(2,1)S(1)}, u32[]{:S(2)}, u32[]{:S(2)}) %collective-permute-start.3) | collective-permute-done | bytes 245792 | tf_op jit(solution)/shard_map/ppermute | solution.py:271
  15.5 1.7 %collective-permute-start.9 = (bf16[240,512]{1,0:T(8,128)(2,1)S(1)}, bf16[240,512]{1,0:T(8,128)(2,1)S(1)}, u32[]{:S(2)}, u32[]{:S(2)}) collective-permute-start(bf16[240,512]{1,0:T(8,128)(2,1)S(1)} %collective-permute-done.3.in_ref.refs_4_), channel_id=1, source_target_pairs={{0,16},{8,24},{16,0},{24,8},{1,17},{9,25},{17,1},{25,9},{2,18},{10... | collective-permute-start | bytes 737288 | tf_op jit(solution)/shard_map/ppermute | solution.py:271
  17.2 0.1 collective-permute-start.7
  17.3 2.8 %collective-permute-done.refs_2_ = bf16[240,512]{1,0:T(8,128)(2,1)S(1)} collective-permute-done((bf16[240,512]{1,0:T(8,128)(2,1)S(1)}, bf16[240,512]{1,0:T(8,128)(2,1)S(1)}, u32[]{:S(2)}, u32[]{:S(2)}) %collective-permute-start) | collective-permute-done | bytes 245792 | tf_op jit(solution)/shard_map/ppermute | solution.py:271
  20.1 1.5 %collective-permute-start.1 = (bf16[240,512]{1,0:T(8,128)(2,1)S(1)}, bf16[240,512]{1,0:T(8,128)(2,1)S(1)}, u32[]{:S(2)}, u32[]{:S(2)}) collective-permute-start(bf16[240,512]{1,0:T(8,128)(2,1)S(1)} %collective-permute-done.refs_2_), channel_id=1, source_target_pairs={{0,1},{1,0},{2,3},{3,2},{4,5},{5,4},{6,7},{7,6},{8,9},{9,8},{10,11... | collective-permute-start | bytes 737288 | tf_op jit(solution)/shard_map/ppermute | solution.py:271
  21.6 0.0 collective-permute-done.8.in_ref.refs_3_
  21.6 0.0 collective-permute-start.6
  21.7 0.0 collective-permute-done.2.refs_1_
  21.7 0.6 %collective-permute-start.10 = (bf16[128,512]{1,0:T(8,128)(2,1)S(1)}, bf16[128,512]{1,0:T(8,128)(2,1)S(1)}, u32[]{:S(2)}, u32[]{:S(2)}) collective-permute-start(bf16[128,512]{1,0:T(8,128)(2,1)S(1)} %get-tuple-element.31), channel_id=1, source_target_pairs={{0,8},{8,0},{16,24},{24,16},{1,9},{9,1},{17,25},{25,17},{2,10},{10... | collective-permute-start | bytes 393224 | tf_op jit(solution)/shard_map/ppermute | solution.py:271
  22.3 0.1 collective-permute-start.11
  22.3 0.7 %collective-permute-done.6.refs_7_ = bf16[128,512]{1,0:T(8,128)(2,1)S(1)} collective-permute-done((bf16[128,512]{1,0:T(8,128)(2,1)S(1)}, bf16[128,512]{1,0:T(8,128)(2,1)S(1)}, u32[]{:S(2)}, u32[]{:S(2)}) %collective-permute-start.6) | collective-permute-done | bytes 131104 | tf_op jit(solution)/shard_map/ppermute | solution.py:271
  23.0 1.3 %first_scores.2 = (bf16[8,8,16,512]{3,2,1,0:T(8,128)(2,1)S(1)}, f32[8,128]{1,0:T(8,128)S(1)}, f32[6,8,128]{2,1,0:T(8,128)S(1)}) custom-call(bf16[240,512]{1,0:T(8,128)(2,1)S(1)} %embed.1.in_ref.refs_0_.refs_3_, bf16[240,512]{1,0:T(8,128)(2,1)S(1)} %collective-permute-done.2.refs_1_, bf16[240,512]{1,0:T(8,128)(2,1)S(1)} %collective-permute-done.refs_2_, ...), custom_call_target="tpu_custom_call" | custom-call | tf_op jit(solution)/shard_map/first_scores/pallas_call | solution.py:164
  24.3 0.0 collective-permute-done.9.in_ref.refs_4_
  24.3 0.2 collective-permute-start.12
  24.5 0.4 collective-permute-start.13
  24.9 0.1 collective-permute-start.14
  25.0 0.0 collective-permute-done.10.refs_5_
  25.0 0.4 collective-permute-start.15
  25.4 0.9 %collective-permute-done.15.refs_10_ = bf16[48,512]{1,0:T(8,128)(2,1)S(1)} collective-permute-done((bf16[48,512]{1,0:T(8,128)(2,1)S(1)}, bf16[48,512]{1,0:T(8,128)(2,1)S(1)}, u32[]{:S(2)}, u32[]{:S(2)}) %collective-permute-start.15) | collective-permute-done | bytes 49184 | tf_op jit(solution)/shard_map/ppermute | solution.py:271
  26.3 1.3 %first_scores.3 = (bf16[8,8,16,512]{3,2,1,0:T(8,128)(2,1)S(1)}, f32[8,128]{1,0:T(8,128)S(1)}, f32[6,8,128]{2,1,0:T(8,128)S(1)}) custom-call(bf16[240,512]{1,0:T(8,128)(2,1)S(1)} %embed.1.in_ref.refs_0_.refs_3_, bf16[240,512]{1,0:T(8,128)(2,1)S(1)} %collective-permute-done.2.refs_1_, bf16[240,512]{1,0:T(8,128)(2,1)S(1)} %collective-permute-done.refs_2_, ...), custom_call_target="tpu_custom_call" | custom-call | tf_op jit(solution)/shard_map/first_scores/pallas_call | solution.py:164
  27.5 0.1 collective-permute-done.1.refs_0_
  27.7 0.9 %finish.1 = f32[8,8,4,128]{3,2,1,0:T(4,128)S(1)} custom-call(bf16[240,512]{1,0:T(8,128)(2,1)S(1)} %collective-permute-done.1.refs_0_, bf16[8,8,16,512]{3,2,1,0:T(8,128)(2,1)S(1)} %get-tuple-element.29.refs_1_, f32[8,128]{1,0:T(8,128)S(1)} %get-tuple-element.30.refs_2_, bf16[8,8,16,512]{3,2,1,0:T(8,128)(2,1)S(1)} %get-tuple-element.42.refs_3_, ...), custom_call_target="tpu_custom_call" | custom-call | tf_op jit(solution)/shard_map/finish/pallas_call | solution.py:224
  28.6 11.8 %all_to_all.5.parts = f32[8,8,4,128]{3,2,1,0:T(4,128)S(1)} all-to-all(f32[8,8,4,128]{3,2,1,0:T(4,128)S(1)} %finish.1), channel_id=1, replica_groups=mesh['grp'=4,'dev'=8] {'dev'}, dimensions={0} | all-to-all | bytes 262144 | tf_op jit(solution)/shard_map/all_to_all | solution.py:353
  40.4 0.7 %gather_results.1 = (f32[16,8,128]{2,1,0:T(8,128)}, f32[8,16]{1,0:T(8,128)}) custom-call(f32[8,8,4,128]{3,2,1,0:T(4,128)S(1)} %all_to_all.5.parts), custom_call_target="tpu_custom_call" | custom-call | tf_op jit(solution)/shard_map/gather_results/pallas_call | solution.py:257
  (10 shorter events, 0.1 us)
Async XLA Ops:
  2.4 13.1 %collective-permute-start.3 = (bf16[240,512]{1,0:T(8,128)(2,1)S(1)}, bf16[240,512]{1,0:T(8,128)(2,1)S(1)}, u32[]{:S(2)}, u32[]{:S(2)}) collective-permute-start(bf16[240,512]{1,0:T(8,128)(2,1)S(1)} %embed.1.in_ref.refs_0_.refs_3_), channel_id=1, source_target_pairs={{0,2},{1,3},{2,0},{3,1},{4,6},{5,7},{6,4},{7,5},{8,10},{9,11},{10,... | collective-permute-start | bytes 737288 | tf_op jit(solution)/shard_map/ppermute | solution.py:271
  5.5 5.7 %collective-permute-start.5 = (bf16[112,512]{1,0:T(8,128)(2,1)S(1)}, bf16[112,512]{1,0:T(8,128)(2,1)S(1)}, u32[]{:S(2)}, u32[]{:S(2)}) collective-permute-start(bf16[112,512]{1,0:T(8,128)(2,1)S(1)} %get-tuple-element.26), channel_id=1, source_target_pairs={{0,8},{8,0},{16,24},{24,16},{1,9},{9,1},{17,25},{25,17},{2,10},{10... | collective-permute-start | bytes 344072 | tf_op jit(solution)/shard_map/ppermute | solution.py:271
  5.6 14.6 %collective-permute-start = (bf16[240,512]{1,0:T(8,128)(2,1)S(1)}, bf16[240,512]{1,0:T(8,128)(2,1)S(1)}, u32[]{:S(2)}, u32[]{:S(2)}) collective-permute-start(bf16[240,512]{1,0:T(8,128)(2,1)S(1)} %embed.1.in_ref.refs_0_.refs_3_), channel_id=1, source_target_pairs={{0,4},{1,5},{2,6},{3,7},{4,0},{5,1},{6,2},{7,3},{8,12},{9,13},{10,... | collective-permute-start | bytes 737288 | tf_op jit(solution)/shard_map/ppermute | solution.py:271
  8.2 13.4 %collective-permute-start.8 = (bf16[240,512]{1,0:T(8,128)(2,1)S(1)}, bf16[240,512]{1,0:T(8,128)(2,1)S(1)}, u32[]{:S(2)}, u32[]{:S(2)}) collective-permute-start(bf16[240,512]{1,0:T(8,128)(2,1)S(1)} %embed.1.in_ref.refs_0_.refs_3_), channel_id=1, source_target_pairs={{0,16},{8,24},{16,0},{24,8},{1,17},{9,25},{17,1},{25,9},{2,18},{10... | collective-permute-start | bytes 737288 | tf_op jit(solution)/shard_map/ppermute | solution.py:271
  9.7 11.9 %collective-permute-start.2 = (bf16[240,512]{1,0:T(8,128)(2,1)S(1)}, bf16[240,512]{1,0:T(8,128)(2,1)S(1)}, u32[]{:S(2)}, u32[]{:S(2)}) collective-permute-start(bf16[240,512]{1,0:T(8,128)(2,1)S(1)} %embed.1.in_ref.refs_0_.refs_3_), channel_id=1, source_target_pairs={{0,1},{1,0},{2,3},{3,2},{4,5},{5,4},{6,7},{7,6},{8,9},{9,8},{10,11... | collective-permute-start | bytes 737288 | tf_op jit(solution)/shard_map/ppermute | solution.py:271
  11.2 6.0 %collective-permute-start.4 = (bf16[128,512]{1,0:T(8,128)(2,1)S(1)}, bf16[128,512]{1,0:T(8,128)(2,1)S(1)}, u32[]{:S(2)}, u32[]{:S(2)}) collective-permute-start(bf16[128,512]{1,0:T(8,128)(2,1)S(1)} %get-tuple-element.25), channel_id=1, source_target_pairs={{0,8},{8,0},{16,24},{24,16},{1,9},{9,1},{17,25},{25,17},{2,10},{10... | collective-permute-start | bytes 393224 | tf_op jit(solution)/shard_map/ppermute | solution.py:271
  15.5 8.7 %collective-permute-start.9 = (bf16[240,512]{1,0:T(8,128)(2,1)S(1)}, bf16[240,512]{1,0:T(8,128)(2,1)S(1)}, u32[]{:S(2)}, u32[]{:S(2)}) collective-permute-start(bf16[240,512]{1,0:T(8,128)(2,1)S(1)} %collective-permute-done.3.in_ref.refs_4_), channel_id=1, source_target_pairs={{0,16},{8,24},{16,0},{24,8},{1,17},{9,25},{17,1},{25,9},{2,18},{10... | collective-permute-start | bytes 737288 | tf_op jit(solution)/shard_map/ppermute | solution.py:271
  17.2 5.0 %collective-permute-start.7 = (bf16[112,512]{1,0:T(8,128)(2,1)S(1)}, bf16[112,512]{1,0:T(8,128)(2,1)S(1)}, u32[]{:S(2)}, u32[]{:S(2)}) collective-permute-start(bf16[112,512]{1,0:T(8,128)(2,1)S(1)} %get-tuple-element.28), channel_id=1, source_target_pairs={{0,8},{8,0},{16,24},{24,16},{1,9},{9,1},{17,25},{25,17},{2,10},{10... | collective-permute-start | bytes 344072 | tf_op jit(solution)/shard_map/ppermute | solution.py:271
  20.1 7.5 %collective-permute-start.1 = (bf16[240,512]{1,0:T(8,128)(2,1)S(1)}, bf16[240,512]{1,0:T(8,128)(2,1)S(1)}, u32[]{:S(2)}, u32[]{:S(2)}) collective-permute-start(bf16[240,512]{1,0:T(8,128)(2,1)S(1)} %collective-permute-done.refs_2_), channel_id=1, source_target_pairs={{0,1},{1,0},{2,3},{3,2},{4,5},{5,4},{6,7},{7,6},{8,9},{9,8},{10,11... | collective-permute-start | bytes 737288 | tf_op jit(solution)/shard_map/ppermute | solution.py:271
  21.6 1.3 %collective-permute-start.6 = (bf16[128,512]{1,0:T(8,128)(2,1)S(1)}, bf16[128,512]{1,0:T(8,128)(2,1)S(1)}, u32[]{:S(2)}, u32[]{:S(2)}) collective-permute-start(bf16[128,512]{1,0:T(8,128)(2,1)S(1)} %get-tuple-element.27), channel_id=1, source_target_pairs={{0,8},{8,0},{16,24},{24,16},{1,9},{9,1},{17,25},{25,17},{2,10},{10... | collective-permute-start | bytes 393224 | tf_op jit(solution)/shard_map/ppermute | solution.py:271
  21.7 3.3 %collective-permute-start.10 = (bf16[128,512]{1,0:T(8,128)(2,1)S(1)}, bf16[128,512]{1,0:T(8,128)(2,1)S(1)}, u32[]{:S(2)}, u32[]{:S(2)}) collective-permute-start(bf16[128,512]{1,0:T(8,128)(2,1)S(1)} %get-tuple-element.31), channel_id=1, source_target_pairs={{0,8},{8,0},{16,24},{24,16},{1,9},{9,1},{17,25},{25,17},{2,10},{10... | collective-permute-start | bytes 393224 | tf_op jit(solution)/shard_map/ppermute | solution.py:271
  22.3 2.6 %collective-permute-start.11 = (bf16[112,512]{1,0:T(8,128)(2,1)S(1)}, bf16[112,512]{1,0:T(8,128)(2,1)S(1)}, u32[]{:S(2)}, u32[]{:S(2)}) collective-permute-start(bf16[112,512]{1,0:T(8,128)(2,1)S(1)} %get-tuple-element.32), channel_id=1, source_target_pairs={{0,8},{8,0},{16,24},{24,16},{1,9},{9,1},{17,25},{25,17},{2,10},{10... | collective-permute-start | bytes 344072 | tf_op jit(solution)/shard_map/ppermute | solution.py:271
  24.3 2.0 %collective-permute-start.12 = (bf16[64,512]{1,0:T(8,128)(2,1)S(1)}, bf16[64,512]{1,0:T(8,128)(2,1)S(1)}, u32[]{:S(2)}, u32[]{:S(2)}) collective-permute-start(bf16[64,512]{1,0:T(8,128)(2,1)S(1)} %get-tuple-element.38), channel_id=1, source_target_pairs={{0,8},{8,0},{16,24},{24,16},{1,9},{9,1},{17,25},{25,17},{2,10},{10... | collective-permute-start | bytes 196616 | tf_op jit(solution)/shard_map/ppermute | solution.py:271
  24.5 1.8 %collective-permute-start.13 = (bf16[64,512]{1,0:T(8,128)(2,1)S(1)}, bf16[64,512]{1,0:T(8,128)(2,1)S(1)}, u32[]{:S(2)}, u32[]{:S(2)}) collective-permute-start(bf16[64,512]{1,0:T(8,128)(2,1)S(1)} %get-tuple-element.39), channel_id=1, source_target_pairs={{0,8},{8,0},{16,24},{24,16},{1,9},{9,1},{17,25},{25,17},{2,10},{10... | collective-permute-start | bytes 196616 | tf_op jit(solution)/shard_map/ppermute | solution.py:271
  24.9 1.4 %collective-permute-start.14 = (bf16[64,512]{1,0:T(8,128)(2,1)S(1)}, bf16[64,512]{1,0:T(8,128)(2,1)S(1)}, u32[]{:S(2)}, u32[]{:S(2)}) collective-permute-start(bf16[64,512]{1,0:T(8,128)(2,1)S(1)} %get-tuple-element.40), channel_id=1, source_target_pairs={{0,8},{8,0},{16,24},{24,16},{1,9},{9,1},{17,25},{25,17},{2,10},{10... | collective-permute-start | bytes 196616 | tf_op jit(solution)/shard_map/ppermute | solution.py:271
  25.0 1.2 %collective-permute-start.15 = (bf16[48,512]{1,0:T(8,128)(2,1)S(1)}, bf16[48,512]{1,0:T(8,128)(2,1)S(1)}, u32[]{:S(2)}, u32[]{:S(2)}) collective-permute-start(bf16[48,512]{1,0:T(8,128)(2,1)S(1)} %get-tuple-element.41), channel_id=1, source_target_pairs={{0,8},{8,0},{16,24},{24,16},{1,9},{9,1},{17,25},{25,17},{2,10},{10... | collective-permute-start | bytes 147464 | tf_op jit(solution)/shard_map/ppermute | solution.py:271

commit v7 on v6

--- a/solution.py
+++ b/solution.py
@@ -20,8 +20,13 @@
 PARAMS = pltpu.CompilerParams(vmem_limit_bytes=VMEM_LIMIT)
 
 
+def part_sizes(rows, count):
+    ends = [-(-n * rows // (count * CHUNK)) * CHUNK for n in range(count + 1)]
+    return [end - start for start, end in zip(ends, ends[1:])]
+
+
 def embed_kernel(features_in, counts_in, projection_in, *refs):
-    out_ref, features_ref, counts_ref, projection_ref, sems = refs
+    (out_ref, *part_refs), (features_ref, counts_ref, projection_ref, sems) = refs[:-4], refs[-4:]
     copies = [
         pltpu.make_async_copy(projection_in, projection_ref, sems.at[0]),
         pltpu.make_async_copy(features_in, features_ref, sems.at[1]),
@@ -31,10 +36,12 @@
         copy.start()
     for copy in copies:
         copy.wait()
-    slides, slots, _ = features_ref.shape
+    slides, slots, depth = features_ref.shape
+    tiles = features_ref[...].reshape(slides * slots, depth)
+    every = jnp.dot(tiles, projection_ref[...], preferred_element_type=jnp.float32)
     tails = []
     for s in range(slides):
-        raw = jnp.dot(features_ref[s], projection_ref[...], preferred_element_type=jnp.float32)
+        raw = every[s * slots : (s + 1) * slots]
         scale = lax.rsqrt(jnp.sum(raw * raw, axis=1, keepdims=True) + 1e-06)
         unit = raw * scale
         slot = lax.broadcasted_iota(jnp.int32, unit.shape, 0)
@@ -44,16 +51,20 @@
         out_ref[pl.ds(s * MAIN, MAIN), :] = unit[:MAIN].astype(out_ref.dtype)
         tails.append(unit[MAIN:USED])
     out_ref[pl.ds(slides * MAIN, slides * TAIL), :] = jnp.concatenate(tails, axis=0).astype(out_ref.dtype)
+    start = 0
+    for part_ref in part_refs:
+        part_ref[...] = out_ref[pl.ds(start, part_ref.shape[0]), :]
+        start += part_ref.shape[0]
 
 
 def embed_tiles(features, tile_counts, projection):
-    slides = features.shape[0]
-    width = projection.shape[1]
-    return pl.pallas_call(
+    rows, width = features.shape[0] * USED, projection.shape[1]
+    sizes = [rows, *part_sizes(rows, 2)]
+    whole, *parts = pl.pallas_call(
         embed_kernel,
-        out_shape=jax.ShapeDtypeStruct((slides * USED, width), jnp.bfloat16),
+        out_shape=[jax.ShapeDtypeStruct((size, width), jnp.bfloat16) for size in sizes],
         in_specs=[HBM] * 3,
-        out_specs=VMEM,
+        out_specs=[VMEM] * len(sizes),
         scratch_shapes=[
             pltpu.VMEM(features.shape, features.dtype),
             pltpu.SMEM(tile_counts.shape, tile_counts.dtype),
@@ -63,6 +74,7 @@
         compiler_params=PARAMS,
         name="embed",
     )(*[pltpu.with_memory_space_constraint(x, pltpu.HBM) for x in (features, tile_counts, projection)])
+    return whole, parts
 
 
 def slide_count(head, row):
@@ -295,10 +307,9 @@
 
 def split_block(block, count):
     rows, width = block.shape
-    ends = [-(-n * rows // (count * CHUNK)) * CHUNK for n in range(count + 1)]
     return pl.pallas_call(
         split_kernel,
-        out_shape=[jax.ShapeDtypeStruct((end - start, width), block.dtype) for start, end in zip(ends, ends[1:])],
+        out_shape=[jax.ShapeDtypeStruct((size, width), block.dtype) for size in part_sizes(rows, count)],
         in_specs=[VMEM],
         out_specs=[VMEM] * count,
         compiler_params=PARAMS,
@@ -309,7 +320,7 @@
 def on_device(features, tile_counts, projection):
     size, groups = lax.axis_size("dev"), lax.axis_size("grp")
     slots = features.shape[1]
-    whole = embed_tiles(features, tile_counts, projection)
+    whole, halves = embed_tiles(features, tile_counts, projection)
     per = features.shape[0]
     opposite, across, beside = flip(whole, "dev", 4), flip(whole, "dev", 1), flip(whole, "dev", 2)
     labels, columns = [(0, 0, 0), (0, 1, 0)], [whole, beside]
@@ -318,8 +329,8 @@
         columns += [flip(block, "grp", bit) for block in columns]
         labels += [(mask ^ bit, pair, 0) for mask, pair, _ in labels]
         bit //= 2
-    cut = [2, 2, 2, 4]
-    cut = [split_block(block, count) for block, count in zip(columns, cut + [2] * len(columns))]
+    cut = [2, 2, 2, 3]
+    cut = [halves] + [split_block(block, count) for block, count in zip(columns[1:], cut[1:] + [2] * len(columns))]
     swapped = [[flip(part, "grp", 1) for part in cut[n]] for n in range(2)]
     rows = [(whole, 0), (across, 1), (opposite, 4), (flip(opposite, "dev", 1), 5)]
     bit = 8

time: 41.3 us -> 41.3 us (level)
  starting transfers between devices: 13.8 us -> 13.3 us
  waiting for transfers between devices: 8.79 us -> 9.29 us
    ppermute x16 -> x15, waiting for transfers between devices: 8.79 us -> 9.29 us  [flip(): lax.ppermute(value, axis, [(i, i ^ mask) for i in range(lax.axis_size(axi...]
    ppermute x16 -> x15, starting transfers between devices: 13.8 us -> 13.3 us  [flip(): lax.ppermute(value, axis, [(i, i ^ mask) for i in range(lax.axis_size(axi...]
    pallas_call x5 -> x4, Pallas kernels: 1.8 us -> 1.78 us  [the longest x1 1.73 us: embed_tiles(): pl.pallas_call(embed_kernel, out_shape=[jax.ShapeDtypeStruct((size, width...]
  transfers between devices with their start and end apart: 16 -> 15, of which waited for: 5 -> 7; matrix products, arithmetic and copies ran while one was open for 0% -> 0% of each run, Pallas kernels for 6% -> 6%
where the time goes in v7:
time: 41.3 us; the launch traced here: 41.1 us
  starting transfers between devices  13.3 us (32%)
  blocking collectives  11.8 us (29%)
  waiting for transfers between devices  9.29 us (22%)
  Pallas kernels  5.93 us (14%)
  between operations  0.69 us (2%)
    ppermute x15, starting transfers between devices, flip(): lax.ppermute(value, axis, [(i, i ^ mask) for i in range(lax.axis_size(axi...  13.3 us
    all_to_all x1, blocking collectives, on_device(): lax.all_to_all(results, 'dev', split_axis=0, concat_axis=0, tiled=True)  11.8 us
    ppermute x15, waiting for transfers between devices, flip(): lax.ppermute(value, axis, [(i, i ^ mask) for i in range(lax.axis_size(axi...  9.29 us
    pallas_call x2, Pallas kernels, first_step(): pl.pallas_call(functools.partial(first_kernel, len(pieces), labels, per,...  2.54 us
    pallas_call x1, Pallas kernels, embed_tiles(): pl.pallas_call(embed_kernel, out_shape=[jax.ShapeDtypeStruct((size, width...  1.73 us
    pallas_call x1, Pallas kernels, finish_step(): pl.pallas_call(functools.partial(finish_kernel, size, groups, len(pieces)...  0.92 us
  transfers between devices with their start and end apart: 15, of which 7 were waited for; matrix products, arithmetic and copies ran while one was open for 0% of the time, Pallas kernels for 6%

profile of v7, /device:TPU:0, one launch (start us, length us, event | category | flops | bytes accessed | tf_op | source)
XLA Modules:
  0.0 41.1 jit_solution(7538325589830978904)
XLA Ops:
  0.6 1.7 %embed.1 = (bf16[240,512]{1,0:T(8,128)(2,1)S(1)}, bf16[128,512]{1,0:T(8,128)(2,1)S(1)}, bf16[112,512]{1,0:T(8,128)(2,1)S(1)}) custom-call(bf16[2,128,768]{2,1,0:T(8,128)(2,1)} %features_in.1, s32[2]{0:T(128)} %counts_in.1, bf16[768,512]{1,0:T(8,128)(2,1)} %projection_in.1), custom_call_target="tpu_custom_call" | custom-call | tf_op jit(solution)/shard_map/embed/pallas_call | solution.py:63
  2.4 3.1 %collective-permute-start.3 = (bf16[240,512]{1,0:T(8,128)(2,1)S(1)}, bf16[240,512]{1,0:T(8,128)(2,1)S(1)}, u32[]{:S(2)}, u32[]{:S(2)}) collective-permute-start(bf16[240,512]{1,0:T(8,128)(2,1)S(1)} %get-tuple-element.24.refs_0_.refs_3_), channel_id=1, source_target_pairs={{0,2},{1,3},{2,0},{3,1},{4,6},{5,7},{6,4},{7,5},{8,10},{9,11},{10,... | collective-permute-start | bytes 737288 | tf_op jit(solution)/shard_map/ppermute | solution.py:283
  5.5 2.6 %collective-permute-start = (bf16[240,512]{1,0:T(8,128)(2,1)S(1)}, bf16[240,512]{1,0:T(8,128)(2,1)S(1)}, u32[]{:S(2)}, u32[]{:S(2)}) collective-permute-start(bf16[240,512]{1,0:T(8,128)(2,1)S(1)} %get-tuple-element.24.refs_0_.refs_3_), channel_id=1, source_target_pairs={{0,4},{1,5},{2,6},{3,7},{4,0},{5,1},{6,2},{7,3},{8,12},{9,13},{10,... | collective-permute-start | bytes 737288 | tf_op jit(solution)/shard_map/ppermute | solution.py:283
  8.0 1.5 %collective-permute-start.8 = (bf16[240,512]{1,0:T(8,128)(2,1)S(1)}, bf16[240,512]{1,0:T(8,128)(2,1)S(1)}, u32[]{:S(2)}, u32[]{:S(2)}) collective-permute-start(bf16[240,512]{1,0:T(8,128)(2,1)S(1)} %get-tuple-element.24.refs_0_.refs_3_), channel_id=1, source_target_pairs={{0,16},{8,24},{16,0},{24,8},{1,17},{9,25},{17,1},{25,9},{2,18},{10... | collective-permute-start | bytes 737288 | tf_op jit(solution)/shard_map/ppermute | solution.py:283
  9.6 1.5 %collective-permute-start.2 = (bf16[240,512]{1,0:T(8,128)(2,1)S(1)}, bf16[240,512]{1,0:T(8,128)(2,1)S(1)}, u32[]{:S(2)}, u32[]{:S(2)}) collective-permute-start(bf16[240,512]{1,0:T(8,128)(2,1)S(1)} %get-tuple-element.24.refs_0_.refs_3_), channel_id=1, source_target_pairs={{0,1},{1,0},{2,3},{3,2},{4,5},{5,4},{6,7},{7,6},{8,9},{9,8},{10,11... | collective-permute-start | bytes 737288 | tf_op jit(solution)/shard_map/ppermute | solution.py:283
  11.1 0.0 collective-permute-done.5.refs_6_
  11.1 0.0 collective-permute-start.4
  11.1 4.5 %collective-permute-done.3.in_ref.refs_4_ = bf16[240,512]{1,0:T(8,128)(2,1)S(1)} collective-permute-done((bf16[240,512]{1,0:T(8,128)(2,1)S(1)}, bf16[240,512]{1,0:T(8,128)(2,1)S(1)}, u32[]{:S(2)}, u32[]{:S(2)}) %collective-permute-start.3) | collective-permute-done | bytes 245792 | tf_op jit(solution)/shard_map/ppermute | solution.py:283
  15.6 1.7 %collective-permute-start.9 = (bf16[240,512]{1,0:T(8,128)(2,1)S(1)}, bf16[240,512]{1,0:T(8,128)(2,1)S(1)}, u32[]{:S(2)}, u32[]{:S(2)}) collective-permute-start(bf16[240,512]{1,0:T(8,128)(2,1)S(1)} %collective-permute-done.3.in_ref.refs_4_), channel_id=1, source_target_pairs={{0,16},{8,24},{16,0},{24,8},{1,17},{9,25},{17,1},{25,9},{2,18},{10... | collective-permute-start | bytes 737288 | tf_op jit(solution)/shard_map/ppermute | solution.py:283
  17.3 0.0 collective-permute-done.4.refs_5_
  17.3 0.1 collective-permute-start.7
  17.4 2.6 %collective-permute-done.refs_2_ = bf16[240,512]{1,0:T(8,128)(2,1)S(1)} collective-permute-done((bf16[240,512]{1,0:T(8,128)(2,1)S(1)}, bf16[240,512]{1,0:T(8,128)(2,1)S(1)}, u32[]{:S(2)}, u32[]{:S(2)}) %collective-permute-start) | collective-permute-done | bytes 245792 | tf_op jit(solution)/shard_map/ppermute | solution.py:283
  20.0 1.5 %collective-permute-start.1 = (bf16[240,512]{1,0:T(8,128)(2,1)S(1)}, bf16[240,512]{1,0:T(8,128)(2,1)S(1)}, u32[]{:S(2)}, u32[]{:S(2)}) collective-permute-start(bf16[240,512]{1,0:T(8,128)(2,1)S(1)} %collective-permute-done.refs_2_), channel_id=1, source_target_pairs={{0,1},{1,0},{2,3},{3,2},{4,5},{5,4},{6,7},{7,6},{8,9},{9,8},{10,11... | collective-permute-start | bytes 737288 | tf_op jit(solution)/shard_map/ppermute | solution.py:283
  21.5 0.0 collective-permute-done.8.in_ref.refs_3_
  21.5 0.0 collective-permute-start.6
  21.6 0.6 %collective-permute-start.11 = (bf16[112,512]{1,0:T(8,128)(2,1)S(1)}, bf16[112,512]{1,0:T(8,128)(2,1)S(1)}, u32[]{:S(2)}, u32[]{:S(2)}) collective-permute-start(bf16[112,512]{1,0:T(8,128)(2,1)S(1)} %get-tuple-element.32), channel_id=1, source_target_pairs={{0,8},{8,0},{16,24},{24,16},{1,9},{9,1},{17,25},{25,17},{2,10},{10... | collective-permute-start | bytes 344072 | tf_op jit(solution)/shard_map/ppermute | solution.py:283
  22.1 0.0 collective-permute-done.7.refs_8_
  22.1 0.1 collective-permute-start.10
  22.2 0.7 %collective-permute-done.6.refs_7_ = bf16[128,512]{1,0:T(8,128)(2,1)S(1)} collective-permute-done((bf16[128,512]{1,0:T(8,128)(2,1)S(1)}, bf16[128,512]{1,0:T(8,128)(2,1)S(1)}, u32[]{:S(2)}, u32[]{:S(2)}) %collective-permute-start.6) | collective-permute-done | bytes 131104 | tf_op jit(solution)/shard_map/ppermute | solution.py:283
  22.9 1.3 %first_scores.2 = (bf16[8,8,16,512]{3,2,1,0:T(8,128)(2,1)S(1)}, f32[8,128]{1,0:T(8,128)S(1)}, f32[6,8,128]{2,1,0:T(8,128)S(1)}) custom-call(bf16[240,512]{1,0:T(8,128)(2,1)S(1)} %get-tuple-element.24.refs_0_.refs_3_, bf16[240,512]{1,0:T(8,128)(2,1)S(1)} %collective-permute-done.2.refs_1_, bf16[240,512]{1,0:T(8,128)(2,1)S(1)} %collective-permute-done.refs_2_, ...), custom_call_target="tpu_custom_call" | custom-call | tf_op jit(solution)/shard_map/first_scores/pallas_call | solution.py:176
  24.1 0.0 collective-permute-done.9.in_ref.refs_4_
  24.2 0.2 collective-permute-start.12
  24.4 0.4 collective-permute-start.13
  24.8 0.1 collective-permute-start.14
  24.9 0.6 %collective-permute-done.12.refs_7_ = bf16[80,512]{1,0:T(8,128)(2,1)S(1)} collective-permute-done((bf16[80,512]{1,0:T(8,128)(2,1)S(1)}, bf16[80,512]{1,0:T(8,128)(2,1)S(1)}, u32[]{:S(2)}, u32[]{:S(2)}) %collective-permute-start.12) | collective-permute-done | bytes 81952 | tf_op jit(solution)/shard_map/ppermute | solution.py:283
  25.5 0.2 collective-permute-done.13.refs_8_
  25.7 0.4 collective-permute-done.14.refs_9_
  26.0 1.3 %first_scores.3 = (bf16[8,8,16,512]{3,2,1,0:T(8,128)(2,1)S(1)}, f32[8,128]{1,0:T(8,128)S(1)}, f32[6,8,128]{2,1,0:T(8,128)S(1)}) custom-call(bf16[240,512]{1,0:T(8,128)(2,1)S(1)} %get-tuple-element.24.refs_0_.refs_3_, bf16[240,512]{1,0:T(8,128)(2,1)S(1)} %collective-permute-done.2.refs_1_, bf16[240,512]{1,0:T(8,128)(2,1)S(1)} %collective-permute-done.refs_2_, ...), custom_call_target="tpu_custom_call" | custom-call | tf_op jit(solution)/shard_map/first_scores/pallas_call | solution.py:176
  27.3 0.3 collective-permute-done.1.refs_0_
  27.6 0.9 %finish.1 = f32[8,8,4,128]{3,2,1,0:T(4,128)S(1)} custom-call(bf16[240,512]{1,0:T(8,128)(2,1)S(1)} %collective-permute-done.1.refs_0_, bf16[8,8,16,512]{3,2,1,0:T(8,128)(2,1)S(1)} %get-tuple-element.29.refs_1_, f32[8,128]{1,0:T(8,128)S(1)} %get-tuple-element.30.refs_2_, bf16[8,8,16,512]{3,2,1,0:T(8,128)(2,1)S(1)} %get-tuple-element.40.refs_3_, ...), custom_call_target="tpu_custom_call" | custom-call | tf_op jit(solution)/shard_map/finish/pallas_call | solution.py:236
  28.5 11.8 %all_to_all.5.parts = f32[8,8,4,128]{3,2,1,0:T(4,128)S(1)} all-to-all(f32[8,8,4,128]{3,2,1,0:T(4,128)S(1)} %finish.1), channel_id=1, replica_groups=mesh['grp'=4,'dev'=8] {'dev'}, dimensions={0} | all-to-all | bytes 262144 | tf_op jit(solution)/shard_map/all_to_all | solution.py:364
  40.4 0.7 %gather_results.1 = (f32[16,8,128]{2,1,0:T(8,128)}, f32[8,16]{1,0:T(8,128)}) custom-call(f32[8,8,4,128]{3,2,1,0:T(4,128)S(1)} %all_to_all.5.parts), custom_call_target="tpu_custom_call" | custom-call | tf_op jit(solution)/shard_map/gather_results/pallas_call | solution.py:269
  (7 shorter events, 0.1 us)
Async XLA Ops:
  2.4 13.2 %collective-permute-start.3 = (bf16[240,512]{1,0:T(8,128)(2,1)S(1)}, bf16[240,512]{1,0:T(8,128)(2,1)S(1)}, u32[]{:S(2)}, u32[]{:S(2)}) collective-permute-start(bf16[240,512]{1,0:T(8,128)(2,1)S(1)} %get-tuple-element.24.refs_0_.refs_3_), channel_id=1, source_target_pairs={{0,2},{1,3},{2,0},{3,1},{4,6},{5,7},{6,4},{7,5},{8,10},{9,11},{10,... | collective-permute-start | bytes 737288 | tf_op jit(solution)/shard_map/ppermute | solution.py:283
  5.5 5.6 %collective-permute-start.5 = (bf16[112,512]{1,0:T(8,128)(2,1)S(1)}, bf16[112,512]{1,0:T(8,128)(2,1)S(1)}, u32[]{:S(2)}, u32[]{:S(2)}) collective-permute-start(bf16[112,512]{1,0:T(8,128)(2,1)S(1)} %get-tuple-element.26), channel_id=1, source_target_pairs={{0,8},{8,0},{16,24},{24,16},{1,9},{9,1},{17,25},{25,17},{2,10},{10... | collective-permute-start | bytes 344072 | tf_op jit(solution)/shard_map/ppermute | solution.py:283
  5.5 14.6 %collective-permute-start = (bf16[240,512]{1,0:T(8,128)(2,1)S(1)}, bf16[240,512]{1,0:T(8,128)(2,1)S(1)}, u32[]{:S(2)}, u32[]{:S(2)}) collective-permute-start(bf16[240,512]{1,0:T(8,128)(2,1)S(1)} %get-tuple-element.24.refs_0_.refs_3_), channel_id=1, source_target_pairs={{0,4},{1,5},{2,6},{3,7},{4,0},{5,1},{6,2},{7,3},{8,12},{9,13},{10,... | collective-permute-start | bytes 737288 | tf_op jit(solution)/shard_map/ppermute | solution.py:283
  8.0 13.5 %collective-permute-start.8 = (bf16[240,512]{1,0:T(8,128)(2,1)S(1)}, bf16[240,512]{1,0:T(8,128)(2,1)S(1)}, u32[]{:S(2)}, u32[]{:S(2)}) collective-permute-start(bf16[240,512]{1,0:T(8,128)(2,1)S(1)} %get-tuple-element.24.refs_0_.refs_3_), channel_id=1, source_target_pairs={{0,16},{8,24},{16,0},{24,8},{1,17},{9,25},{17,1},{25,9},{2,18},{10... | collective-permute-start | bytes 737288 | tf_op jit(solution)/shard_map/ppermute | solution.py:283
  9.6 12.0 %collective-permute-start.2 = (bf16[240,512]{1,0:T(8,128)(2,1)S(1)}, bf16[240,512]{1,0:T(8,128)(2,1)S(1)}, u32[]{:S(2)}, u32[]{:S(2)}) collective-permute-start(bf16[240,512]{1,0:T(8,128)(2,1)S(1)} %get-tuple-element.24.refs_0_.refs_3_), channel_id=1, source_target_pairs={{0,1},{1,0},{2,3},{3,2},{4,5},{5,4},{6,7},{7,6},{8,9},{9,8},{10,11... | collective-permute-start | bytes 737288 | tf_op jit(solution)/shard_map/ppermute | solution.py:283
  11.1 6.3 %collective-permute-start.4 = (bf16[128,512]{1,0:T(8,128)(2,1)S(1)}, bf16[128,512]{1,0:T(8,128)(2,1)S(1)}, u32[]{:S(2)}, u32[]{:S(2)}) collective-permute-start(bf16[128,512]{1,0:T(8,128)(2,1)S(1)} %get-tuple-element.25), channel_id=1, source_target_pairs={{0,8},{8,0},{16,24},{24,16},{1,9},{9,1},{17,25},{25,17},{2,10},{10... | collective-permute-start | bytes 393224 | tf_op jit(solution)/shard_map/ppermute | solution.py:283
  15.6 8.5 %collective-permute-start.9 = (bf16[240,512]{1,0:T(8,128)(2,1)S(1)}, bf16[240,512]{1,0:T(8,128)(2,1)S(1)}, u32[]{:S(2)}, u32[]{:S(2)}) collective-permute-start(bf16[240,512]{1,0:T(8,128)(2,1)S(1)} %collective-permute-done.3.in_ref.refs_4_), channel_id=1, source_target_pairs={{0,16},{8,24},{16,0},{24,8},{1,17},{9,25},{17,1},{25,9},{2,18},{10... | collective-permute-start | bytes 737288 | tf_op jit(solution)/shard_map/ppermute | solution.py:283
  17.3 4.8 %collective-permute-start.7 = (bf16[112,512]{1,0:T(8,128)(2,1)S(1)}, bf16[112,512]{1,0:T(8,128)(2,1)S(1)}, u32[]{:S(2)}, u32[]{:S(2)}) collective-permute-start(bf16[112,512]{1,0:T(8,128)(2,1)S(1)} %get-tuple-element.28), channel_id=1, source_target_pairs={{0,8},{8,0},{16,24},{24,16},{1,9},{9,1},{17,25},{25,17},{2,10},{10... | collective-permute-start | bytes 344072 | tf_op jit(solution)/shard_map/ppermute | solution.py:283
  20.0 7.6 %collective-permute-start.1 = (bf16[240,512]{1,0:T(8,128)(2,1)S(1)}, bf16[240,512]{1,0:T(8,128)(2,1)S(1)}, u32[]{:S(2)}, u32[]{:S(2)}) collective-permute-start(bf16[240,512]{1,0:T(8,128)(2,1)S(1)} %collective-permute-done.refs_2_), channel_id=1, source_target_pairs={{0,1},{1,0},{2,3},{3,2},{4,5},{5,4},{6,7},{7,6},{8,9},{9,8},{10,11... | collective-permute-start | bytes 737288 | tf_op jit(solution)/shard_map/ppermute | solution.py:283
  21.5 1.3 %collective-permute-start.6 = (bf16[128,512]{1,0:T(8,128)(2,1)S(1)}, bf16[128,512]{1,0:T(8,128)(2,1)S(1)}, u32[]{:S(2)}, u32[]{:S(2)}) collective-permute-start(bf16[128,512]{1,0:T(8,128)(2,1)S(1)} %get-tuple-element.27), channel_id=1, source_target_pairs={{0,8},{8,0},{16,24},{24,16},{1,9},{9,1},{17,25},{25,17},{2,10},{10... | collective-permute-start | bytes 393224 | tf_op jit(solution)/shard_map/ppermute | solution.py:283
  21.6 3.2 %collective-permute-start.11 = (bf16[112,512]{1,0:T(8,128)(2,1)S(1)}, bf16[112,512]{1,0:T(8,128)(2,1)S(1)}, u32[]{:S(2)}, u32[]{:S(2)}) collective-permute-start(bf16[112,512]{1,0:T(8,128)(2,1)S(1)} %get-tuple-element.32), channel_id=1, source_target_pairs={{0,8},{8,0},{16,24},{24,16},{1,9},{9,1},{17,25},{25,17},{2,10},{10... | collective-permute-start | bytes 344072 | tf_op jit(solution)/shard_map/ppermute | solution.py:283
  22.1 2.8 %collective-permute-start.10 = (bf16[128,512]{1,0:T(8,128)(2,1)S(1)}, bf16[128,512]{1,0:T(8,128)(2,1)S(1)}, u32[]{:S(2)}, u32[]{:S(2)}) collective-permute-start(bf16[128,512]{1,0:T(8,128)(2,1)S(1)} %get-tuple-element.31), channel_id=1, source_target_pairs={{0,8},{8,0},{16,24},{24,16},{1,9},{9,1},{17,25},{25,17},{2,10},{10... | collective-permute-start | bytes 393224 | tf_op jit(solution)/shard_map/ppermute | solution.py:283
  24.2 1.3 %collective-permute-start.12 = (bf16[80,512]{1,0:T(8,128)(2,1)S(1)}, bf16[80,512]{1,0:T(8,128)(2,1)S(1)}, u32[]{:S(2)}, u32[]{:S(2)}) collective-permute-start(bf16[80,512]{1,0:T(8,128)(2,1)S(1)} %get-tuple-element.37), channel_id=1, source_target_pairs={{0,8},{8,0},{16,24},{24,16},{1,9},{9,1},{17,25},{25,17},{2,10},{10... | collective-permute-start | bytes 245768 | tf_op jit(solution)/shard_map/ppermute | solution.py:283
  24.4 1.3 %collective-permute-start.13 = (bf16[80,512]{1,0:T(8,128)(2,1)S(1)}, bf16[80,512]{1,0:T(8,128)(2,1)S(1)}, u32[]{:S(2)}, u32[]{:S(2)}) collective-permute-start(bf16[80,512]{1,0:T(8,128)(2,1)S(1)} %get-tuple-element.38), channel_id=1, source_target_pairs={{0,8},{8,0},{16,24},{24,16},{1,9},{9,1},{17,25},{25,17},{2,10},{10... | collective-permute-start | bytes 245768 | tf_op jit(solution)/shard_map/ppermute | solution.py:283
  24.8 1.3 %collective-permute-start.14 = (bf16[80,512]{1,0:T(8,128)(2,1)S(1)}, bf16[80,512]{1,0:T(8,128)(2,1)S(1)}, u32[]{:S(2)}, u32[]{:S(2)}) collective-permute-start(bf16[80,512]{1,0:T(8,128)(2,1)S(1)} %get-tuple-element.39), channel_id=1, source_target_pairs={{0,8},{8,0},{16,24},{24,16},{1,9},{9,1},{17,25},{25,17},{2,10},{10... | collective-permute-start | bytes 245768 | tf_op jit(solution)/shard_map/ppermute | solution.py:283

commit v8 on v7

--- a/solution.py
+++ b/solution.py
@@ -322,7 +322,7 @@
     slots = features.shape[1]
     whole, halves = embed_tiles(features, tile_counts, projection)
     per = features.shape[0]
-    opposite, across, beside = flip(whole, "dev", 4), flip(whole, "dev", 1), flip(whole, "dev", 2)
+    opposite, across, beside = flip(whole, "dev", 6), flip(whole, "dev", 1), flip(whole, "dev", 2)
     labels, columns = [(0, 0, 0), (0, 1, 0)], [whole, beside]
     bit = groups // 2
     while bit > 1:
@@ -332,7 +332,7 @@
     cut = [2, 2, 2, 3]
     cut = [halves] + [split_block(block, count) for block, count in zip(columns[1:], cut[1:] + [2] * len(columns))]
     swapped = [[flip(part, "grp", 1) for part in cut[n]] for n in range(2)]
-    rows = [(whole, 0), (across, 1), (opposite, 4), (flip(opposite, "dev", 1), 5)]
+    rows = [(whole, 0), (across, 1), (opposite, 6), (flip(opposite, "dev", 1), 7)]
     bit = 8
     while bit < size:
         rows += [(flip(block, "dev", bit), mask ^ bit) for block, mask in rows]

time: 41.3 us -> 41.6 us (level)
  blocking collectives: 11.8 us -> 13.6 us
  waiting for transfers between devices: 9.29 us -> 8.2 us
    all_to_all x1, blocking collectives: 11.8 us -> 13.6 us  [on_device(): lax.all_to_all(results, 'dev', split_axis=0, concat_axis=0, tiled=True)]
    ppermute x15, waiting for transfers between devices: 9.29 us -> 8.2 us  [flip(): lax.ppermute(value, axis, [(i, i ^ mask) for i in range(lax.axis_size(axi...]
  transfers between devices with their start and end apart: 15 -> 15, of which waited for: 7 -> 6; matrix products, arithmetic and copies ran while one was open for 0% -> 0% of each run, Pallas kernels for 6% -> 6%
where the time goes in v8:
time: 41.6 us; the launch traced here: 41.4 us
  blocking collectives  13.6 us (33%)
  starting transfers between devices  13 us (31%)
  waiting for transfers between devices  8.2 us (20%)
  Pallas kernels  5.94 us (14%)
  between operations  0.69 us (2%)
    all_to_all x1, blocking collectives, on_device(): lax.all_to_all(results, 'dev', split_axis=0, concat_axis=0, tiled=True)  13.6 us
    ppermute x15, starting transfers between devices, flip(): lax.ppermute(value, axis, [(i, i ^ mask) for i in range(lax.axis_size(axi...  13 us
    ppermute x15, waiting for transfers between devices, flip(): lax.ppermute(value, axis, [(i, i ^ mask) for i in range(lax.axis_size(axi...  8.2 us
    pallas_call x2, Pallas kernels, first_step(): pl.pallas_call(functools.partial(first_kernel, len(pieces), labels, per,...  2.54 us
    pallas_call x1, Pallas kernels, embed_tiles(): pl.pallas_call(embed_kernel, out_shape=[jax.ShapeDtypeStruct((size, width...  1.73 us
    pallas_call x1, Pallas kernels, finish_step(): pl.pallas_call(functools.partial(finish_kernel, size, groups, len(pieces)...  0.93 us
  transfers between devices with their start and end apart: 15, of which 6 were waited for; matrix products, arithmetic and copies ran while one was open for 0% of the time, Pallas kernels for 6%

profile of v8, /device:TPU:0, one launch (start us, length us, event | category | flops | bytes accessed | tf_op | source)
XLA Modules:
  0.0 41.4 jit_solution(15030197858850138342)
XLA Ops:
  0.6 1.7 %embed.1 = (bf16[240,512]{1,0:T(8,128)(2,1)S(1)}, bf16[128,512]{1,0:T(8,128)(2,1)S(1)}, bf16[112,512]{1,0:T(8,128)(2,1)S(1)}) custom-call(bf16[2,128,768]{2,1,0:T(8,128)(2,1)} %features_in.1, s32[2]{0:T(128)} %counts_in.1, bf16[768,512]{1,0:T(8,128)(2,1)} %projection_in.1), custom_call_target="tpu_custom_call" | custom-call | tf_op jit(solution)/shard_map/embed/pallas_call | solution.py:63
  2.4 3.1 %collective-permute-start.3 = (bf16[240,512]{1,0:T(8,128)(2,1)S(1)}, bf16[240,512]{1,0:T(8,128)(2,1)S(1)}, u32[]{:S(2)}, u32[]{:S(2)}) collective-permute-start(bf16[240,512]{1,0:T(8,128)(2,1)S(1)} %get-tuple-element.24.refs_0_.refs_3_), channel_id=1, source_target_pairs={{0,2},{1,3},{2,0},{3,1},{4,6},{5,7},{6,4},{7,5},{8,10},{9,11},{10,... | collective-permute-start | bytes 737288 | tf_op jit(solution)/shard_map/ppermute | solution.py:283
  5.5 0.0 collective-permute-start.5
  5.5 2.5 %collective-permute-start = (bf16[240,512]{1,0:T(8,128)(2,1)S(1)}, bf16[240,512]{1,0:T(8,128)(2,1)S(1)}, u32[]{:S(2)}, u32[]{:S(2)}) collective-permute-start(bf16[240,512]{1,0:T(8,128)(2,1)S(1)} %get-tuple-element.24.refs_0_.refs_3_), channel_id=1, source_target_pairs={{0,6},{1,7},{2,4},{3,5},{4,2},{5,3},{6,0},{7,1},{8,14},{9,15},{10,... | collective-permute-start | bytes 737288 | tf_op jit(solution)/shard_map/ppermute | solution.py:283
  7.9 1.5 %collective-permute-start.8 = (bf16[240,512]{1,0:T(8,128)(2,1)S(1)}, bf16[240,512]{1,0:T(8,128)(2,1)S(1)}, u32[]{:S(2)}, u32[]{:S(2)}) collective-permute-start(bf16[240,512]{1,0:T(8,128)(2,1)S(1)} %get-tuple-element.24.refs_0_.refs_3_), channel_id=1, source_target_pairs={{0,16},{8,24},{16,0},{24,8},{1,17},{9,25},{17,1},{25,9},{2,18},{10... | collective-permute-start | bytes 737288 | tf_op jit(solution)/shard_map/ppermute | solution.py:283
  9.5 1.5 %collective-permute-start.2 = (bf16[240,512]{1,0:T(8,128)(2,1)S(1)}, bf16[240,512]{1,0:T(8,128)(2,1)S(1)}, u32[]{:S(2)}, u32[]{:S(2)}) collective-permute-start(bf16[240,512]{1,0:T(8,128)(2,1)S(1)} %get-tuple-element.24.refs_0_.refs_3_), channel_id=1, source_target_pairs={{0,1},{1,0},{2,3},{3,2},{4,5},{5,4},{6,7},{7,6},{8,9},{9,8},{10,11... | collective-permute-start | bytes 737288 | tf_op jit(solution)/shard_map/ppermute | solution.py:283
  10.9 0.0 collective-permute-done.5.refs_6_
  10.9 0.0 collective-permute-start.4
  10.9 0.9 %collective-permute-done.3.in_ref.refs_4_ = bf16[240,512]{1,0:T(8,128)(2,1)S(1)} collective-permute-done((bf16[240,512]{1,0:T(8,128)(2,1)S(1)}, bf16[240,512]{1,0:T(8,128)(2,1)S(1)}, u32[]{:S(2)}, u32[]{:S(2)}) %collective-permute-start.3) | collective-permute-done | bytes 245792 | tf_op jit(solution)/shard_map/ppermute | solution.py:283
  11.8 1.5 %collective-permute-start.9 = (bf16[240,512]{1,0:T(8,128)(2,1)S(1)}, bf16[240,512]{1,0:T(8,128)(2,1)S(1)}, u32[]{:S(2)}, u32[]{:S(2)}) collective-permute-start(bf16[240,512]{1,0:T(8,128)(2,1)S(1)} %collective-permute-done.3.in_ref.refs_4_), channel_id=1, source_target_pairs={{0,16},{8,24},{16,0},{24,8},{1,17},{9,25},{17,1},{25,9},{2,18},{10... | collective-permute-start | bytes 737288 | tf_op jit(solution)/shard_map/ppermute | solution.py:283
  13.4 0.0 collective-permute-done.4.refs_5_
  13.4 0.1 collective-permute-start.7
  13.4 5.5 %collective-permute-done.refs_2_ = bf16[240,512]{1,0:T(8,128)(2,1)S(1)} collective-permute-done((bf16[240,512]{1,0:T(8,128)(2,1)S(1)}, bf16[240,512]{1,0:T(8,128)(2,1)S(1)}, u32[]{:S(2)}, u32[]{:S(2)}) %collective-permute-start) | collective-permute-done | bytes 245792 | tf_op jit(solution)/shard_map/ppermute | solution.py:283
  19.0 1.5 %collective-permute-start.1 = (bf16[240,512]{1,0:T(8,128)(2,1)S(1)}, bf16[240,512]{1,0:T(8,128)(2,1)S(1)}, u32[]{:S(2)}, u32[]{:S(2)}) collective-permute-start(bf16[240,512]{1,0:T(8,128)(2,1)S(1)} %collective-permute-done.refs_2_), channel_id=1, source_target_pairs={{0,1},{1,0},{2,3},{3,2},{4,5},{5,4},{6,7},{7,6},{8,9},{9,8},{10,11... | collective-permute-start | bytes 737288 | tf_op jit(solution)/shard_map/ppermute | solution.py:283
  20.5 0.6 %collective-permute-start.11 = (bf16[112,512]{1,0:T(8,128)(2,1)S(1)}, bf16[112,512]{1,0:T(8,128)(2,1)S(1)}, u32[]{:S(2)}, u32[]{:S(2)}) collective-permute-start(bf16[112,512]{1,0:T(8,128)(2,1)S(1)} %get-tuple-element.32), channel_id=1, source_target_pairs={{0,8},{8,0},{16,24},{24,16},{1,9},{9,1},{17,25},{25,17},{2,10},{10... | collective-permute-start | bytes 344072 | tf_op jit(solution)/shard_map/ppermute | solution.py:283
  21.1 0.0 collective-permute-done.7.refs_8_
  21.1 0.1 collective-permute-start.10
  21.2 0.7 %collective-permute-done.6.refs_7_ = bf16[128,512]{1,0:T(8,128)(2,1)S(1)} collective-permute-done((bf16[128,512]{1,0:T(8,128)(2,1)S(1)}, bf16[128,512]{1,0:T(8,128)(2,1)S(1)}, u32[]{:S(2)}, u32[]{:S(2)}) %collective-permute-start.6) | collective-permute-done | bytes 131104 | tf_op jit(solution)/shard_map/ppermute | solution.py:283
  21.8 1.3 %first_scores.2 = (bf16[8,8,16,512]{3,2,1,0:T(8,128)(2,1)S(1)}, f32[8,128]{1,0:T(8,128)S(1)}, f32[6,8,128]{2,1,0:T(8,128)S(1)}) custom-call(bf16[240,512]{1,0:T(8,128)(2,1)S(1)} %get-tuple-element.24.refs_0_.refs_3_, bf16[240,512]{1,0:T(8,128)(2,1)S(1)} %collective-permute-done.2.refs_1_, bf16[240,512]{1,0:T(8,128)(2,1)S(1)} %collective-permute-done.refs_2_, ...), custom_call_target="tpu_custom_call" | custom-call | tf_op jit(solution)/shard_map/first_scores/pallas_call | solution.py:176
  23.1 0.0 collective-permute-done.9.in_ref.refs_4_
  23.1 0.2 collective-permute-start.12
  23.3 0.4 collective-permute-start.13
  23.7 0.0 collective-permute-done.11.refs_6_
  23.7 0.1 collective-permute-start.14
  23.8 0.0 collective-permute-done.10.refs_5_
  23.8 0.6 %collective-permute-done.12.refs_7_ = bf16[80,512]{1,0:T(8,128)(2,1)S(1)} collective-permute-done((bf16[80,512]{1,0:T(8,128)(2,1)S(1)}, bf16[80,512]{1,0:T(8,128)(2,1)S(1)}, u32[]{:S(2)}, u32[]{:S(2)}) %collective-permute-start.12) | collective-permute-done | bytes 81952 | tf_op jit(solution)/shard_map/ppermute | solution.py:283
  24.5 0.2 collective-permute-done.13.refs_8_
  24.6 0.4 collective-permute-done.14.refs_9_
  25.0 1.3 %first_scores.3 = (bf16[8,8,16,512]{3,2,1,0:T(8,128)(2,1)S(1)}, f32[8,128]{1,0:T(8,128)S(1)}, f32[6,8,128]{2,1,0:T(8,128)S(1)}) custom-call(bf16[240,512]{1,0:T(8,128)(2,1)S(1)} %get-tuple-element.24.refs_0_.refs_3_, bf16[240,512]{1,0:T(8,128)(2,1)S(1)} %collective-permute-done.2.refs_1_, bf16[240,512]{1,0:T(8,128)(2,1)S(1)} %collective-permute-done.refs_2_, ...), custom_call_target="tpu_custom_call" | custom-call | tf_op jit(solution)/shard_map/first_scores/pallas_call | solution.py:176
  26.2 0.9 %finish.1 = f32[8,8,4,128]{3,2,1,0:T(4,128)S(1)} custom-call(bf16[240,512]{1,0:T(8,128)(2,1)S(1)} %collective-permute-done.1.refs_0_, bf16[8,8,16,512]{3,2,1,0:T(8,128)(2,1)S(1)} %get-tuple-element.29.refs_1_, f32[8,128]{1,0:T(8,128)S(1)} %get-tuple-element.30.refs_2_, bf16[8,8,16,512]{3,2,1,0:T(8,128)(2,1)S(1)} %get-tuple-element.40.refs_3_, ...), custom_call_target="tpu_custom_call" | custom-call | tf_op jit(solution)/shard_map/finish/pallas_call | solution.py:236
  27.2 13.6 %all_to_all.5.parts = f32[8,8,4,128]{3,2,1,0:T(4,128)S(1)} all-to-all(f32[8,8,4,128]{3,2,1,0:T(4,128)S(1)} %finish.1), channel_id=1, replica_groups=mesh['grp'=4,'dev'=8] {'dev'}, dimensions={0} | all-to-all | bytes 262144 | tf_op jit(solution)/shard_map/all_to_all | solution.py:364
  40.7 0.7 %gather_results.1 = (f32[16,8,128]{2,1,0:T(8,128)}, f32[8,16]{1,0:T(8,128)}) custom-call(f32[8,8,4,128]{3,2,1,0:T(4,128)S(1)} %all_to_all.5.parts), custom_call_target="tpu_custom_call" | custom-call | tf_op jit(solution)/shard_map/gather_results/pallas_call | solution.py:269
  (7 shorter events, 0.1 us)
Async XLA Ops:
  2.4 9.5 %collective-permute-start.3 = (bf16[240,512]{1,0:T(8,128)(2,1)S(1)}, bf16[240,512]{1,0:T(8,128)(2,1)S(1)}, u32[]{:S(2)}, u32[]{:S(2)}) collective-permute-start(bf16[240,512]{1,0:T(8,128)(2,1)S(1)} %get-tuple-element.24.refs_0_.refs_3_), channel_id=1, source_target_pairs={{0,2},{1,3},{2,0},{3,1},{4,6},{5,7},{6,4},{7,5},{8,10},{9,11},{10,... | collective-permute-start | bytes 737288 | tf_op jit(solution)/shard_map/ppermute | solution.py:283
  5.5 5.5 %collective-permute-start.5 = (bf16[112,512]{1,0:T(8,128)(2,1)S(1)}, bf16[112,512]{1,0:T(8,128)(2,1)S(1)}, u32[]{:S(2)}, u32[]{:S(2)}) collective-permute-start(bf16[112,512]{1,0:T(8,128)(2,1)S(1)} %get-tuple-element.26), channel_id=1, source_target_pairs={{0,8},{8,0},{16,24},{24,16},{1,9},{9,1},{17,25},{25,17},{2,10},{10... | collective-permute-start | bytes 344072 | tf_op jit(solution)/shard_map/ppermute | solution.py:283
  5.5 13.5 %collective-permute-start = (bf16[240,512]{1,0:T(8,128)(2,1)S(1)}, bf16[240,512]{1,0:T(8,128)(2,1)S(1)}, u32[]{:S(2)}, u32[]{:S(2)}) collective-permute-start(bf16[240,512]{1,0:T(8,128)(2,1)S(1)} %get-tuple-element.24.refs_0_.refs_3_), channel_id=1, source_target_pairs={{0,6},{1,7},{2,4},{3,5},{4,2},{5,3},{6,0},{7,1},{8,14},{9,15},{10,... | collective-permute-start | bytes 737288 | tf_op jit(solution)/shard_map/ppermute | solution.py:283
  7.9 12.5 %collective-permute-start.8 = (bf16[240,512]{1,0:T(8,128)(2,1)S(1)}, bf16[240,512]{1,0:T(8,128)(2,1)S(1)}, u32[]{:S(2)}, u32[]{:S(2)}) collective-permute-start(bf16[240,512]{1,0:T(8,128)(2,1)S(1)} %get-tuple-element.24.refs_0_.refs_3_), channel_id=1, source_target_pairs={{0,16},{8,24},{16,0},{24,8},{1,17},{9,25},{17,1},{25,9},{2,18},{10... | collective-permute-start | bytes 737288 | tf_op jit(solution)/shard_map/ppermute | solution.py:283
  9.5 11.0 %collective-permute-start.2 = (bf16[240,512]{1,0:T(8,128)(2,1)S(1)}, bf16[240,512]{1,0:T(8,128)(2,1)S(1)}, u32[]{:S(2)}, u32[]{:S(2)}) collective-permute-start(bf16[240,512]{1,0:T(8,128)(2,1)S(1)} %get-tuple-element.24.refs_0_.refs_3_), channel_id=1, source_target_pairs={{0,1},{1,0},{2,3},{3,2},{4,5},{5,4},{6,7},{7,6},{8,9},{9,8},{10,11... | collective-permute-start | bytes 737288 | tf_op jit(solution)/shard_map/ppermute | solution.py:283
  10.9 2.4 %collective-permute-start.4 = (bf16[128,512]{1,0:T(8,128)(2,1)S(1)}, bf16[128,512]{1,0:T(8,128)(2,1)S(1)}, u32[]{:S(2)}, u32[]{:S(2)}) collective-permute-start(bf16[128,512]{1,0:T(8,128)(2,1)S(1)} %get-tuple-element.25), channel_id=1, source_target_pairs={{0,8},{8,0},{16,24},{24,16},{1,9},{9,1},{17,25},{25,17},{2,10},{10... | collective-permute-start | bytes 393224 | tf_op jit(solution)/shard_map/ppermute | solution.py:283
  11.8 11.3 %collective-permute-start.9 = (bf16[240,512]{1,0:T(8,128)(2,1)S(1)}, bf16[240,512]{1,0:T(8,128)(2,1)S(1)}, u32[]{:S(2)}, u32[]{:S(2)}) collective-permute-start(bf16[240,512]{1,0:T(8,128)(2,1)S(1)} %collective-permute-done.3.in_ref.refs_4_), channel_id=1, source_target_pairs={{0,16},{8,24},{16,0},{24,8},{1,17},{9,25},{17,1},{25,9},{2,18},{10... | collective-permute-start | bytes 737288 | tf_op jit(solution)/shard_map/ppermute | solution.py:283
  13.4 7.7 %collective-permute-start.7 = (bf16[112,512]{1,0:T(8,128)(2,1)S(1)}, bf16[112,512]{1,0:T(8,128)(2,1)S(1)}, u32[]{:S(2)}, u32[]{:S(2)}) collective-permute-start(bf16[112,512]{1,0:T(8,128)(2,1)S(1)} %get-tuple-element.28), channel_id=1, source_target_pairs={{0,8},{8,0},{16,24},{24,16},{1,9},{9,1},{17,25},{25,17},{2,10},{10... | collective-permute-start | bytes 344072 | tf_op jit(solution)/shard_map/ppermute | solution.py:283
  19.0 7.3 %collective-permute-start.1 = (bf16[240,512]{1,0:T(8,128)(2,1)S(1)}, bf16[240,512]{1,0:T(8,128)(2,1)S(1)}, u32[]{:S(2)}, u32[]{:S(2)}) collective-permute-start(bf16[240,512]{1,0:T(8,128)(2,1)S(1)} %collective-permute-done.refs_2_), channel_id=1, source_target_pairs={{0,1},{1,0},{2,3},{3,2},{4,5},{5,4},{6,7},{7,6},{8,9},{9,8},{10,11... | collective-permute-start | bytes 737288 | tf_op jit(solution)/shard_map/ppermute | solution.py:283
  20.5 1.3 %collective-permute-start.6 = (bf16[128,512]{1,0:T(8,128)(2,1)S(1)}, bf16[128,512]{1,0:T(8,128)(2,1)S(1)}, u32[]{:S(2)}, u32[]{:S(2)}) collective-permute-start(bf16[128,512]{1,0:T(8,128)(2,1)S(1)} %get-tuple-element.27), channel_id=1, source_target_pairs={{0,8},{8,0},{16,24},{24,16},{1,9},{9,1},{17,25},{25,17},{2,10},{10... | collective-permute-start | bytes 393224 | tf_op jit(solution)/shard_map/ppermute | solution.py:283
  20.5 3.2 %collective-permute-start.11 = (bf16[112,512]{1,0:T(8,128)(2,1)S(1)}, bf16[112,512]{1,0:T(8,128)(2,1)S(1)}, u32[]{:S(2)}, u32[]{:S(2)}) collective-permute-start(bf16[112,512]{1,0:T(8,128)(2,1)S(1)} %get-tuple-element.32), channel_id=1, source_target_pairs={{0,8},{8,0},{16,24},{24,16},{1,9},{9,1},{17,25},{25,17},{2,10},{10... | collective-permute-start | bytes 344072 | tf_op jit(solution)/shard_map/ppermute | solution.py:283
  21.1 2.8 %collective-permute-start.10 = (bf16[128,512]{1,0:T(8,128)(2,1)S(1)}, bf16[128,512]{1,0:T(8,128)(2,1)S(1)}, u32[]{:S(2)}, u32[]{:S(2)}) collective-permute-start(bf16[128,512]{1,0:T(8,128)(2,1)S(1)} %get-tuple-element.31), channel_id=1, source_target_pairs={{0,8},{8,0},{16,24},{24,16},{1,9},{9,1},{17,25},{25,17},{2,10},{10... | collective-permute-start | bytes 393224 | tf_op jit(solution)/shard_map/ppermute | solution.py:283
  23.1 1.3 %collective-permute-start.12 = (bf16[80,512]{1,0:T(8,128)(2,1)S(1)}, bf16[80,512]{1,0:T(8,128)(2,1)S(1)}, u32[]{:S(2)}, u32[]{:S(2)}) collective-permute-start(bf16[80,512]{1,0:T(8,128)(2,1)S(1)} %get-tuple-element.37), channel_id=1, source_target_pairs={{0,8},{8,0},{16,24},{24,16},{1,9},{9,1},{17,25},{25,17},{2,10},{10... | collective-permute-start | bytes 245768 | tf_op jit(solution)/shard_map/ppermute | solution.py:283
  23.3 1.3 %collective-permute-start.13 = (bf16[80,512]{1,0:T(8,128)(2,1)S(1)}, bf16[80,512]{1,0:T(8,128)(2,1)S(1)}, u32[]{:S(2)}, u32[]{:S(2)}) collective-permute-start(bf16[80,512]{1,0:T(8,128)(2,1)S(1)} %get-tuple-element.38), channel_id=1, source_target_pairs={{0,8},{8,0},{16,24},{24,16},{1,9},{9,1},{17,25},{25,17},{2,10},{10... | collective-permute-start | bytes 245768 | tf_op jit(solution)/shard_map/ppermute | solution.py:283
  23.7 1.3 %collective-permute-start.14 = (bf16[80,512]{1,0:T(8,128)(2,1)S(1)}, bf16[80,512]{1,0:T(8,128)(2,1)S(1)}, u32[]{:S(2)}, u32[]{:S(2)}) collective-permute-start(bf16[80,512]{1,0:T(8,128)(2,1)S(1)} %get-tuple-element.39), channel_id=1, source_target_pairs={{0,8},{8,0},{16,24},{24,16},{1,9},{9,1},{17,25},{25,17},{2,10},{10... | collective-permute-start | bytes 245768 | tf_op jit(solution)/shard_map/ppermute | solution.py:283

commit v9 on v7

--- a/solution.py
+++ b/solution.py
@@ -13,6 +13,7 @@
 MAIN = USED - TAIL
 MARK = 128.0
 LANES = 128
+PIECE = 256
 VMEM_LIMIT = 40 * 1024 * 1024
 NT = (((1,), (1,)), ((), ()))
 VMEM = pl.BlockSpec(memory_space=pltpu.VMEM)
@@ -27,18 +28,26 @@
 
 def embed_kernel(features_in, counts_in, projection_in, *refs):
     (out_ref, *part_refs), (features_ref, counts_ref, projection_ref, sems) = refs[:-4], refs[-4:]
-    copies = [
-        pltpu.make_async_copy(projection_in, projection_ref, sems.at[0]),
-        pltpu.make_async_copy(features_in, features_ref, sems.at[1]),
-        pltpu.make_async_copy(counts_in, counts_ref, sems.at[2]),
+    slides, slots, depth = features_ref.shape
+    pieces = [pl.ds(start, PIECE) for start in range(0, depth, PIECE)]
+    first = [
+        pltpu.make_async_copy(features_in, features_ref, sems.at[0]),
+        pltpu.make_async_copy(counts_in, counts_ref, sems.at[1]),
     ]
-    for copy in copies:
+    loads = [
+        pltpu.make_async_copy(projection_in.at[piece], projection_ref.at[piece], sems.at[2 + n])
+        for n, piece in enumerate(pieces)
+    ]
+    for copy in first + loads:
         copy.start()
-    for copy in copies:
+    for copy in first:
         copy.wait()
-    slides, slots, depth = features_ref.shape
     tiles = features_ref[...].reshape(slides * slots, depth)
-    every = jnp.dot(tiles, projection_ref[...], preferred_element_type=jnp.float32)
+    every = jnp.zeros((slides * slots, projection_ref.shape[1]), jnp.float32)
+    for n, piece in enumerate(pieces):
+        loads[n].wait()
+        part = tiles[:, n * PIECE : (n + 1) * PIECE]
+        every = every + jnp.dot(part, projection_ref[piece, :], preferred_element_type=jnp.float32)
     tails = []
     for s in range(slides):
         raw = every[s * slots : (s + 1) * slots]
@@ -69,7 +78,7 @@
             pltpu.VMEM(features.shape, features.dtype),
             pltpu.SMEM(tile_counts.shape, tile_counts.dtype),
             pltpu.VMEM(projection.shape, projection.dtype),
-            pltpu.SemaphoreType.DMA((3,)),
+            pltpu.SemaphoreType.DMA((2 + projection.shape[0] // PIECE,)),
         ],
         compiler_params=PARAMS,
         name="embed",

time: 41.3 us -> 41.2 us (level)
  no operation moved by 1% of the time
where the time goes in v9:
time: 41.2 us; the launch traced here: 41 us
  starting transfers between devices  13.3 us (32%)
  blocking collectives  11.8 us (29%)
  waiting for transfers between devices  9.28 us (23%)
  Pallas kernels  5.91 us (14%)
  between operations  0.69 us (2%)
    ppermute x15, starting transfers between devices, flip(): lax.ppermute(value, axis, [(i, i ^ mask) for i in range(lax.axis_size(axi...  13.3 us
    all_to_all x1, blocking collectives, on_device(): lax.all_to_all(results, 'dev', split_axis=0, concat_axis=0, tiled=True)  11.8 us
    ppermute x15, waiting for transfers between devices, flip(): lax.ppermute(value, axis, [(i, i ^ mask) for i in range(lax.axis_size(axi...  9.28 us
    pallas_call x2, Pallas kernels, first_step(): pl.pallas_call(functools.partial(first_kernel, len(pieces), labels, per,...  2.54 us
    pallas_call x1, Pallas kernels, embed_tiles(): pl.pallas_call(embed_kernel, out_shape=[jax.ShapeDtypeStruct((size, width...  1.7 us
    pallas_call x1, Pallas kernels, finish_step(): pl.pallas_call(functools.partial(finish_kernel, size, groups, len(pieces)...  0.92 us
  transfers between devices with their start and end apart: 15, of which 7 were waited for; matrix products, arithmetic and copies ran while one was open for 0% of the time, Pallas kernels for 6%

profile of v9, /device:TPU:0, one launch (start us, length us, event | category | flops | bytes accessed | tf_op | source)
XLA Modules:
  0.0 41.0 jit_solution(13701049652895487908)
XLA Ops:
  0.6 1.7 %embed.1 = (bf16[240,512]{1,0:T(8,128)(2,1)S(1)}, bf16[128,512]{1,0:T(8,128)(2,1)S(1)}, bf16[112,512]{1,0:T(8,128)(2,1)S(1)}) custom-call(bf16[2,128,768]{2,1,0:T(8,128)(2,1)} %features_in.1, s32[2]{0:T(128)} %counts_in.1, bf16[768,512]{1,0:T(8,128)(2,1)} %projection_in.1), custom_call_target="tpu_custom_call" | custom-call | tf_op jit(solution)/shard_map/embed/pallas_call | solution.py:72
  2.3 3.1 %collective-permute-start.3 = (bf16[240,512]{1,0:T(8,128)(2,1)S(1)}, bf16[240,512]{1,0:T(8,128)(2,1)S(1)}, u32[]{:S(2)}, u32[]{:S(2)}) collective-permute-start(bf16[240,512]{1,0:T(8,128)(2,1)S(1)} %get-tuple-element.24.refs_0_.refs_3_), channel_id=1, source_target_pairs={{0,2},{1,3},{2,0},{3,1},{4,6},{5,7},{6,4},{7,5},{8,10},{9,11},{10,... | collective-permute-start | bytes 737288 | tf_op jit(solution)/shard_map/ppermute | solution.py:292
  5.4 0.0 collective-permute-start.5
  5.4 2.6 %collective-permute-start = (bf16[240,512]{1,0:T(8,128)(2,1)S(1)}, bf16[240,512]{1,0:T(8,128)(2,1)S(1)}, u32[]{:S(2)}, u32[]{:S(2)}) collective-permute-start(bf16[240,512]{1,0:T(8,128)(2,1)S(1)} %get-tuple-element.24.refs_0_.refs_3_), channel_id=1, source_target_pairs={{0,4},{1,5},{2,6},{3,7},{4,0},{5,1},{6,2},{7,3},{8,12},{9,13},{10,... | collective-permute-start | bytes 737288 | tf_op jit(solution)/shard_map/ppermute | solution.py:292
  8.0 1.5 %collective-permute-start.8 = (bf16[240,512]{1,0:T(8,128)(2,1)S(1)}, bf16[240,512]{1,0:T(8,128)(2,1)S(1)}, u32[]{:S(2)}, u32[]{:S(2)}) collective-permute-start(bf16[240,512]{1,0:T(8,128)(2,1)S(1)} %get-tuple-element.24.refs_0_.refs_3_), channel_id=1, source_target_pairs={{0,16},{8,24},{16,0},{24,8},{1,17},{9,25},{17,1},{25,9},{2,18},{10... | collective-permute-start | bytes 737288 | tf_op jit(solution)/shard_map/ppermute | solution.py:292
  9.5 1.5 %collective-permute-start.2 = (bf16[240,512]{1,0:T(8,128)(2,1)S(1)}, bf16[240,512]{1,0:T(8,128)(2,1)S(1)}, u32[]{:S(2)}, u32[]{:S(2)}) collective-permute-start(bf16[240,512]{1,0:T(8,128)(2,1)S(1)} %get-tuple-element.24.refs_0_.refs_3_), channel_id=1, source_target_pairs={{0,1},{1,0},{2,3},{3,2},{4,5},{5,4},{6,7},{7,6},{8,9},{9,8},{10,11... | collective-permute-start | bytes 737288 | tf_op jit(solution)/shard_map/ppermute | solution.py:292
  11.0 0.0 collective-permute-done.5.refs_6_
  11.0 4.5 %collective-permute-done.3.in_ref.refs_4_ = bf16[240,512]{1,0:T(8,128)(2,1)S(1)} collective-permute-done((bf16[240,512]{1,0:T(8,128)(2,1)S(1)}, bf16[240,512]{1,0:T(8,128)(2,1)S(1)}, u32[]{:S(2)}, u32[]{:S(2)}) %collective-permute-start.3) | collective-permute-done | bytes 245792 | tf_op jit(solution)/shard_map/ppermute | solution.py:292
  15.6 1.7 %collective-permute-start.9 = (bf16[240,512]{1,0:T(8,128)(2,1)S(1)}, bf16[240,512]{1,0:T(8,128)(2,1)S(1)}, u32[]{:S(2)}, u32[]{:S(2)}) collective-permute-start(bf16[240,512]{1,0:T(8,128)(2,1)S(1)} %collective-permute-done.3.in_ref.refs_4_), channel_id=1, source_target_pairs={{0,16},{8,24},{16,0},{24,8},{1,17},{9,25},{17,1},{25,9},{2,18},{10... | collective-permute-start | bytes 737288 | tf_op jit(solution)/shard_map/ppermute | solution.py:292
  17.3 0.0 collective-permute-done.4.refs_5_
  17.3 0.1 collective-permute-start.7
  17.4 2.6 %collective-permute-done.refs_2_ = bf16[240,512]{1,0:T(8,128)(2,1)S(1)} collective-permute-done((bf16[240,512]{1,0:T(8,128)(2,1)S(1)}, bf16[240,512]{1,0:T(8,128)(2,1)S(1)}, u32[]{:S(2)}, u32[]{:S(2)}) %collective-permute-start) | collective-permute-done | bytes 245792 | tf_op jit(solution)/shard_map/ppermute | solution.py:292
  20.0 1.5 %collective-permute-start.1 = (bf16[240,512]{1,0:T(8,128)(2,1)S(1)}, bf16[240,512]{1,0:T(8,128)(2,1)S(1)}, u32[]{:S(2)}, u32[]{:S(2)}) collective-permute-start(bf16[240,512]{1,0:T(8,128)(2,1)S(1)} %collective-permute-done.refs_2_), channel_id=1, source_target_pairs={{0,1},{1,0},{2,3},{3,2},{4,5},{5,4},{6,7},{7,6},{8,9},{9,8},{10,11... | collective-permute-start | bytes 737288 | tf_op jit(solution)/shard_map/ppermute | solution.py:292
  21.5 0.0 collective-permute-done.8.in_ref.refs_3_
  21.5 0.6 %collective-permute-start.11 = (bf16[112,512]{1,0:T(8,128)(2,1)S(1)}, bf16[112,512]{1,0:T(8,128)(2,1)S(1)}, u32[]{:S(2)}, u32[]{:S(2)}) collective-permute-start(bf16[112,512]{1,0:T(8,128)(2,1)S(1)} %get-tuple-element.32), channel_id=1, source_target_pairs={{0,8},{8,0},{16,24},{24,16},{1,9},{9,1},{17,25},{25,17},{2,10},{10... | collective-permute-start | bytes 344072 | tf_op jit(solution)/shard_map/ppermute | solution.py:292
  22.1 0.0 collective-permute-done.7.refs_8_
  22.1 0.1 collective-permute-start.10
  22.2 0.7 %collective-permute-done.6.refs_7_ = bf16[128,512]{1,0:T(8,128)(2,1)S(1)} collective-permute-done((bf16[128,512]{1,0:T(8,128)(2,1)S(1)}, bf16[128,512]{1,0:T(8,128)(2,1)S(1)}, u32[]{:S(2)}, u32[]{:S(2)}) %collective-permute-start.6) | collective-permute-done | bytes 131104 | tf_op jit(solution)/shard_map/ppermute | solution.py:292
  22.9 1.3 %first_scores.2 = (bf16[8,8,16,512]{3,2,1,0:T(8,128)(2,1)S(1)}, f32[8,128]{1,0:T(8,128)S(1)}, f32[6,8,128]{2,1,0:T(8,128)S(1)}) custom-call(bf16[240,512]{1,0:T(8,128)(2,1)S(1)} %get-tuple-element.24.refs_0_.refs_3_, bf16[240,512]{1,0:T(8,128)(2,1)S(1)} %collective-permute-done.2.refs_1_, bf16[240,512]{1,0:T(8,128)(2,1)S(1)} %collective-permute-done.refs_2_, ...), custom_call_target="tpu_custom_call" | custom-call | tf_op jit(solution)/shard_map/first_scores/pallas_call | solution.py:185
  24.1 0.0 collective-permute-done.9.in_ref.refs_4_
  24.2 0.2 collective-permute-start.12
  24.4 0.4 collective-permute-start.13
  24.7 0.0 collective-permute-done.11.refs_6_
  24.7 0.1 collective-permute-start.14
  24.9 0.6 %collective-permute-done.12.refs_7_ = bf16[80,512]{1,0:T(8,128)(2,1)S(1)} collective-permute-done((bf16[80,512]{1,0:T(8,128)(2,1)S(1)}, bf16[80,512]{1,0:T(8,128)(2,1)S(1)}, u32[]{:S(2)}, u32[]{:S(2)}) %collective-permute-start.12) | collective-permute-done | bytes 81952 | tf_op jit(solution)/shard_map/ppermute | solution.py:292
  25.5 0.2 collective-permute-done.13.refs_8_
  25.7 0.4 collective-permute-done.14.refs_9_
  26.0 1.3 %first_scores.3 = (bf16[8,8,16,512]{3,2,1,0:T(8,128)(2,1)S(1)}, f32[8,128]{1,0:T(8,128)S(1)}, f32[6,8,128]{2,1,0:T(8,128)S(1)}) custom-call(bf16[240,512]{1,0:T(8,128)(2,1)S(1)} %get-tuple-element.24.refs_0_.refs_3_, bf16[240,512]{1,0:T(8,128)(2,1)S(1)} %collective-permute-done.2.refs_1_, bf16[240,512]{1,0:T(8,128)(2,1)S(1)} %collective-permute-done.refs_2_, ...), custom_call_target="tpu_custom_call" | custom-call | tf_op jit(solution)/shard_map/first_scores/pallas_call | solution.py:185
  27.3 0.3 collective-permute-done.1.refs_0_
  27.6 0.9 %finish.1 = f32[8,8,4,128]{3,2,1,0:T(4,128)S(1)} custom-call(bf16[240,512]{1,0:T(8,128)(2,1)S(1)} %collective-permute-done.1.refs_0_, bf16[8,8,16,512]{3,2,1,0:T(8,128)(2,1)S(1)} %get-tuple-element.29.refs_1_, f32[8,128]{1,0:T(8,128)S(1)} %get-tuple-element.30.refs_2_, bf16[8,8,16,512]{3,2,1,0:T(8,128)(2,1)S(1)} %get-tuple-element.40.refs_3_, ...), custom_call_target="tpu_custom_call" | custom-call | tf_op jit(solution)/shard_map/finish/pallas_call | solution.py:245
  28.5 11.8 %all_to_all.5.parts = f32[8,8,4,128]{3,2,1,0:T(4,128)S(1)} all-to-all(f32[8,8,4,128]{3,2,1,0:T(4,128)S(1)} %finish.1), channel_id=1, replica_groups=mesh['grp'=4,'dev'=8] {'dev'}, dimensions={0} | all-to-all | bytes 262144 | tf_op jit(solution)/shard_map/all_to_all | solution.py:373
  40.3 0.7 %gather_results.1 = (f32[16,8,128]{2,1,0:T(8,128)}, f32[8,16]{1,0:T(8,128)}) custom-call(f32[8,8,4,128]{3,2,1,0:T(4,128)S(1)} %all_to_all.5.parts), custom_call_target="tpu_custom_call" | custom-call | tf_op jit(solution)/shard_map/gather_results/pallas_call | solution.py:278
  (7 shorter events, 0.1 us)
Async XLA Ops:
  2.3 13.2 %collective-permute-start.3 = (bf16[240,512]{1,0:T(8,128)(2,1)S(1)}, bf16[240,512]{1,0:T(8,128)(2,1)S(1)}, u32[]{:S(2)}, u32[]{:S(2)}) collective-permute-start(bf16[240,512]{1,0:T(8,128)(2,1)S(1)} %get-tuple-element.24.refs_0_.refs_3_), channel_id=1, source_target_pairs={{0,2},{1,3},{2,0},{3,1},{4,6},{5,7},{6,4},{7,5},{8,10},{9,11},{10,... | collective-permute-start | bytes 737288 | tf_op jit(solution)/shard_map/ppermute | solution.py:292
  5.4 5.6 %collective-permute-start.5 = (bf16[112,512]{1,0:T(8,128)(2,1)S(1)}, bf16[112,512]{1,0:T(8,128)(2,1)S(1)}, u32[]{:S(2)}, u32[]{:S(2)}) collective-permute-start(bf16[112,512]{1,0:T(8,128)(2,1)S(1)} %get-tuple-element.26), channel_id=1, source_target_pairs={{0,8},{8,0},{16,24},{24,16},{1,9},{9,1},{17,25},{25,17},{2,10},{10... | collective-permute-start | bytes 344072 | tf_op jit(solution)/shard_map/ppermute | solution.py:292
  5.4 14.6 %collective-permute-start = (bf16[240,512]{1,0:T(8,128)(2,1)S(1)}, bf16[240,512]{1,0:T(8,128)(2,1)S(1)}, u32[]{:S(2)}, u32[]{:S(2)}) collective-permute-start(bf16[240,512]{1,0:T(8,128)(2,1)S(1)} %get-tuple-element.24.refs_0_.refs_3_), channel_id=1, source_target_pairs={{0,4},{1,5},{2,6},{3,7},{4,0},{5,1},{6,2},{7,3},{8,12},{9,13},{10,... | collective-permute-start | bytes 737288 | tf_op jit(solution)/shard_map/ppermute | solution.py:292
  8.0 13.5 %collective-permute-start.8 = (bf16[240,512]{1,0:T(8,128)(2,1)S(1)}, bf16[240,512]{1,0:T(8,128)(2,1)S(1)}, u32[]{:S(2)}, u32[]{:S(2)}) collective-permute-start(bf16[240,512]{1,0:T(8,128)(2,1)S(1)} %get-tuple-element.24.refs_0_.refs_3_), channel_id=1, source_target_pairs={{0,16},{8,24},{16,0},{24,8},{1,17},{9,25},{17,1},{25,9},{2,18},{10... | collective-permute-start | bytes 737288 | tf_op jit(solution)/shard_map/ppermute | solution.py:292
  9.5 12.0 %collective-permute-start.2 = (bf16[240,512]{1,0:T(8,128)(2,1)S(1)}, bf16[240,512]{1,0:T(8,128)(2,1)S(1)}, u32[]{:S(2)}, u32[]{:S(2)}) collective-permute-start(bf16[240,512]{1,0:T(8,128)(2,1)S(1)} %get-tuple-element.24.refs_0_.refs_3_), channel_id=1, source_target_pairs={{0,1},{1,0},{2,3},{3,2},{4,5},{5,4},{6,7},{7,6},{8,9},{9,8},{10,11... | collective-permute-start | bytes 737288 | tf_op jit(solution)/shard_map/ppermute | solution.py:292
  11.0 6.2 %collective-permute-start.4 = (bf16[128,512]{1,0:T(8,128)(2,1)S(1)}, bf16[128,512]{1,0:T(8,128)(2,1)S(1)}, u32[]{:S(2)}, u32[]{:S(2)}) collective-permute-start(bf16[128,512]{1,0:T(8,128)(2,1)S(1)} %get-tuple-element.25), channel_id=1, source_target_pairs={{0,8},{8,0},{16,24},{24,16},{1,9},{9,1},{17,25},{25,17},{2,10},{10... | collective-permute-start | bytes 393224 | tf_op jit(solution)/shard_map/ppermute | solution.py:292
  15.6 8.6 %collective-permute-start.9 = (bf16[240,512]{1,0:T(8,128)(2,1)S(1)}, bf16[240,512]{1,0:T(8,128)(2,1)S(1)}, u32[]{:S(2)}, u32[]{:S(2)}) collective-permute-start(bf16[240,512]{1,0:T(8,128)(2,1)S(1)} %collective-permute-done.3.in_ref.refs_4_), channel_id=1, source_target_pairs={{0,16},{8,24},{16,0},{24,8},{1,17},{9,25},{17,1},{25,9},{2,18},{10... | collective-permute-start | bytes 737288 | tf_op jit(solution)/shard_map/ppermute | solution.py:292
  17.3 4.8 %collective-permute-start.7 = (bf16[112,512]{1,0:T(8,128)(2,1)S(1)}, bf16[112,512]{1,0:T(8,128)(2,1)S(1)}, u32[]{:S(2)}, u32[]{:S(2)}) collective-permute-start(bf16[112,512]{1,0:T(8,128)(2,1)S(1)} %get-tuple-element.28), channel_id=1, source_target_pairs={{0,8},{8,0},{16,24},{24,16},{1,9},{9,1},{17,25},{25,17},{2,10},{10... | collective-permute-start | bytes 344072 | tf_op jit(solution)/shard_map/ppermute | solution.py:292
  20.0 7.6 %collective-permute-start.1 = (bf16[240,512]{1,0:T(8,128)(2,1)S(1)}, bf16[240,512]{1,0:T(8,128)(2,1)S(1)}, u32[]{:S(2)}, u32[]{:S(2)}) collective-permute-start(bf16[240,512]{1,0:T(8,128)(2,1)S(1)} %collective-permute-done.refs_2_), channel_id=1, source_target_pairs={{0,1},{1,0},{2,3},{3,2},{4,5},{5,4},{6,7},{7,6},{8,9},{9,8},{10,11... | collective-permute-start | bytes 737288 | tf_op jit(solution)/shard_map/ppermute | solution.py:292
  21.5 1.3 %collective-permute-start.6 = (bf16[128,512]{1,0:T(8,128)(2,1)S(1)}, bf16[128,512]{1,0:T(8,128)(2,1)S(1)}, u32[]{:S(2)}, u32[]{:S(2)}) collective-permute-start(bf16[128,512]{1,0:T(8,128)(2,1)S(1)} %get-tuple-element.27), channel_id=1, source_target_pairs={{0,8},{8,0},{16,24},{24,16},{1,9},{9,1},{17,25},{25,17},{2,10},{10... | collective-permute-start | bytes 393224 | tf_op jit(solution)/shard_map/ppermute | solution.py:292
  21.5 3.2 %collective-permute-start.11 = (bf16[112,512]{1,0:T(8,128)(2,1)S(1)}, bf16[112,512]{1,0:T(8,128)(2,1)S(1)}, u32[]{:S(2)}, u32[]{:S(2)}) collective-permute-start(bf16[112,512]{1,0:T(8,128)(2,1)S(1)} %get-tuple-element.32), channel_id=1, source_target_pairs={{0,8},{8,0},{16,24},{24,16},{1,9},{9,1},{17,25},{25,17},{2,10},{10... | collective-permute-start | bytes 344072 | tf_op jit(solution)/shard_map/ppermute | solution.py:292
  22.1 2.8 %collective-permute-start.10 = (bf16[128,512]{1,0:T(8,128)(2,1)S(1)}, bf16[128,512]{1,0:T(8,128)(2,1)S(1)}, u32[]{:S(2)}, u32[]{:S(2)}) collective-permute-start(bf16[128,512]{1,0:T(8,128)(2,1)S(1)} %get-tuple-element.31), channel_id=1, source_target_pairs={{0,8},{8,0},{16,24},{24,16},{1,9},{9,1},{17,25},{25,17},{2,10},{10... | collective-permute-start | bytes 393224 | tf_op jit(solution)/shard_map/ppermute | solution.py:292
  24.2 1.3 %collective-permute-start.12 = (bf16[80,512]{1,0:T(8,128)(2,1)S(1)}, bf16[80,512]{1,0:T(8,128)(2,1)S(1)}, u32[]{:S(2)}, u32[]{:S(2)}) collective-permute-start(bf16[80,512]{1,0:T(8,128)(2,1)S(1)} %get-tuple-element.37), channel_id=1, source_target_pairs={{0,8},{8,0},{16,24},{24,16},{1,9},{9,1},{17,25},{25,17},{2,10},{10... | collective-permute-start | bytes 245768 | tf_op jit(solution)/shard_map/ppermute | solution.py:292
  24.4 1.3 %collective-permute-start.13 = (bf16[80,512]{1,0:T(8,128)(2,1)S(1)}, bf16[80,512]{1,0:T(8,128)(2,1)S(1)}, u32[]{:S(2)}, u32[]{:S(2)}) collective-permute-start(bf16[80,512]{1,0:T(8,128)(2,1)S(1)} %get-tuple-element.38), channel_id=1, source_target_pairs={{0,8},{8,0},{16,24},{24,16},{1,9},{9,1},{17,25},{25,17},{2,10},{10... | collective-permute-start | bytes 245768 | tf_op jit(solution)/shard_map/ppermute | solution.py:292
  24.7 1.3 %collective-permute-start.14 = (bf16[80,512]{1,0:T(8,128)(2,1)S(1)}, bf16[80,512]{1,0:T(8,128)(2,1)S(1)}, u32[]{:S(2)}, u32[]{:S(2)}) collective-permute-start(bf16[80,512]{1,0:T(8,128)(2,1)S(1)} %get-tuple-element.39), channel_id=1, source_target_pairs={{0,8},{8,0},{16,24},{24,16},{1,9},{9,1},{17,25},{25,17},{2,10},{10... | collective-permute-start | bytes 245768 | tf_op jit(solution)/shard_map/ppermute | solution.py:292

commit v10 on v7

--- a/solution.py
+++ b/solution.py
@@ -330,7 +330,7 @@
         labels += [(mask ^ bit, pair, 0) for mask, pair, _ in labels]
         bit //= 2
     cut = [2, 2, 2, 3]
-    cut = [halves] + [split_block(block, count) for block, count in zip(columns[1:], cut[1:] + [2] * len(columns))]
+    cut = [[whole]] + [split_block(block, count) for block, count in zip(columns[1:], cut[1:] + [2] * len(columns))]
     swapped = [[flip(part, "grp", 1) for part in cut[n]] for n in range(2)]
     rows = [(whole, 0), (across, 1), (opposite, 4), (flip(opposite, "dev", 1), 5)]
     bit = 8

time: 41.3 us -> 41.8 us (1.012)
  Pallas kernels: 5.93 us -> 6.58 us
    pallas_call x1, Pallas kernels: 1.73 us -> 2.38 us  [embed_tiles(): pl.pallas_call(embed_kernel, out_shape=[jax.ShapeDtypeStruct((size, width...]
    ppermute x15 -> x14, waiting for transfers between devices: 9.29 us -> 9.15 us  [flip(): lax.ppermute(value, axis, [(i, i ^ mask) for i in range(lax.axis_size(axi...]
    ppermute x15 -> x14, starting transfers between devices: 13.3 us -> 13.3 us  [flip(): lax.ppermute(value, axis, [(i, i ^ mask) for i in range(lax.axis_size(axi...]
  transfers between devices with their start and end apart: 15 -> 14, of which waited for: 7 -> 8; matrix products, arithmetic and copies ran while one was open for 0% -> 0% of each run, Pallas kernels for 6% -> 6%
where the time goes in v10:
time: 41.8 us; the launch traced here: 41.6 us
  starting transfers between devices  13.3 us (32%)
  blocking collectives  11.8 us (28%)
  waiting for transfers between devices  9.15 us (22%)
  Pallas kernels  6.58 us (16%)
  between operations  0.68 us (2%)
    ppermute x14, starting transfers between devices, flip(): lax.ppermute(value, axis, [(i, i ^ mask) for i in range(lax.axis_size(axi...  13.3 us
    all_to_all x1, blocking collectives, on_device(): lax.all_to_all(results, 'dev', split_axis=0, concat_axis=0, tiled=True)  11.8 us
    ppermute x14, waiting for transfers between devices, flip(): lax.ppermute(value, axis, [(i, i ^ mask) for i in range(lax.axis_size(axi...  9.15 us
    pallas_call x2, Pallas kernels, first_step(): pl.pallas_call(functools.partial(first_kernel, len(pieces), labels, per,...  2.53 us
    pallas_call x1, Pallas kernels, embed_tiles(): pl.pallas_call(embed_kernel, out_shape=[jax.ShapeDtypeStruct((size, width...  2.38 us
    pallas_call x1, Pallas kernels, finish_step(): pl.pallas_call(functools.partial(finish_kernel, size, groups, len(pieces)...  0.92 us
  transfers between devices with their start and end apart: 14, of which 8 were waited for; matrix products, arithmetic and copies ran while one was open for 0% of the time, Pallas kernels for 6%

profile of v10, /device:TPU:0, one launch (start us, length us, event | category | flops | bytes accessed | tf_op | source)
XLA Modules:
  0.0 41.6 jit_solution(8193123641062683396)
XLA Ops:
  0.6 2.4 %embed.1 = (bf16[240,512]{1,0:T(8,128)(2,1)S(1)}, bf16[128,512]{1,0:T(8,128)(2,1)}, bf16[112,512]{1,0:T(8,128)(2,1)}) custom-call(bf16[2,128,768]{2,1,0:T(8,128)(2,1)} %features_in.1, s32[2]{0:T(128)} %counts_in.1, bf16[768,512]{1,0:T(8,128)(2,1)} %projection_in.1), custom_call_target="tpu_custom_call" | custom-call | tf_op jit(solution)/shard_map/embed/pallas_call | solution.py:63
  3.0 3.1 %collective-permute-start.3 = (bf16[240,512]{1,0:T(8,128)(2,1)S(1)}, bf16[240,512]{1,0:T(8,128)(2,1)S(1)}, u32[]{:S(2)}, u32[]{:S(2)}) collective-permute-start(bf16[240,512]{1,0:T(8,128)(2,1)S(1)} %get-tuple-element.22.refs_0_.refs_3_), channel_id=1, source_target_pairs={{0,2},{1,3},{2,0},{3,1},{4,6},{5,7},{6,4},{7,5},{8,10},{9,11},{10,... | collective-permute-start | bytes 737288 | tf_op jit(solution)/shard_map/ppermute | solution.py:283
  6.1 2.6 %collective-permute-start = (bf16[240,512]{1,0:T(8,128)(2,1)S(1)}, bf16[240,512]{1,0:T(8,128)(2,1)S(1)}, u32[]{:S(2)}, u32[]{:S(2)}) collective-permute-start(bf16[240,512]{1,0:T(8,128)(2,1)S(1)} %get-tuple-element.22.refs_0_.refs_3_), channel_id=1, source_target_pairs={{0,4},{1,5},{2,6},{3,7},{4,0},{5,1},{6,2},{7,3},{8,12},{9,13},{10,... | collective-permute-start | bytes 737288 | tf_op jit(solution)/shard_map/ppermute | solution.py:283
  8.7 1.5 %collective-permute-start.2 = (bf16[240,512]{1,0:T(8,128)(2,1)S(1)}, bf16[240,512]{1,0:T(8,128)(2,1)S(1)}, u32[]{:S(2)}, u32[]{:S(2)}) collective-permute-start(bf16[240,512]{1,0:T(8,128)(2,1)S(1)} %get-tuple-element.22.refs_0_.refs_3_), channel_id=1, source_target_pairs={{0,1},{1,0},{2,3},{3,2},{4,5},{5,4},{6,7},{7,6},{8,9},{9,8},{10,11... | collective-permute-start | bytes 737288 | tf_op jit(solution)/shard_map/ppermute | solution.py:283
  10.2 1.5 %collective-permute-start.7 = (bf16[240,512]{1,0:T(8,128)(2,1)S(1)}, bf16[240,512]{1,0:T(8,128)(2,1)S(1)}, u32[]{:S(2)}, u32[]{:S(2)}) collective-permute-start(bf16[240,512]{1,0:T(8,128)(2,1)S(1)} %get-tuple-element.22.refs_0_.refs_3_), channel_id=1, source_target_pairs={{0,16},{8,24},{16,0},{24,8},{1,17},{9,25},{17,1},{25,9},{2,18},{10... | collective-permute-start | bytes 737288 | tf_op jit(solution)/shard_map/ppermute | solution.py:283
  11.7 0.0 collective-permute-start.4
  11.7 5.5 %collective-permute-done.3.in_ref.refs_4_ = bf16[240,512]{1,0:T(8,128)(2,1)S(1)} collective-permute-done((bf16[240,512]{1,0:T(8,128)(2,1)S(1)}, bf16[240,512]{1,0:T(8,128)(2,1)S(1)}, u32[]{:S(2)}, u32[]{:S(2)}) %collective-permute-start.3) | collective-permute-done | bytes 245792 | tf_op jit(solution)/shard_map/ppermute | solution.py:283
  17.2 1.7 %collective-permute-start.8 = (bf16[240,512]{1,0:T(8,128)(2,1)S(1)}, bf16[240,512]{1,0:T(8,128)(2,1)S(1)}, u32[]{:S(2)}, u32[]{:S(2)}) collective-permute-start(bf16[240,512]{1,0:T(8,128)(2,1)S(1)} %collective-permute-done.3.in_ref.refs_4_), channel_id=1, source_target_pairs={{0,16},{8,24},{16,0},{24,8},{1,17},{9,25},{17,1},{25,9},{2,18},{10... | collective-permute-start | bytes 737288 | tf_op jit(solution)/shard_map/ppermute | solution.py:283
  18.9 0.8 %collective-permute-done.refs_2_ = bf16[240,512]{1,0:T(8,128)(2,1)S(1)} collective-permute-done((bf16[240,512]{1,0:T(8,128)(2,1)S(1)}, bf16[240,512]{1,0:T(8,128)(2,1)S(1)}, u32[]{:S(2)}, u32[]{:S(2)}) %collective-permute-start) | collective-permute-done | bytes 245792 | tf_op jit(solution)/shard_map/ppermute | solution.py:283
  19.7 0.0 collective-permute-start.6
  19.7 1.5 %collective-permute-start.1 = (bf16[240,512]{1,0:T(8,128)(2,1)S(1)}, bf16[240,512]{1,0:T(8,128)(2,1)S(1)}, u32[]{:S(2)}, u32[]{:S(2)}) collective-permute-start(bf16[240,512]{1,0:T(8,128)(2,1)S(1)} %collective-permute-done.refs_2_), channel_id=1, source_target_pairs={{0,1},{1,0},{2,3},{3,2},{4,5},{5,4},{6,7},{7,6},{8,9},{9,8},{10,11... | collective-permute-start | bytes 737288 | tf_op jit(solution)/shard_map/ppermute | solution.py:283
  21.2 0.0 collective-permute-done.7.in_ref.refs_3_
  21.2 0.2 collective-permute-start.5
  21.5 0.0 collective-permute-done.4.refs_5_
  21.5 0.3 collective-permute-start.10
  21.8 0.0 collective-permute-done.6.refs_7_
  21.9 0.2 collective-permute-start.9
  22.1 0.5 %collective-permute-done.5.refs_6_ = bf16[128,512]{1,0:T(8,128)(2,1)S(1)} collective-permute-done((bf16[128,512]{1,0:T(8,128)(2,1)S(1)}, bf16[128,512]{1,0:T(8,128)(2,1)S(1)}, u32[]{:S(2)}, u32[]{:S(2)}) %collective-permute-start.5) | collective-permute-done | bytes 131104 | tf_op jit(solution)/shard_map/ppermute | solution.py:283
  22.6 1.3 %first_scores.2 = (bf16[8,8,16,512]{3,2,1,0:T(8,128)(2,1)S(1)}, f32[8,128]{1,0:T(8,128)S(1)}, f32[6,8,128]{2,1,0:T(8,128)S(1)}) custom-call(bf16[240,512]{1,0:T(8,128)(2,1)S(1)} %get-tuple-element.22.refs_0_.refs_3_, bf16[240,512]{1,0:T(8,128)(2,1)S(1)} %collective-permute-done.2.refs_1_, bf16[240,512]{1,0:T(8,128)(2,1)S(1)} %collective-permute-done.refs_2_, ...), custom_call_target="tpu_custom_call" | custom-call | tf_op jit(solution)/shard_map/first_scores/pallas_call | solution.py:176
  23.9 0.5 %collective-permute-done.8.in_ref.refs_4_ = bf16[240,512]{1,0:T(8,128)(2,1)S(1)} collective-permute-done((bf16[240,512]{1,0:T(8,128)(2,1)S(1)}, bf16[240,512]{1,0:T(8,128)(2,1)S(1)}, u32[]{:S(2)}, u32[]{:S(2)}) %collective-permute-start.8) | collective-permute-done | bytes 245792 | tf_op jit(solution)/shard_map/ppermute | solution.py:283
  24.4 0.1 collective-permute-start.11
  24.5 0.5 %collective-permute-start.12 = (bf16[80,512]{1,0:T(8,128)(2,1)S(1)}, bf16[80,512]{1,0:T(8,128)(2,1)S(1)}, u32[]{:S(2)}, u32[]{:S(2)}) collective-permute-start(bf16[80,512]{1,0:T(8,128)(2,1)S(1)} %get-tuple-element.34), channel_id=1, source_target_pairs={{0,8},{8,0},{16,24},{24,16},{1,9},{9,1},{17,25},{25,17},{2,10},{10... | collective-permute-start | bytes 245768 | tf_op jit(solution)/shard_map/ppermute | solution.py:283
  24.9 0.0 collective-permute-done.10.refs_6_
  25.0 0.1 collective-permute-start.13
  25.0 0.7 %collective-permute-done.11.refs_7_ = bf16[80,512]{1,0:T(8,128)(2,1)S(1)} collective-permute-done((bf16[80,512]{1,0:T(8,128)(2,1)S(1)}, bf16[80,512]{1,0:T(8,128)(2,1)S(1)}, u32[]{:S(2)}, u32[]{:S(2)}) %collective-permute-start.11) | collective-permute-done | bytes 81952 | tf_op jit(solution)/shard_map/ppermute | solution.py:283
  25.7 0.2 collective-permute-done.12.refs_8_
  25.9 0.4 collective-permute-done.13.refs_9_
  26.2 1.3 %first_scores.3 = (bf16[8,8,16,512]{3,2,1,0:T(8,128)(2,1)S(1)}, f32[8,128]{1,0:T(8,128)S(1)}, f32[6,8,128]{2,1,0:T(8,128)S(1)}) custom-call(bf16[240,512]{1,0:T(8,128)(2,1)S(1)} %get-tuple-element.22.refs_0_.refs_3_, bf16[240,512]{1,0:T(8,128)(2,1)S(1)} %collective-permute-done.2.refs_1_, bf16[240,512]{1,0:T(8,128)(2,1)S(1)} %collective-permute-done.refs_2_, ...), custom_call_target="tpu_custom_call" | custom-call | tf_op jit(solution)/shard_map/first_scores/pallas_call | solution.py:176
  27.5 0.6 %collective-permute-done.1.refs_0_ = bf16[240,512]{1,0:T(8,128)(2,1)S(1)} collective-permute-done((bf16[240,512]{1,0:T(8,128)(2,1)S(1)}, bf16[240,512]{1,0:T(8,128)(2,1)S(1)}, u32[]{:S(2)}, u32[]{:S(2)}) %collective-permute-start.1) | collective-permute-done | bytes 245792 | tf_op jit(solution)/shard_map/ppermute | solution.py:283
  28.1 0.9 %finish.1 = f32[8,8,4,128]{3,2,1,0:T(4,128)S(1)} custom-call(bf16[240,512]{1,0:T(8,128)(2,1)S(1)} %collective-permute-done.1.refs_0_, bf16[8,8,16,512]{3,2,1,0:T(8,128)(2,1)S(1)} %get-tuple-element.25.refs_1_, f32[8,128]{1,0:T(8,128)S(1)} %get-tuple-element.26.refs_2_, bf16[8,8,16,512]{3,2,1,0:T(8,128)(2,1)S(1)} %get-tuple-element.36.refs_3_, ...), custom_call_target="tpu_custom_call" | custom-call | tf_op jit(solution)/shard_map/finish/pallas_call | solution.py:236
  29.0 11.8 %all_to_all.5.parts = f32[8,8,4,128]{3,2,1,0:T(4,128)S(1)} all-to-all(f32[8,8,4,128]{3,2,1,0:T(4,128)S(1)} %finish.1), channel_id=1, replica_groups=mesh['grp'=4,'dev'=8] {'dev'}, dimensions={0} | all-to-all | bytes 262144 | tf_op jit(solution)/shard_map/all_to_all | solution.py:364
  40.9 0.7 %gather_results.1 = (f32[16,8,128]{2,1,0:T(8,128)}, f32[8,16]{1,0:T(8,128)}) custom-call(f32[8,8,4,128]{3,2,1,0:T(4,128)S(1)} %all_to_all.5.parts), custom_call_target="tpu_custom_call" | custom-call | tf_op jit(solution)/shard_map/gather_results/pallas_call | solution.py:269
  (5 shorter events, 0.1 us)
Async XLA Ops:
  3.0 14.2 %collective-permute-start.3 = (bf16[240,512]{1,0:T(8,128)(2,1)S(1)}, bf16[240,512]{1,0:T(8,128)(2,1)S(1)}, u32[]{:S(2)}, u32[]{:S(2)}) collective-permute-start(bf16[240,512]{1,0:T(8,128)(2,1)S(1)} %get-tuple-element.22.refs_0_.refs_3_), channel_id=1, source_target_pairs={{0,2},{1,3},{2,0},{3,1},{4,6},{5,7},{6,4},{7,5},{8,10},{9,11},{10,... | collective-permute-start | bytes 737288 | tf_op jit(solution)/shard_map/ppermute | solution.py:283
  6.1 13.6 %collective-permute-start = (bf16[240,512]{1,0:T(8,128)(2,1)S(1)}, bf16[240,512]{1,0:T(8,128)(2,1)S(1)}, u32[]{:S(2)}, u32[]{:S(2)}) collective-permute-start(bf16[240,512]{1,0:T(8,128)(2,1)S(1)} %get-tuple-element.22.refs_0_.refs_3_), channel_id=1, source_target_pairs={{0,4},{1,5},{2,6},{3,7},{4,0},{5,1},{6,2},{7,3},{8,12},{9,13},{10,... | collective-permute-start | bytes 737288 | tf_op jit(solution)/shard_map/ppermute | solution.py:283
  8.7 11.0 %collective-permute-start.2 = (bf16[240,512]{1,0:T(8,128)(2,1)S(1)}, bf16[240,512]{1,0:T(8,128)(2,1)S(1)}, u32[]{:S(2)}, u32[]{:S(2)}) collective-permute-start(bf16[240,512]{1,0:T(8,128)(2,1)S(1)} %get-tuple-element.22.refs_0_.refs_3_), channel_id=1, source_target_pairs={{0,1},{1,0},{2,3},{3,2},{4,5},{5,4},{6,7},{7,6},{8,9},{9,8},{10,11... | collective-permute-start | bytes 737288 | tf_op jit(solution)/shard_map/ppermute | solution.py:283
  10.2 11.0 %collective-permute-start.7 = (bf16[240,512]{1,0:T(8,128)(2,1)S(1)}, bf16[240,512]{1,0:T(8,128)(2,1)S(1)}, u32[]{:S(2)}, u32[]{:S(2)}) collective-permute-start(bf16[240,512]{1,0:T(8,128)(2,1)S(1)} %get-tuple-element.22.refs_0_.refs_3_), channel_id=1, source_target_pairs={{0,16},{8,24},{16,0},{24,8},{1,17},{9,25},{17,1},{25,9},{2,18},{10... | collective-permute-start | bytes 737288 | tf_op jit(solution)/shard_map/ppermute | solution.py:283
  11.7 9.8 %collective-permute-start.4 = (bf16[240,512]{1,0:T(8,128)(2,1)S(1)}, bf16[240,512]{1,0:T(8,128)(2,1)S(1)}, u32[]{:S(2)}, u32[]{:S(2)}) collective-permute-start(bf16[240,512]{1,0:T(8,128)(2,1)S(1)} %get-tuple-element.22.refs_0_.refs_3_), channel_id=1, source_target_pairs={{0,8},{8,0},{16,24},{24,16},{1,9},{9,1},{17,25},{25,17},{2,10},{10... | collective-permute-start | bytes 737288 | tf_op jit(solution)/shard_map/ppermute | solution.py:283
  17.2 7.1 %collective-permute-start.8 = (bf16[240,512]{1,0:T(8,128)(2,1)S(1)}, bf16[240,512]{1,0:T(8,128)(2,1)S(1)}, u32[]{:S(2)}, u32[]{:S(2)}) collective-permute-start(bf16[240,512]{1,0:T(8,128)(2,1)S(1)} %collective-permute-done.3.in_ref.refs_4_), channel_id=1, source_target_pairs={{0,16},{8,24},{16,0},{24,8},{1,17},{9,25},{17,1},{25,9},{2,18},{10... | collective-permute-start | bytes 737288 | tf_op jit(solution)/shard_map/ppermute | solution.py:283
  19.7 2.1 %collective-permute-start.6 = (bf16[112,512]{1,0:T(8,128)(2,1)S(1)}, bf16[112,512]{1,0:T(8,128)(2,1)S(1)}, u32[]{:S(2)}, u32[]{:S(2)}) collective-permute-start(bf16[112,512]{1,0:T(8,128)(2,1)S(1)} %get-tuple-element.24), channel_id=1, source_target_pairs={{0,8},{8,0},{16,24},{24,16},{1,9},{9,1},{17,25},{25,17},{2,10},{10... | collective-permute-start | bytes 344072 | tf_op jit(solution)/shard_map/ppermute | solution.py:283
  19.7 8.4 %collective-permute-start.1 = (bf16[240,512]{1,0:T(8,128)(2,1)S(1)}, bf16[240,512]{1,0:T(8,128)(2,1)S(1)}, u32[]{:S(2)}, u32[]{:S(2)}) collective-permute-start(bf16[240,512]{1,0:T(8,128)(2,1)S(1)} %collective-permute-done.refs_2_), channel_id=1, source_target_pairs={{0,1},{1,0},{2,3},{3,2},{4,5},{5,4},{6,7},{7,6},{8,9},{9,8},{10,11... | collective-permute-start | bytes 737288 | tf_op jit(solution)/shard_map/ppermute | solution.py:283
  21.2 1.3 %collective-permute-start.5 = (bf16[128,512]{1,0:T(8,128)(2,1)S(1)}, bf16[128,512]{1,0:T(8,128)(2,1)S(1)}, u32[]{:S(2)}, u32[]{:S(2)}) collective-permute-start(bf16[128,512]{1,0:T(8,128)(2,1)S(1)} %get-tuple-element.23), channel_id=1, source_target_pairs={{0,8},{8,0},{16,24},{24,16},{1,9},{9,1},{17,25},{25,17},{2,10},{10... | collective-permute-start | bytes 393224 | tf_op jit(solution)/shard_map/ppermute | solution.py:283
  21.5 3.5 %collective-permute-start.10 = (bf16[112,512]{1,0:T(8,128)(2,1)S(1)}, bf16[112,512]{1,0:T(8,128)(2,1)S(1)}, u32[]{:S(2)}, u32[]{:S(2)}) collective-permute-start(bf16[112,512]{1,0:T(8,128)(2,1)S(1)} %get-tuple-element.28), channel_id=1, source_target_pairs={{0,8},{8,0},{16,24},{24,16},{1,9},{9,1},{17,25},{25,17},{2,10},{10... | collective-permute-start | bytes 344072 | tf_op jit(solution)/shard_map/ppermute | solution.py:283
  21.9 3.2 %collective-permute-start.9 = (bf16[128,512]{1,0:T(8,128)(2,1)S(1)}, bf16[128,512]{1,0:T(8,128)(2,1)S(1)}, u32[]{:S(2)}, u32[]{:S(2)}) collective-permute-start(bf16[128,512]{1,0:T(8,128)(2,1)S(1)} %get-tuple-element.27), channel_id=1, source_target_pairs={{0,8},{8,0},{16,24},{24,16},{1,9},{9,1},{17,25},{25,17},{2,10},{10... | collective-permute-start | bytes 393224 | tf_op jit(solution)/shard_map/ppermute | solution.py:283
  24.4 1.3 %collective-permute-start.11 = (bf16[80,512]{1,0:T(8,128)(2,1)S(1)}, bf16[80,512]{1,0:T(8,128)(2,1)S(1)}, u32[]{:S(2)}, u32[]{:S(2)}) collective-permute-start(bf16[80,512]{1,0:T(8,128)(2,1)S(1)} %get-tuple-element.33), channel_id=1, source_target_pairs={{0,8},{8,0},{16,24},{24,16},{1,9},{9,1},{17,25},{25,17},{2,10},{10... | collective-permute-start | bytes 245768 | tf_op jit(solution)/shard_map/ppermute | solution.py:283
  24.5 1.4 %collective-permute-start.12 = (bf16[80,512]{1,0:T(8,128)(2,1)S(1)}, bf16[80,512]{1,0:T(8,128)(2,1)S(1)}, u32[]{:S(2)}, u32[]{:S(2)}) collective-permute-start(bf16[80,512]{1,0:T(8,128)(2,1)S(1)} %get-tuple-element.34), channel_id=1, source_target_pairs={{0,8},{8,0},{16,24},{24,16},{1,9},{9,1},{17,25},{25,17},{2,10},{10... | collective-permute-start | bytes 245768 | tf_op jit(solution)/shard_map/ppermute | solution.py:283
  25.0 1.3 %collective-permute-start.13 = (bf16[80,512]{1,0:T(8,128)(2,1)S(1)}, bf16[80,512]{1,0:T(8,128)(2,1)S(1)}, u32[]{:S(2)}, u32[]{:S(2)}) collective-permute-start(bf16[80,512]{1,0:T(8,128)(2,1)S(1)} %get-tuple-element.35), channel_id=1, source_target_pairs={{0,8},{8,0},{16,24},{24,16},{1,9},{9,1},{17,25},{25,17},{2,10},{10... | collective-permute-start | bytes 245768 | tf_op jit(solution)/shard_map/ppermute | solution.py:283
